TPU v7x, 128 devices: a whole 4x4x4 slice. The times are simulated.
128 devices in a mesh: bx: 8 (over z_hi, y), by: 16 (over x, z_lo, core).
Axes of the slice: x: 4, y: 4, z: 4 (z_hi: 2, z_lo: 2; z = z_hi * 2 + z_lo), core: 2. Of those that a mesh axis runs over, the one named last changes fastest.
Arguments:
- tracers: float32 [4, 60, 192, 2048], P(None, None, 'bx', 'by'), may hold values from -40 to 40
- rates: float32 [4, 60, 192, 2048], P(None, None, 'bx', 'by'), may hold values from 0.02 to 0.24
- column_order: int32 [128, 3072], P(('bx', 'by')), may hold values from 0 to 3071, as said below
- norm_gain: float32 [240], replicated, may hold values from 0.25 to 1.75
- norm_shift: float32 [240], replicated, may hold values from -3 to 3
- weight_first: bfloat16 [512, 240], replicated, may hold values from -0.375 to 0.375
- weight_hidden: bfloat16 [3, 512, 512], replicated, may hold values from -0.25 to 0.25
- weight_last: bfloat16 [240, 512], replicated, may hold values from -0.25 to 0.25
- bias_hidden: float32 [4, 512], replicated, may hold values from -3 to 3
- bias_last: float32 [240], replicated, may hold values from -3 to 3
Outputs:
- new_tracers: float32 [4, 60, 192, 2048], P(None, None, 'bx', 'by')
Inputs may be any that keep to these rules, and one draw needn't show every extreme that they name: `column_order`: each row is a permutation of the block's 3072 columns.
All inputs are finite; a program needn't handle non-finite values.
Results may differ from a plain program's by a relative error of at most 0.0023.
Values may be sent and summed in bfloat16 or wider, within the bound.
No kernel may reach another device: no remote copies, remote signals or barrier semaphores. Data moves between devices by JAX's collectives and lax.ppermute only.
A program may use at most 128 MiB of HBM per device.

v0:
```python
import functools

import jax
import jax.numpy as jnp
from jax import lax
from jax.experimental import pallas as pl
from jax.experimental.pallas import tpu as pltpu
from jax.sharding import PartitionSpec as P

FIELDS = 4
LEVELS = 60
CHUNKS = 8
ROWS = 24
COLS = 128
FEATS = 256
HALF = ROWS // 2
MIB = 1 << 20
NT = (((1,), (1,)), ((), ()))
NN = (((1,), (0,)), ((), ()))


def params(limit=32):
    return pltpu.CompilerParams(
        dimension_semantics=("arbitrary",), vmem_limit_bytes=limit * MIB
    )


def lanes_of(shape):
    return lax.broadcasted_iota(jnp.int32, shape, 1)


def valid_rows(chunk):
    level = chunk * 8 + lax.broadcasted_iota(jnp.int32, (8, COLS), 0)
    return level < LEVELS


class ColumnPacker:
    def __init__(self):
        self.pair = lanes_of((8, COLS)) // 2
        self.halves = [jnp.zeros((8, COLS), jnp.float32) for _ in range(2)]

    def add(self, i, f, tile):
        m = 4 * (i % HALF) + f
        moved = pltpu.roll(tile, 2 * m + 1, axis=1)
        self.halves[i // HALF] = jnp.where(self.pair == m, moved, self.halves[i // HALF])

    def store(self, ref):
        for h in range(2):
            ref[:, COLS * h : COLS * (h + 1)] = self.halves[h]


def pack_kernel(x_ref, q_ref, first_ref, last_ref, cols_ref):
    valid = valid_rows(pl.program_id(0))
    packer = ColumnPacker()
    for i in range(ROWS):
        for f in range(FIELDS):
            tile = jnp.where(valid, x_ref[f, pl.ds(i, 8, stride=ROWS), :], 0.0)
            q_ref[i, 8 * f : 8 * f + 8, :] = tile
            if i == 0:
                first_ref[8 * f : 8 * f + 8, :] = tile
            if i == ROWS - 1:
                last_ref[8 * f : 8 * f + 8, :] = tile
            packer.add(i, f, tile)
    packer.store(cols_ref)


def advance_tiles(q_ref, rates_ref, up_ref, down_ref, left_ref, right_ref, emit):
    valid = valid_rows(pl.program_id(0))
    lane = lanes_of((8, COLS))
    even = lane % 2 == 0
    ring = []
    for h in range(2):
        part = slice(COLS * h, COLS * (h + 1))
        ring.append(
            jnp.where(
                even,
                pltpu.roll(right_ref[:, part], COLS - 1, axis=1),
                pltpu.roll(left_ref[:, part], 1, axis=1),
            )
        )
    for i in range(ROWS):
        rate = [rates_ref[k, pl.ds(i, 8, stride=ROWS), :] for k in range(4)]
        for f in range(FIELDS):
            rows = slice(8 * f, 8 * f + 8)
            m = 4 * (i % HALF) + f
            here = q_ref[i, rows, :]
            above = up_ref[rows, :] if i == 0 else q_ref[i - 1, rows, :]
            below = down_ref[rows, :] if i == ROWS - 1 else q_ref[i + 1, rows, :]
            edge = pltpu.roll(ring[i // HALF], COLS - (2 * m + 1), axis=1)
            after = jnp.where(lane == COLS - 1, edge, pltpu.roll(here, COLS - 1, axis=1))
            before = jnp.where(lane == 0, edge, pltpu.roll(here, 1, axis=1))
            new = (
                here
                + rate[0] * (below - here)
                + rate[1] * (above - here)
                + rate[2] * (after - here)
                + rate[3] * (before - here)
            )
            emit(i, f, jnp.where(valid, new, 0.0))


def first_kernel(
    q_ref, rates_ref, up_ref, down_ref, left_ref, right_ref, out_ref, first_ref, last_ref, cols_ref
):
    packer = ColumnPacker()

    def emit(i, f, tile):
        out_ref[i, 8 * f : 8 * f + 8, :] = tile
        if i == 0:
            first_ref[8 * f : 8 * f + 8, :] = tile
        if i == ROWS - 1:
            last_ref[8 * f : 8 * f + 8, :] = tile
        packer.add(i, f, tile)

    advance_tiles(q_ref, rates_ref, up_ref, down_ref, left_ref, right_ref, emit)
    packer.store(cols_ref)


def second_kernel(
    share,
    q_ref,
    rates_ref,
    up_ref,
    down_ref,
    left_ref,
    right_ref,
    hot_ref,
    batch_ref,
    out_ref,
    stats_ref,
    x_ref,
    hi_ref,
    lo_ref,
):
    chunk = pl.program_id(0)
    kept = {}

    def emit(i, f, tile):
        out_ref[i, 8 * f : 8 * f + 8, :] = tile
        kept[f] = tile
        if f % 2 == 1:
            both = jnp.concatenate([kept[f - 1], tile], axis=0).astype(jnp.bfloat16)
            start = pl.multiple_of(32 * chunk + 8 * (f - 1), 16)
            x_ref[pl.ds(start, 16), COLS * i : COLS * (i + 1)] = both

    advance_tiles(q_ref, rates_ref, up_ref, down_ref, left_ref, right_ref, emit)

    @pl.when(chunk == CHUNKS - 1)
    def _():
        hot = hot_ref[...]
        sums = lax.dot_general(x_ref[...], hot, NT, preferred_element_type=jnp.float32)
        mean = sums * (1.0 / share)
        for i in range(ROWS):
            part = slice(COLS * i, COLS * (i + 1))
            index = jnp.broadcast_to(batch_ref[i : i + 1, :], (FEATS, COLS))
            own = jnp.take_along_axis(mean, index, axis=1)
            away = x_ref[:, part].astype(jnp.float32) - own
            square = away * away
            high = square.astype(jnp.bfloat16)
            hi_ref[:, part] = high
            lo_ref[:, part] = (square - high.astype(jnp.float32)).astype(jnp.bfloat16)
        spread = lax.dot_general(
            hi_ref[...], hot, NT, preferred_element_type=jnp.float32
        ) + lax.dot_general(lo_ref[...], hot, NT, preferred_element_type=jnp.float32)
        stats_ref[:, :FEATS] = mean.T
        stats_ref[:, FEATS:] = spread.T


def batch_kernel(order_ref, owner_ref, batch_ref, hot_ref):
    order = order_ref[...]
    shape = (32, order.shape[1])
    high = lax.broadcasted_iota(jnp.int32, shape, 0) == order // COLS
    left = jnp.where(high, owner_ref[...], 0.0).astype(jnp.bfloat16)
    shape = (COLS, order.shape[1])
    low = lax.broadcasted_iota(jnp.int32, shape, 0) == order % COLS
    right = jnp.where(low, 1.0, 0.0).astype(jnp.bfloat16)
    found = lax.dot_general(left, right, NT, preferred_element_type=jnp.float32)
    batch = found[:ROWS].astype(jnp.int32)
    batch_ref[...] = batch
    groups = lax.broadcasted_iota(jnp.int32, (COLS, COLS), 0)
    for i in range(ROWS):
        hot_ref[:, COLS * i : COLS * (i + 1)] = jnp.where(
            groups == batch[i : i + 1, :], 1.0, 0.0
        ).astype(jnp.bfloat16)


def merge_kernel(share, stats_ref, gain_ref, out_ref):
    count = stats_ref.shape[0]
    means = stats_ref[:, :FEATS]
    mean = jnp.sum(means, axis=0, keepdims=True) * (1.0 / count)
    away = means - mean
    total = jnp.sum(stats_ref[:, FEATS:] + share * (away * away), axis=0, keepdims=True)
    scale = lax.rsqrt(total * (1.0 / (count * share)) + 1e-05) * gain_ref[...]
    out_ref[:, :FEATS] = jnp.broadcast_to(mean, (count, FEATS))
    out_ref[:, FEATS:] = jnp.broadcast_to(scale, (count, FEATS))


def network_kernel(
    moved_ref,
    batch_ref,
    stats_ref,
    shift_ref,
    first_ref,
    inner_ref,
    last_ref,
    bias_ref,
    final_ref,
    out_ref,
    mean_ref,
    scale_ref,
):
    step = pl.program_id(0)

    @pl.when(step == 0)
    def _():
        mean_ref[...] = stats_ref[:, :FEATS].T
        scale_ref[...] = stats_ref[:, FEATS:].T

    mean = mean_ref[...]
    scale = scale_ref[...]
    shift = shift_ref[...]

    def wide(tile):
        return jnp.concatenate([tile, tile], axis=1)

    def act(product, layer):
        t = product + wide(bias_ref[layer])
        return (t + t * jnp.tanh(t)).astype(jnp.bfloat16)

    for pair in range(4):
        normed = []
        for i in (2 * pair, 2 * pair + 1):
            index = jnp.broadcast_to(batch_ref[i : i + 1, :], (FEATS, COLS))
            x = moved_ref[i].astype(jnp.bfloat16).astype(jnp.float32)
            away = x - jnp.take_along_axis(mean, index, axis=1)
            tile = away * jnp.take_along_axis(scale, index, axis=1) + shift
            normed.append(tile.astype(jnp.bfloat16))
        hidden = jnp.concatenate(normed, axis=1)
        hidden = act(
            lax.dot_general(first_ref[...], hidden, NN, preferred_element_type=jnp.float32), 0
        )
        for layer in range(3):
            hidden = act(
                lax.dot_general(
                    inner_ref[layer], hidden, NN, preferred_element_type=jnp.float32
                ),
                layer + 1,
            )
        tendency = lax.dot_general(
            last_ref[...], hidden, NN, preferred_element_type=jnp.float32
        ) + wide(final_ref[...])
        tendency = tendency.astype(jnp.bfloat16).astype(jnp.float32)
        for k in range(2):
            i = 2 * pair + k
            new = moved_ref[i] + tendency[:, COLS * k : COLS * (k + 1)]
            for chunk in range(CHUNKS):
                rows = min(8, LEVELS - 8 * chunk)
                for f in range(FIELDS):
                    row = 32 * chunk + 8 * f
                    out_ref[pl.ds((LEVELS * f + 8 * chunk) * 8 + i, rows, stride=8), :] = new[
                        row : row + rows
                    ]


def network_outer(*refs):
    (*inputs, out_ref, mean_ref, scale_ref) = refs
    network_kernel(*inputs, out_ref.reshape(FIELDS * LEVELS * 8, COLS), mean_ref, scale_ref)


def whole(shape):
    return pl.BlockSpec(shape, lambda c: (0,) * len(shape))


GRID_SPEC = pl.BlockSpec((ROWS, 32, COLS), lambda c: (0, c, 0))
NATIVE_SPEC = pl.BlockSpec((4, 8 * ROWS, COLS), lambda c: (0, c, 0))
ROW_SPEC = pl.BlockSpec((32, COLS), lambda c: (c, 0))
COL_SPEC = pl.BlockSpec((8, 2 * COLS), lambda c: (c, 0))
GRID_SHAPE = jax.ShapeDtypeStruct((ROWS, FEATS, COLS), jnp.float32)
ROW_SHAPE = jax.ShapeDtypeStruct((FEATS, COLS), jnp.float32)
COL_SHAPE = jax.ShapeDtypeStruct((64, 2 * COLS), jnp.float32)


def cost(flops, size):
    return pl.CostEstimate(flops=flops, bytes_accessed=size, transcendentals=0)


def ring(axis, by):
    count = lax.axis_size(axis)
    return [(i, (i + by) % count) for i in range(count)]


def halos(first, last, cols):
    up = lax.ppermute(last, "bx", ring("bx", 1))
    down = lax.ppermute(first, "bx", ring("bx", -1))
    left = lax.ppermute(cols, "by", ring("by", 1))
    right = lax.ppermute(cols, "by", ring("by", -1))
    return up, down, left, right


def by_row(values):
    rest = values.shape[1:]
    values = values.reshape(FIELDS, LEVELS, *rest)
    values = jnp.pad(values, ((0, 0), (0, 64 - LEVELS)) + ((0, 0),) * len(rest))
    values = values.reshape(FIELDS, CHUNKS, 8, *rest).swapaxes(0, 1)
    return values.reshape(FEATS, *rest)


def body(
    tracers,
    rates,
    column_order,
    norm_gain,
    norm_shift,
    weight_first,
    weight_hidden,
    weight_last,
    bias_hidden,
    bias_last,
):
    count = lax.axis_size("bx") * lax.axis_size("by")
    columns = ROWS * COLS
    share = columns // count
    width = weight_first.shape[0]
    x = tracers.reshape(FIELDS, LEVELS * ROWS, COLS)
    r = rates.reshape(4, LEVELS * ROWS, COLS)

    q, first, last, cols = pl.pallas_call(
        pack_kernel,
        grid=(CHUNKS,),
        in_specs=[NATIVE_SPEC],
        out_specs=[GRID_SPEC, ROW_SPEC, ROW_SPEC, COL_SPEC],
        out_shape=[GRID_SHAPE, ROW_SHAPE, ROW_SHAPE, COL_SHAPE],
        compiler_params=params(),
        cost_estimate=cost(10**6, 6 * 10**6),
        name="pack_edges",
    )(x)
    edges = halos(first, last, cols)

    owner = (jnp.arange(columns, dtype=jnp.int32) // share).astype(jnp.float32)[None, :]
    batch, hot = pl.pallas_call(
        batch_kernel,
        grid=(1,),
        in_specs=[whole((1, columns)), whole((1, columns))],
        out_specs=[whole((ROWS, COLS)), whole((COLS, columns))],
        out_shape=[
            jax.ShapeDtypeStruct((ROWS, COLS), jnp.int32),
            jax.ShapeDtypeStruct((COLS, columns), jnp.bfloat16),
        ],
        compiler_params=params(),
        cost_estimate=cost(10**9, 2 * 10**6),
        name="batch_ids",
    )(column_order, owner)

    state_specs = [GRID_SPEC, NATIVE_SPEC, ROW_SPEC, ROW_SPEC, COL_SPEC, COL_SPEC]
    q, first, last, cols = pl.pallas_call(
        first_kernel,
        grid=(CHUNKS,),
        in_specs=state_specs,
        out_specs=[GRID_SPEC, ROW_SPEC, ROW_SPEC, COL_SPEC],
        out_shape=[GRID_SHAPE, ROW_SHAPE, ROW_SHAPE, COL_SHAPE],
        compiler_params=params(),
        cost_estimate=cost(10**7, 9 * 10**6),
        name="first_substep",
    )(q, r, *edges)
    edges = halos(first, last, cols)

    moved, stats = pl.pallas_call(
        functools.partial(second_kernel, share),
        grid=(CHUNKS,),
        in_specs=state_specs + [whole((COLS, columns)), whole((ROWS, COLS))],
        out_specs=[GRID_SPEC, whole((COLS, 2 * FEATS))],
        out_shape=[GRID_SHAPE, jax.ShapeDtypeStruct((COLS, 2 * FEATS), jnp.float32)],
        scratch_shapes=[pltpu.VMEM((FEATS, columns), jnp.bfloat16) for _ in range(3)],
        compiler_params=params(),
        cost_estimate=cost(10**9, 9 * 10**6),
        name="second_substep",
    )(q, r, *edges, hot, batch)

    gathered = lax.all_to_all(stats, ("bx", "by"), split_axis=0, concat_axis=0, tiled=True)
    merged = pl.pallas_call(
        functools.partial(merge_kernel, float(share)),
        grid=(1,),
        in_specs=[whole((count, 2 * FEATS)), whole((1, FEATS))],
        out_specs=whole((count, 2 * FEATS)),
        out_shape=jax.ShapeDtypeStruct((count, 2 * FEATS), jnp.float32),
        compiler_params=params(),
        cost_estimate=cost(10**6, 10**6),
        name="merge_statistics",
    )(gathered, by_row(norm_gain)[None, :])
    known = lax.all_to_all(merged, ("bx", "by"), split_axis=0, concat_axis=0, tiled=True)

    def tile(values):
        return jnp.broadcast_to(values[..., None], (*values.shape, COLS))

    half = jnp.bfloat16(0.5)
    new = pl.pallas_call(
        network_outer,
        grid=(3,),
        in_specs=[
            pl.BlockSpec((8, FEATS, COLS), lambda c: (c, 0, 0)),
            pl.BlockSpec((8, COLS), lambda c: (c, 0)),
            whole((count, 2 * FEATS)),
            whole((FEATS, COLS)),
            whole((width, FEATS)),
            whole((3, width, width)),
            whole((FEATS, width)),
            whole((4, width, COLS)),
            whole((FEATS, COLS)),
        ],
        out_specs=pl.BlockSpec((FIELDS * LEVELS, 8, COLS), lambda c: (0, c, 0)),
        out_shape=jax.ShapeDtypeStruct((FIELDS * LEVELS, ROWS, COLS), jnp.float32),
        scratch_shapes=[pltpu.VMEM((FEATS, COLS), jnp.float32) for _ in range(2)],
        compiler_params=params(40),
        cost_estimate=cost(6 * 10**9, 9 * 10**6),
        name="network",
    )(
        moved,
        batch,
        known,
        tile(by_row(norm_shift)),
        by_row(weight_first.T).T * half,
        weight_hidden * half,
        by_row(weight_last),
        tile(bias_hidden * 0.5),
        tile(by_row(bias_last)),
    )
    return new.reshape(tracers.shape)


def solution(mesh):
    placed = (
        P(None, None, "bx", "by"),
        P(None, None, "bx", "by"),
        P(("bx", "by"), None),
        P(),
        P(),
        P(),
        P(),
        P(),
        P(),
        P(),
    )
    return jax.shard_map(
        body, mesh=mesh, in_specs=placed, out_specs=P(None, None, "bx", "by"), check_vma=False
    )
```

profile of v0, /device:TPU:1, one launch (start us, length us, event | category | flops | bytes accessed | tf_op | source)
XLA Modules:
  0.0 136.2 jit_solution(11676490678364895335)
XLA Ops:
  0.0 2.0 %copy-done.5 = f32[4,60,24,128]{3,2,1,0:T(8,128)S(1)} copy-done((f32[4,60,24,128]{3,2,1,0:T(8,128)S(1)}, f32[4,60,24,128]{3,2,1,0:T(8,128)}, u32[]{:S(2)}) %copy-start.5) | copy-done | bytes 2949144
  2.0 3.7 %pack_edges.1 = (f32[24,256,128]{2,1,0:T(8,128)S(1)}, f32[256,128]{1,0:T(8,128)S(1)}, f32[256,128]{1,0:T(8,128)}, f32[64,256]{1,0:T(8,128)S(1)}) custom-call(f32[4,1440,128]{2,1,0:T(8,128)S(1)} %bitcast.28), custom_call_target="tpu_custom_call" | custom-call | flops 1000000 | bytes 6000000 | tf_op jit(solution)/shard_map/pack_edges/pallas_call | solution.py:327
  5.6 1.6 %copy-done.1 = f32[24,256,128]{2,1,0:T(8,128)} copy-done((f32[24,256,128]{2,1,0:T(8,128)}, f32[24,256,128]{2,1,0:T(8,128)S(1)}, u32[]{:S(2)}) %copy-start.1) | copy-done | bytes 3145752
  7.3 3.0 %collective-permute-start.2 = (f32[64,256]{1,0:T(8,128)S(1)}, f32[64,256]{1,0:T(8,128)S(1)}, u32[]{:S(2)}, u32[]{:S(2)}) collective-permute-start(f32[64,256]{1,0:T(8,128)S(1)} %get-tuple-element.20), channel_id=1, source_target_pairs={{0,1},{1,2},{2,3},{3,4},{4,5},{5,6},{6,7},{7,8},{8,9},{9,10},{10,1... | collective-permute-start | bytes 196616 | tf_op jit(solution)/shard_map/ppermute | solution.py:295
  10.3 1.3 collective-permute-start
  11.6 4.5 %collective-permute-start.1 = (f32[256,128]{1,0:T(8,128)S(1)}, f32[256,128]{1,0:T(8,128)S(1)}, u32[]{:S(2)}, u32[]{:S(2)}) collective-permute-start(f32[256,128]{1,0:T(8,128)S(1)} %get-tuple-element.19), channel_id=1, source_target_pairs={{0,112},{16,0},{32,16},{48,32},{64,48},{80,64},{96,80},{112,96},{1... | collective-permute-start | bytes 393224 | tf_op jit(solution)/shard_map/ppermute | solution.py:294
  16.1 1.7 %reshape.95 = bf16[4,60,512]{2,1,0:T(8,128)(2,1)} reshape(bf16[240,512]{1,0:T(8,128)(2,1)} %bitcast.36) | data formatting | bytes 491520 | tf_op jit(solution)/shard_map/reshape | solution.py:302
  17.8 1.4 %collective-permute-done.up_ref = f32[256,128]{1,0:T(8,128)S(1)} collective-permute-done((f32[256,128]{1,0:T(8,128)}, f32[256,128]{1,0:T(8,128)S(1)}, u32[]{:S(2)}, u32[]{:S(2)}) %collective-permute-start) | collective-permute-done | bytes 131104 | tf_op jit(solution)/shard_map/ppermute | solution.py:293
  19.2 1.9 %copy-done.2 = f32[24,256,128]{2,1,0:T(8,128)S(1)} copy-done((f32[24,256,128]{2,1,0:T(8,128)S(1)}, f32[24,256,128]{2,1,0:T(8,128)}, u32[]{:S(2)}) %copy-start.2) | copy-done | bytes 3145752
  21.1 30.6 %first_substep.1 = (f32[24,256,128]{2,1,0:T(8,128)S(1)}, f32[256,128]{1,0:T(8,128)S(1)}, f32[256,128]{1,0:T(8,128)}, f32[64,256]{1,0:T(8,128)S(1)}) custom-call(f32[24,256,128]{2,1,0:T(8,128)S(1)} %copy-done.2, f32[4,1440,128]{2,1,0:T(8,128)S(1)} %bitcast.26, f32[256,128]{1,0:T(8,128)S(1)} %collective-permute-done.up_ref, ...), custom_call_target="tpu_custom_call" | custom-call | flops 10000000 | bytes 9000000 | tf_op jit(solution)/shard_map/first_substep/pallas_call | solution.py:355
  51.7 1.6 %copy-done.3 = f32[24,256,128]{2,1,0:T(8,128)} copy-done((f32[24,256,128]{2,1,0:T(8,128)}, f32[24,256,128]{2,1,0:T(8,128)S(1)}, u32[]{:S(2)}) %copy-start.3) | copy-done | bytes 3145752
  53.3 5.1 %collective-permute-start.5 = (f32[256,128]{1,0:T(8,128)S(1)}, f32[256,128]{1,0:T(8,128)S(1)}, u32[]{:S(2)}, u32[]{:S(2)}) collective-permute-start(f32[256,128]{1,0:T(8,128)S(1)} %get-tuple-element.23), channel_id=1, source_target_pairs={{0,112},{16,0},{32,16},{48,32},{64,48},{80,64},{96,80},{112,96},{1... | collective-permute-start | bytes 393224 | tf_op jit(solution)/shard_map/ppermute | solution.py:294
  58.4 0.7 multiply_bitcast_fusion
  59.4 1.7 %reshape.96 = bf16[4,60,512]{2,1,0:T(8,128)(2,1)} reshape(bf16[240,512]{1,0:T(8,128)(2,1)} %param.17) | data formatting | bytes 491520 | tf_op jit(solution)/shard_map/reshape | solution.py:302
  61.1 2.4 %collective-permute-start.6 = (f32[64,256]{1,0:T(8,128)S(1)}, f32[64,256]{1,0:T(8,128)S(1)}, u32[]{:S(2)}, u32[]{:S(2)}) collective-permute-start(f32[64,256]{1,0:T(8,128)S(1)} %get-tuple-element.24), channel_id=1, source_target_pairs={{0,1},{1,2},{2,3},{3,4},{4,5},{5,6},{6,7},{7,8},{8,9},{9,10},{10,1... | collective-permute-start | bytes 196616 | tf_op jit(solution)/shard_map/ppermute | solution.py:295
  63.6 1.1 collective-permute-start.7
  64.6 0.7 copy-done.8
  65.4 0.6 batch_ids.1
  66.0 1.3 collective-permute-done.7.right_ref
  67.3 8.0 %second_substep.1 = (f32[24,256,128]{2,1,0:T(8,128)S(1)}, f32[128,512]{1,0:T(8,128)S(1)}) custom-call(f32[24,256,128]{2,1,0:T(8,128)S(1)} %copy-done.4, f32[4,1440,128]{2,1,0:T(8,128)S(1)} %bitcast.27, f32[256,128]{1,0:T(8,128)S(1)} %collective-permute-done.4.up_ref, f32[256,128]{1,0:T(8,128)S(1)} %collective-permute-done.5.down_ref, ...), custom_call_target="tpu_custom_call" | custom-call | flops 1000000000 | bytes 9000000 | tf_op jit(solution)/shard_map/second_substep/pallas_call | solution.py:367
  75.3 1.6 %copy-done.6 = f32[24,256,128]{2,1,0:T(8,128)} copy-done((f32[24,256,128]{2,1,0:T(8,128)}, f32[24,256,128]{2,1,0:T(8,128)S(1)}, u32[]{:S(2)}) %copy-start.6) | copy-done | bytes 3145752
  76.9 1.0 copy.21
  77.9 9.6 %all-to-all-start = ((f32[128,1,512]{2,1,0:T(1,128)}), f32[128,1,512]{2,1,0:T(1,128)S(1)}, u32[]{:S(2)}, u32[]{:S(2)}) async-start(f32[128,1,512]{2,1,0:T(1,128)} %copy.21), calls=%async_computation | async-start | bytes 524288 | tf_op jit(solution)/shard_map/all_to_all | solution.py:379
  87.5 1.6 %broadcast_multiply_fusion.refs_5_ = bf16[3,512,512]{2,1,0:T(8,128)(2,1)S(1)} fusion(bf16[3,512,512]{2,1,0:T(8,128)(2,1)} %param.16), kind=kLoop, calls=%fused_computation | loop fusion | flops 786432 | bytes 3145728 | tf_op jit(solution)/shard_map/mul | solution.py:422
  89.1 9.3 %all-to-all-done = f32[128,1,512]{2,1,0:T(1,128)S(1)} async-done(((f32[128,1,512]{2,1,0:T(1,128)}), f32[128,1,512]{2,1,0:T(1,128)S(1)}, u32[]{:S(2)}, u32[]{:S(2)}) %all-to-all-start) | async-done | bytes 262176 | tf_op jit(solution)/shard_map/all_to_all | solution.py:379
  98.6 1.0 copy.23
  99.6 4.6 %all-to-all-start.1 = ((f32[128,1,512]{2,1,0:T(1,128)}), f32[128,1,512]{2,1,0:T(1,128)S(1)}, u32[]{:S(2)}, u32[]{:S(2)}) async-start(f32[128,1,512]{2,1,0:T(1,128)} %copy.23), calls=%async_computation.1 | async-start | bytes 524288 | tf_op jit(solution)/shard_map/all_to_all | solution.py:390
  104.3 0.1 copy.26
  105.0 10.1 %all-to-all-done.1 = f32[128,1,512]{2,1,0:T(1,128)S(1)} async-done(((f32[128,1,512]{2,1,0:T(1,128)}), f32[128,1,512]{2,1,0:T(1,128)S(1)}, u32[]{:S(2)}, u32[]{:S(2)}) %all-to-all-start.1) | async-done | bytes 262176 | tf_op jit(solution)/shard_map/all_to_all | solution.py:390
  115.2 0.3 broadcast_in_dim.23.refs_7_
  115.7 1.9 %copy-done.7 = f32[24,256,128]{2,1,0:T(8,128)S(1)} copy-done((f32[24,256,128]{2,1,0:T(8,128)S(1)}, f32[24,256,128]{2,1,0:T(8,128)}, u32[]{:S(2)}) %copy-start.7) | copy-done | bytes 3145752
  117.6 18.5 %network.1 = f32[240,24,128]{2,1,0:T(8,128)} custom-call(f32[24,256,128]{2,1,0:T(8,128)S(1)} %copy-done.7, s32[24,128]{1,0:T(8,128)S(1)} %get-tuple-element.26.batch_ref.refs_1_, f32[128,512]{1,0:T(8,128)S(1)} %bitcast.33, f32[256,128]{1,0:T(8,128)S(1)} %broadcast_in_dim.22.refs_3_, bf16[512,256]{1,0:T(8,128)(2,1)S(1)} %bitcast.31, ...), custom_call_target="tpu_custom_call" | custom-call | flops 6000000000 | bytes 9000000 | tf_op jit(solution)/shard_map/network/pallas_call | solution.py:396
  (58 shorter events, 1.3 us)
Async XLA Ops:
  0.0 19.2 %copy-start = (f32[4,60,24,128]{3,2,1,0:T(8,128)S(1)}, f32[4,60,24,128]{3,2,1,0:T(8,128)}, u32[]{:S(2)}) copy-start(f32[4,60,24,128]{3,2,1,0:T(8,128)} %param.11) | copy-start | bytes 8847364
  0.0 2.0 %copy-start.5 = (f32[4,60,24,128]{3,2,1,0:T(8,128)S(1)}, f32[4,60,24,128]{3,2,1,0:T(8,128)}, u32[]{:S(2)}) copy-start(f32[4,60,24,128]{3,2,1,0:T(8,128)} %param.10) | copy-start | bytes 8847364
  5.6 1.6 %copy-start.1 = (f32[24,256,128]{2,1,0:T(8,128)}, f32[24,256,128]{2,1,0:T(8,128)S(1)}, u32[]{:S(2)}) copy-start(f32[24,256,128]{2,1,0:T(8,128)S(1)} %get-tuple-element.17.q_ref) | copy-start | bytes 9437188
  7.3 10.5 %collective-permute-start.2 = (f32[64,256]{1,0:T(8,128)S(1)}, f32[64,256]{1,0:T(8,128)S(1)}, u32[]{:S(2)}, u32[]{:S(2)}) collective-permute-start(f32[64,256]{1,0:T(8,128)S(1)} %get-tuple-element.20), channel_id=1, source_target_pairs={{0,1},{1,2},{2,3},{3,4},{4,5},{5,6},{6,7},{7,8},{8,9},{9,10},{10,1... | collective-permute-start | bytes 196616 | tf_op jit(solution)/shard_map/ppermute | solution.py:295
  10.3 7.5 %collective-permute-start.3 = (f32[64,256]{1,0:T(8,128)S(1)}, f32[64,256]{1,0:T(8,128)S(1)}, u32[]{:S(2)}, u32[]{:S(2)}) collective-permute-start(f32[64,256]{1,0:T(8,128)S(1)} %get-tuple-element.20), channel_id=1, source_target_pairs={{0,15},{1,0},{2,1},{3,2},{4,3},{5,4},{6,5},{7,6},{8,7},{9,8},{10,9... | collective-permute-start | bytes 196616 | tf_op jit(solution)/shard_map/ppermute | solution.py:296
  10.3 8.9 %collective-permute-start = (f32[256,128]{1,0:T(8,128)}, f32[256,128]{1,0:T(8,128)S(1)}, u32[]{:S(2)}, u32[]{:S(2)}) collective-permute-start(f32[256,128]{1,0:T(8,128)} %get-tuple-element.18), channel_id=1, source_target_pairs={{0,16},{16,32},{32,48},{48,64},{64,80},{80,96},{96,112},{112,0},{1... | collective-permute-start | bytes 393224 | tf_op jit(solution)/shard_map/ppermute | solution.py:293
  11.6 7.6 %collective-permute-start.1 = (f32[256,128]{1,0:T(8,128)S(1)}, f32[256,128]{1,0:T(8,128)S(1)}, u32[]{:S(2)}, u32[]{:S(2)}) collective-permute-start(f32[256,128]{1,0:T(8,128)S(1)} %get-tuple-element.19), channel_id=1, source_target_pairs={{0,112},{16,0},{32,16},{48,32},{64,48},{80,64},{96,80},{112,96},{1... | collective-permute-start | bytes 393224 | tf_op jit(solution)/shard_map/ppermute | solution.py:294
  19.2 1.9 %copy-start.2 = (f32[24,256,128]{2,1,0:T(8,128)S(1)}, f32[24,256,128]{2,1,0:T(8,128)}, u32[]{:S(2)}) copy-start(f32[24,256,128]{2,1,0:T(8,128)} %copy-done.1) | copy-start | bytes 9437188
  21.1 37.3 %copy-start.11 = (bf16[4,60,512]{2,1,0:T(8,128)(2,1)S(1)}, bf16[4,60,512]{2,1,0:T(8,128)(2,1)}, u32[]{:S(2)}) copy-start(bf16[4,60,512]{2,1,0:T(8,128)(2,1)} %reshape.95) | copy-start | bytes 737284
  21.1 38.1 %copy-start.13 = (f32[240]{0:T(256)S(1)}, f32[240]{0:T(256)}, u32[]{:S(2)}) copy-start(f32[240]{0:T(256)} %param.13) | copy-start | bytes 2884
  51.7 1.6 %copy-start.3 = (f32[24,256,128]{2,1,0:T(8,128)}, f32[24,256,128]{2,1,0:T(8,128)S(1)}, u32[]{:S(2)}) copy-start(f32[24,256,128]{2,1,0:T(8,128)S(1)} %get-tuple-element.21.q_ref) | copy-start | bytes 9437188
  53.3 13.9 %collective-permute-start.4 = (f32[256,128]{1,0:T(8,128)}, f32[256,128]{1,0:T(8,128)S(1)}, u32[]{:S(2)}, u32[]{:S(2)}) collective-permute-start(f32[256,128]{1,0:T(8,128)} %get-tuple-element.22), channel_id=1, source_target_pairs={{0,16},{16,32},{32,48},{48,64},{64,80},{80,96},{96,112},{112,0},{1... | collective-permute-start | bytes 393224 | tf_op jit(solution)/shard_map/ppermute | solution.py:293
  53.3 13.9 %collective-permute-start.5 = (f32[256,128]{1,0:T(8,128)S(1)}, f32[256,128]{1,0:T(8,128)S(1)}, u32[]{:S(2)}, u32[]{:S(2)}) collective-permute-start(f32[256,128]{1,0:T(8,128)S(1)} %get-tuple-element.23), channel_id=1, source_target_pairs={{0,112},{16,0},{32,16},{48,32},{64,48},{80,64},{96,80},{112,96},{1... | collective-permute-start | bytes 393224 | tf_op jit(solution)/shard_map/ppermute | solution.py:294
  61.1 6.1 %copy-start.4 = (f32[24,256,128]{2,1,0:T(8,128)S(1)}, f32[24,256,128]{2,1,0:T(8,128)}, u32[]{:S(2)}) copy-start(f32[24,256,128]{2,1,0:T(8,128)} %copy-done.3) | copy-start | bytes 9437188
  61.1 4.8 %collective-permute-start.6 = (f32[64,256]{1,0:T(8,128)S(1)}, f32[64,256]{1,0:T(8,128)S(1)}, u32[]{:S(2)}, u32[]{:S(2)}) collective-permute-start(f32[64,256]{1,0:T(8,128)S(1)} %get-tuple-element.24), channel_id=1, source_target_pairs={{0,1},{1,2},{2,3},{3,4},{4,5},{5,6},{6,7},{7,8},{8,9},{9,10},{10,1... | collective-permute-start | bytes 196616 | tf_op jit(solution)/shard_map/ppermute | solution.py:295
  63.6 3.7 %collective-permute-start.7 = (f32[64,256]{1,0:T(8,128)S(1)}, f32[64,256]{1,0:T(8,128)S(1)}, u32[]{:S(2)}, u32[]{:S(2)}) collective-permute-start(f32[64,256]{1,0:T(8,128)S(1)} %get-tuple-element.24), channel_id=1, source_target_pairs={{0,15},{1,0},{2,1},{3,2},{4,3},{5,4},{6,5},{7,6},{8,7},{9,8},{10,9... | collective-permute-start | bytes 196616 | tf_op jit(solution)/shard_map/ppermute | solution.py:296
  64.6 0.7 copy-start.8
  75.3 1.6 %copy-start.6 = (f32[24,256,128]{2,1,0:T(8,128)}, f32[24,256,128]{2,1,0:T(8,128)S(1)}, u32[]{:S(2)}) copy-start(f32[24,256,128]{2,1,0:T(8,128)S(1)} %get-tuple-element.27.refs_0_) | copy-start | bytes 9437188
  77.9 26.3 %copy-start.10 = (bf16[4,60,512]{2,1,0:T(8,128)(2,1)S(1)}, bf16[4,60,512]{2,1,0:T(8,128)(2,1)}, u32[]{:S(2)}) copy-start(bf16[4,60,512]{2,1,0:T(8,128)(2,1)} %reshape.96) | copy-start | bytes 737284
  77.9 20.6 %all-to-all-start = ((f32[128,1,512]{2,1,0:T(1,128)}), f32[128,1,512]{2,1,0:T(1,128)S(1)}, u32[]{:S(2)}, u32[]{:S(2)}) async-start(f32[128,1,512]{2,1,0:T(1,128)} %copy.21), calls=%async_computation | async-start | bytes 524288 | tf_op jit(solution)/shard_map/all_to_all | solution.py:379
  87.5 16.7 %copy-start.9 = (bf16[8,4,8,512]{3,2,0,1:T(8,128)(2,1)S(1)}, bf16[8,4,8,512]{3,2,0,1:T(8,128)(2,1)}, u32[]{:S(2)}) copy-start(bf16[8,4,8,512]{3,2,0,1:T(8,128)(2,1)} %multiply_bitcast_fusion) | copy-start | bytes 786436
  87.5 16.9 %copy-start.14 = (f32[240]{0:T(256)S(1)}, f32[240]{0:T(256)}, u32[]{:S(2)}) copy-start(f32[240]{0:T(256)} %param.14) | copy-start | bytes 2884
  87.5 17.2 %copy-start.15 = (f32[240]{0:T(256)S(1)}, f32[240]{0:T(256)}, u32[]{:S(2)}) copy-start(f32[240]{0:T(256)} %param.19) | copy-start | bytes 2884
  89.1 15.9 %copy-start.12 = (f32[4,512]{1,0:T(4,128)S(1)}, f32[4,512]{1,0:T(4,128)}, u32[]{:S(2)}) copy-start(f32[4,512]{1,0:T(4,128)} %param.18) | copy-start | bytes 24580
  99.6 15.6 %all-to-all-start.1 = ((f32[128,1,512]{2,1,0:T(1,128)}), f32[128,1,512]{2,1,0:T(1,128)S(1)}, u32[]{:S(2)}, u32[]{:S(2)}) async-start(f32[128,1,512]{2,1,0:T(1,128)} %copy.23), calls=%async_computation.1 | async-start | bytes 524288 | tf_op jit(solution)/shard_map/all_to_all | solution.py:390
  115.7 1.9 %copy-start.7 = (f32[24,256,128]{2,1,0:T(8,128)S(1)}, f32[24,256,128]{2,1,0:T(8,128)}, u32[]{:S(2)}) copy-start(f32[24,256,128]{2,1,0:T(8,128)} %copy-done.6) | copy-start | bytes 9437188
where the time goes:
time: 137 us; the launch traced here: 136 us
  Pallas kernels  61.4 us (45%)
  starting transfers between devices  31.6 us (23%)
  waiting for transfers between devices  22.2 us (16%)
  local copies, waits for them, and re-layouts  18.3 us (13%)
  other arithmetic  2.35 us (2%)
    pallas_call x1, Pallas kernels, body(): pl.pallas_call(first_kernel, grid=(CHUNKS,), in_specs=state_specs, out_sp...  30.6 us
    pallas_call x1, Pallas kernels, body(): pl.pallas_call(network_outer, grid=(3,), in_specs=[pl.BlockSpec((8, FEATS...  18.5 us
    unnamed x34, local copies, waits for them, and re-layouts  11.5 us
    all_to_all x1, waiting for transfers between devices, body(): lax.all_to_all(merged, ('bx', 'by'), split_axis=0, concat_axis=0, tiled=T...  10.1 us
    all_to_all x1, starting transfers between devices, body(): lax.all_to_all(stats, ('bx', 'by'), split_axis=0, concat_axis=0, tiled=True)  9.62 us
    ppermute x2, starting transfers between devices, halos(): down = lax.ppermute(first, 'bx', ring('bx', -1))  9.54 us
    all_to_all x1, waiting for transfers between devices, body(): lax.all_to_all(stats, ('bx', 'by'), split_axis=0, concat_axis=0, tiled=True)  9.34 us
    pallas_call x1, Pallas kernels, body(): pl.pallas_call(functools.partial(second_kernel, share), grid=(CHUNKS,), i...  7.98 us
  transfers between devices with their start and end apart: 10, of which 4 were waited for; matrix products, arithmetic and copies ran while one was open for 5% of the time, Pallas kernels for 0%

commit v1 on v0

--- a/solution.py
+++ b/solution.py
@@ -19,7 +19,7 @@
 NN = (((1,), (0,)), ((), ()))
 
 
-def params(limit=32):
+def params(limit=60):
     return pltpu.CompilerParams(
         dimension_semantics=("arbitrary",), vmem_limit_bytes=limit * MIB
     )
@@ -49,34 +49,37 @@
             ref[:, COLS * h : COLS * (h + 1)] = self.halves[h]
 
 
-def pack_kernel(x_ref, q_ref, first_ref, last_ref, cols_ref):
+def store_rows(parity_ref, tiles, near_ref, far_ref):
+    even = jnp.full((32, COLS), parity_ref[0], jnp.int32) == 0
+    near_ref[...] = jnp.where(even, tiles[ROWS - 1], tiles[0])
+    far_ref[...] = jnp.where(even, tiles[0], tiles[ROWS - 1])
+
+
+def pack_kernel(parity_ref, x_ref, q_ref, near_ref, far_ref, cols_ref):
     valid = valid_rows(pl.program_id(0))
     packer = ColumnPacker()
     for i in range(ROWS):
         for f in range(FIELDS):
             tile = jnp.where(valid, x_ref[f, pl.ds(i, 8, stride=ROWS), :], 0.0)
             q_ref[i, 8 * f : 8 * f + 8, :] = tile
-            if i == 0:
-                first_ref[8 * f : 8 * f + 8, :] = tile
-            if i == ROWS - 1:
-                last_ref[8 * f : 8 * f + 8, :] = tile
             packer.add(i, f, tile)
     packer.store(cols_ref)
-
-
-def advance_tiles(q_ref, rates_ref, up_ref, down_ref, left_ref, right_ref, emit):
+    store_rows(parity_ref, q_ref, near_ref, far_ref)
+
+
+def advance_tiles(parity_ref, q_ref, rates_ref, near_ref, far_ref, core_ref, chip_ref, emit):
     valid = valid_rows(pl.program_id(0))
     lane = lanes_of((8, COLS))
     even = lane % 2 == 0
+    even_x = jnp.full((8, COLS), parity_ref[0], jnp.int32) == 0
+    even_y = jnp.full((8, COLS), parity_ref[1], jnp.int32) == 0
     ring = []
     for h in range(2):
         part = slice(COLS * h, COLS * (h + 1))
+        right = jnp.where(even_y, core_ref[:, part], chip_ref[:, part])
+        left = jnp.where(even_y, chip_ref[:, part], core_ref[:, part])
         ring.append(
-            jnp.where(
-                even,
-                pltpu.roll(right_ref[:, part], COLS - 1, axis=1),
-                pltpu.roll(left_ref[:, part], 1, axis=1),
-            )
+            jnp.where(even, pltpu.roll(right, COLS - 1, axis=1), pltpu.roll(left, 1, axis=1))
         )
     for i in range(ROWS):
         rate = [rates_ref[k, pl.ds(i, 8, stride=ROWS), :] for k in range(4)]
@@ -84,8 +87,14 @@
             rows = slice(8 * f, 8 * f + 8)
             m = 4 * (i % HALF) + f
             here = q_ref[i, rows, :]
-            above = up_ref[rows, :] if i == 0 else q_ref[i - 1, rows, :]
-            below = down_ref[rows, :] if i == ROWS - 1 else q_ref[i + 1, rows, :]
+            if i == 0:
+                above = jnp.where(even_x, far_ref[rows, :], near_ref[rows, :])
+            else:
+                above = q_ref[i - 1, rows, :]
+            if i == ROWS - 1:
+                below = jnp.where(even_x, near_ref[rows, :], far_ref[rows, :])
+            else:
+                below = q_ref[i + 1, rows, :]
             edge = pltpu.roll(ring[i // HALF], COLS - (2 * m + 1), axis=1)
             after = jnp.where(lane == COLS - 1, edge, pltpu.roll(here, COLS - 1, axis=1))
             before = jnp.where(lane == 0, edge, pltpu.roll(here, 1, axis=1))
@@ -100,30 +109,39 @@
 
 
 def first_kernel(
-    q_ref, rates_ref, up_ref, down_ref, left_ref, right_ref, out_ref, first_ref, last_ref, cols_ref
+    parity_ref,
+    q_ref,
+    rates_ref,
+    near_ref,
+    far_ref,
+    core_ref,
+    chip_ref,
+    out_ref,
+    near_out_ref,
+    far_out_ref,
+    cols_ref,
 ):
-    packer = ColumnPacker()
-
     def emit(i, f, tile):
         out_ref[i, 8 * f : 8 * f + 8, :] = tile
-        if i == 0:
-            first_ref[8 * f : 8 * f + 8, :] = tile
-        if i == ROWS - 1:
-            last_ref[8 * f : 8 * f + 8, :] = tile
-        packer.add(i, f, tile)
-
-    advance_tiles(q_ref, rates_ref, up_ref, down_ref, left_ref, right_ref, emit)
+
+    advance_tiles(parity_ref, q_ref, rates_ref, near_ref, far_ref, core_ref, chip_ref, emit)
+    store_rows(parity_ref, out_ref, near_out_ref, far_out_ref)
+    packer = ColumnPacker()
+    for i in range(ROWS):
+        for f in range(FIELDS):
+            packer.add(i, f, out_ref[i, 8 * f : 8 * f + 8, :])
     packer.store(cols_ref)
 
 
 def second_kernel(
     share,
+    parity_ref,
     q_ref,
     rates_ref,
-    up_ref,
-    down_ref,
-    left_ref,
-    right_ref,
+    near_ref,
+    far_ref,
+    core_ref,
+    chip_ref,
     hot_ref,
     batch_ref,
     out_ref,
@@ -143,7 +161,7 @@
             start = pl.multiple_of(32 * chunk + 8 * (f - 1), 16)
             x_ref[pl.ds(start, 16), COLS * i : COLS * (i + 1)] = both
 
-    advance_tiles(q_ref, rates_ref, up_ref, down_ref, left_ref, right_ref, emit)
+    advance_tiles(parity_ref, q_ref, rates_ref, near_ref, far_ref, core_ref, chip_ref, emit)
 
     @pl.when(chunk == CHUNKS - 1)
     def _():
@@ -162,8 +180,16 @@
         spread = lax.dot_general(
             hi_ref[...], hot, NT, preferred_element_type=jnp.float32
         ) + lax.dot_general(lo_ref[...], hot, NT, preferred_element_type=jnp.float32)
-        stats_ref[:, :FEATS] = mean.T
-        stats_ref[:, FEATS:] = spread.T
+        store_parts(stats_ref, (mean[:COLS].T, mean[COLS:].T, spread[:COLS].T, spread[COLS:].T))
+
+
+def store_parts(ref, parts):
+    for k, part in enumerate(parts):
+        ref[pl.ds(k, part.shape[0], stride=4), :] = part
+
+
+def load_parts(ref):
+    return [ref[pl.ds(k, ref.shape[0] // 4, stride=4), :] for k in range(4)]
 
 
 def batch_kernel(order_ref, owner_ref, batch_ref, hot_ref):
@@ -185,14 +211,17 @@
 
 
 def merge_kernel(share, stats_ref, gain_ref, out_ref):
-    count = stats_ref.shape[0]
-    means = stats_ref[:, :FEATS]
-    mean = jnp.sum(means, axis=0, keepdims=True) * (1.0 / count)
-    away = means - mean
-    total = jnp.sum(stats_ref[:, FEATS:] + share * (away * away), axis=0, keepdims=True)
-    scale = lax.rsqrt(total * (1.0 / (count * share)) + 1e-05) * gain_ref[...]
-    out_ref[:, :FEATS] = jnp.broadcast_to(mean, (count, FEATS))
-    out_ref[:, FEATS:] = jnp.broadcast_to(scale, (count, FEATS))
+    count = stats_ref.shape[0] // 4
+    parts = load_parts(stats_ref)
+    merged = []
+    for k in range(2):
+        mean = jnp.sum(parts[k], axis=0, keepdims=True) * (1.0 / count)
+        away = parts[k] - mean
+        total = jnp.sum(parts[k + 2] + share * (away * away), axis=0, keepdims=True)
+        gain = gain_ref[:, COLS * k : COLS * (k + 1)]
+        merged.append((mean, lax.rsqrt(total * (1.0 / (count * share)) + 1e-05) * gain))
+    values = (merged[0][0], merged[1][0], merged[0][1], merged[1][1])
+    store_parts(out_ref, [jnp.broadcast_to(v, (count, COLS)) for v in values])
 
 
 def network_kernel(
@@ -213,8 +242,10 @@
 
     @pl.when(step == 0)
     def _():
-        mean_ref[...] = stats_ref[:, :FEATS].T
-        scale_ref[...] = stats_ref[:, FEATS:].T
+        parts = load_parts(stats_ref)
+        for k in range(2):
+            mean_ref[COLS * k : COLS * (k + 1), :] = parts[k].T
+            scale_ref[COLS * k : COLS * (k + 1), :] = parts[k + 2].T
 
     mean = mean_ref[...]
     scale = scale_ref[...]
@@ -271,6 +302,7 @@
     return pl.BlockSpec(shape, lambda c: (0,) * len(shape))
 
 
+SCALAR_SPEC = pl.BlockSpec(memory_space=pltpu.SMEM)
 GRID_SPEC = pl.BlockSpec((ROWS, 32, COLS), lambda c: (0, c, 0))
 NATIVE_SPEC = pl.BlockSpec((4, 8 * ROWS, COLS), lambda c: (0, c, 0))
 ROW_SPEC = pl.BlockSpec((32, COLS), lambda c: (c, 0))
@@ -284,17 +316,20 @@
     return pl.CostEstimate(flops=flops, bytes_accessed=size, transcendentals=0)
 
 
-def ring(axis, by):
+def swap(values, axis, first):
     count = lax.axis_size(axis)
-    return [(i, (i + by) % count) for i in range(count)]
-
-
-def halos(first, last, cols):
-    up = lax.ppermute(last, "bx", ring("bx", 1))
-    down = lax.ppermute(first, "bx", ring("bx", -1))
-    left = lax.ppermute(cols, "by", ring("by", 1))
-    right = lax.ppermute(cols, "by", ring("by", -1))
-    return up, down, left, right
+    step = 0 if first else 1
+    pairs = [((i + step) % count, (i + 1 + step) % count) for i in range(0, count, 2)]
+    return lax.ppermute(values, axis, pairs + [(b, a) for a, b in pairs])
+
+
+def halos(near, far, cols):
+    return (
+        swap(near, "bx", True),
+        swap(far, "bx", False),
+        swap(cols, "by", True),
+        swap(cols, "by", False),
+    )
 
 
 def by_row(values):
@@ -323,18 +358,19 @@
     width = weight_first.shape[0]
     x = tracers.reshape(FIELDS, LEVELS * ROWS, COLS)
     r = rates.reshape(4, LEVELS * ROWS, COLS)
-
-    q, first, last, cols = pl.pallas_call(
+    parity = jnp.stack([lax.axis_index("bx"), lax.axis_index("by")]).astype(jnp.int32) % 2
+
+    q, near, far, cols = pl.pallas_call(
         pack_kernel,
         grid=(CHUNKS,),
-        in_specs=[NATIVE_SPEC],
+        in_specs=[SCALAR_SPEC, NATIVE_SPEC],
         out_specs=[GRID_SPEC, ROW_SPEC, ROW_SPEC, COL_SPEC],
         out_shape=[GRID_SHAPE, ROW_SHAPE, ROW_SHAPE, COL_SHAPE],
         compiler_params=params(),
         cost_estimate=cost(10**6, 6 * 10**6),
         name="pack_edges",
-    )(x)
-    edges = halos(first, last, cols)
+    )(parity, x)
+    edges = halos(near, far, cols)
 
     owner = (jnp.arange(columns, dtype=jnp.int32) // share).astype(jnp.float32)[None, :]
     batch, hot = pl.pallas_call(
@@ -351,8 +387,8 @@
         name="batch_ids",
     )(column_order, owner)
 
-    state_specs = [GRID_SPEC, NATIVE_SPEC, ROW_SPEC, ROW_SPEC, COL_SPEC, COL_SPEC]
-    q, first, last, cols = pl.pallas_call(
+    state_specs = [SCALAR_SPEC, GRID_SPEC, NATIVE_SPEC, ROW_SPEC, ROW_SPEC, COL_SPEC, COL_SPEC]
+    q, near, far, cols = pl.pallas_call(
         first_kernel,
         grid=(CHUNKS,),
         in_specs=state_specs,
@@ -361,28 +397,28 @@
         compiler_params=params(),
         cost_estimate=cost(10**7, 9 * 10**6),
         name="first_substep",
-    )(q, r, *edges)
-    edges = halos(first, last, cols)
+    )(parity, q, r, *edges)
+    edges = halos(near, far, cols)
 
     moved, stats = pl.pallas_call(
         functools.partial(second_kernel, share),
         grid=(CHUNKS,),
         in_specs=state_specs + [whole((COLS, columns)), whole((ROWS, COLS))],
-        out_specs=[GRID_SPEC, whole((COLS, 2 * FEATS))],
-        out_shape=[GRID_SHAPE, jax.ShapeDtypeStruct((COLS, 2 * FEATS), jnp.float32)],
+        out_specs=[GRID_SPEC, whole((4 * count, COLS))],
+        out_shape=[GRID_SHAPE, jax.ShapeDtypeStruct((4 * count, COLS), jnp.float32)],
         scratch_shapes=[pltpu.VMEM((FEATS, columns), jnp.bfloat16) for _ in range(3)],
         compiler_params=params(),
         cost_estimate=cost(10**9, 9 * 10**6),
         name="second_substep",
-    )(q, r, *edges, hot, batch)
+    )(parity, q, r, *edges, hot, batch)
 
     gathered = lax.all_to_all(stats, ("bx", "by"), split_axis=0, concat_axis=0, tiled=True)
     merged = pl.pallas_call(
         functools.partial(merge_kernel, float(share)),
         grid=(1,),
-        in_specs=[whole((count, 2 * FEATS)), whole((1, FEATS))],
-        out_specs=whole((count, 2 * FEATS)),
-        out_shape=jax.ShapeDtypeStruct((count, 2 * FEATS), jnp.float32),
+        in_specs=[whole((4 * count, COLS)), whole((1, FEATS))],
+        out_specs=whole((4 * count, COLS)),
+        out_shape=jax.ShapeDtypeStruct((4 * count, COLS), jnp.float32),
         compiler_params=params(),
         cost_estimate=cost(10**6, 10**6),
         name="merge_statistics",
@@ -399,7 +435,7 @@
         in_specs=[
             pl.BlockSpec((8, FEATS, COLS), lambda c: (c, 0, 0)),
             pl.BlockSpec((8, COLS), lambda c: (c, 0)),
-            whole((count, 2 * FEATS)),
+            whole((4 * count, COLS)),
             whole((FEATS, COLS)),
             whole((width, FEATS)),
             whole((3, width, width)),

time: 137 us -> 113 us (0.82)
  Pallas kernels: 61.4 us -> 50.1 us
  local copies, waits for them, and re-layouts: 18.3 us -> 7.18 us
  starting transfers between devices: 31.6 us -> 29.9 us
    pallas_call x1, Pallas kernels: 30.6 us -> 8.62 us  [body(): pl.pallas_call(first_kernel, grid=(CHUNKS,), in_specs=state_specs, out_sp...]
    unnamed x34, local copies, waits for them, and re-layouts: 11.5 us -> 3.28 us
    pallas_call x1, Pallas kernels: 7.98 us -> 12.3 us  [body(): pl.pallas_call(functools.partial(second_kernel, share), grid=(CHUNKS,), i...]
    pallas_call x1, Pallas kernels: 3.66 us -> 6.8 us  [body(): pl.pallas_call(pack_kernel, grid=(CHUNKS,), in_specs=[SCALAR_SPEC, NATIVE...]
    all_to_all x1, starting transfers between devices: 9.62 us -> 6.57 us  [body(): lax.all_to_all(stats, ('bx', 'by'), split_axis=0, concat_axis=0, tiled=True)]
    reshape x5, local copies, waits for them, and re-layouts: 3.65 us -> 1.08 us  [by_row(): values = values.reshape(FIELDS, LEVELS, *rest)]
    all_to_all x2 -> x0, local copies, waits for them, and re-layouts: 1.95 us -> none  [the longest x1 0.98 us: body(): lax.all_to_all(merged, ('bx', 'by'), split_axis=0, concat_axis=0, tiled=T...]
    pallas_call x1, Pallas kernels: 0.08 us -> 1.73 us  [body(): pl.pallas_call(functools.partial(merge_kernel, float(share)), grid=(1,),...]
  transfers between devices with their start and end apart: 10 -> 10, of which waited for: 4 -> 4; matrix products, arithmetic and copies ran while one was open for 5% -> 4% of each run, Pallas kernels for 0% -> 2%
where the time goes in v1:
time: 113 us; the launch traced here: 112 us
  Pallas kernels  50.1 us (44%)
  starting transfers between devices  29.9 us (26%)
  waiting for transfers between devices  23.4 us (21%)
  local copies, waits for them, and re-layouts  7.18 us (6%)
  other arithmetic  1.46 us (1%)
    ppermute x8, starting transfers between devices, swap(): return lax.ppermute(values, axis, pairs + [(b, a) for a, b in pairs])  18.7 us
    pallas_call x1, Pallas kernels, body(): pl.pallas_call(network_outer, grid=(3,), in_specs=[pl.BlockSpec((8, FEATS...  18.4 us
    pallas_call x1, Pallas kernels, body(): pl.pallas_call(functools.partial(second_kernel, share), grid=(CHUNKS,), i...  12.3 us
    all_to_all x1, waiting for transfers between devices, body(): lax.all_to_all(stats, ('bx', 'by'), split_axis=0, concat_axis=0, tiled=True)  10.6 us
    all_to_all x1, waiting for transfers between devices, body(): lax.all_to_all(merged, ('bx', 'by'), split_axis=0, concat_axis=0, tiled=T...  9.19 us
    pallas_call x1, Pallas kernels, body(): pl.pallas_call(first_kernel, grid=(CHUNKS,), in_specs=state_specs, out_sp...  8.62 us
    pallas_call x1, Pallas kernels, body(): pl.pallas_call(pack_kernel, grid=(CHUNKS,), in_specs=[SCALAR_SPEC, NATIVE...  6.8 us
    all_to_all x1, starting transfers between devices, body(): lax.all_to_all(stats, ('bx', 'by'), split_axis=0, concat_axis=0, tiled=True)  6.57 us
  transfers between devices with their start and end apart: 10, of which 4 were waited for; matrix products, arithmetic and copies ran while one was open for 4% of the time, Pallas kernels for 2%

profile of v1, /device:TPU:1, one launch (start us, length us, event | category | flops | bytes accessed | tf_op | source)
XLA Modules:
  0.0 112.4 jit_solution(1977715454982613432)
XLA Ops:
  0.0 0.7 and_select_fusion.1.parity_ref
  0.7 6.8 %pack_edges.1 = (f32[24,256,128]{2,1,0:T(8,128)}, f32[256,128]{1,0:T(8,128)}, f32[256,128]{1,0:T(8,128)}, f32[64,256]{1,0:T(8,128)}) custom-call(s32[2]{0:T(128)} %and_select_fusion.1.parity_ref, f32[4,1440,128]{2,1,0:T(8,128)} %bitcast.29), custom_call_target="tpu_custom_call" | custom-call | flops 1000000 | bytes 6000000 | tf_op jit(solution)/shard_map/pack_edges/pallas_call | solution.py:363
  7.5 1.4 %collective-permute-start.2 = (f32[64,256]{1,0:T(8,128)}, f32[64,256]{1,0:T(8,128)S(1)}, u32[]{:S(2)}, u32[]{:S(2)}) collective-permute-start(f32[64,256]{1,0:T(8,128)} %get-tuple-element.20), channel_id=1, source_target_pairs={{0,1},{2,3},{4,5},{6,7},{8,9},{10,11},{12,13},{14,15},{1,0},{3,2},... | collective-permute-start | bytes 196616 | tf_op jit(solution)/shard_map/ppermute | solution.py:323
  8.9 1.7 %collective-permute-start.3 = (f32[64,256]{1,0:T(8,128)}, f32[64,256]{1,0:T(8,128)S(1)}, u32[]{:S(2)}, u32[]{:S(2)}) collective-permute-start(f32[64,256]{1,0:T(8,128)} %get-tuple-element.20), channel_id=1, source_target_pairs={{1,2},{3,4},{5,6},{7,8},{9,10},{11,12},{13,14},{15,0},{2,1},{4,3},... | collective-permute-start | bytes 196616 | tf_op jit(solution)/shard_map/ppermute | solution.py:323
  10.6 1.3 %collective-permute-start = (f32[256,128]{1,0:T(8,128)}, f32[256,128]{1,0:T(8,128)S(1)}, u32[]{:S(2)}, u32[]{:S(2)}) collective-permute-start(f32[256,128]{1,0:T(8,128)} %get-tuple-element.18), channel_id=1, source_target_pairs={{0,16},{32,48},{64,80},{96,112},{16,0},{48,32},{80,64},{112,96},{1... | collective-permute-start | bytes 393224 | tf_op jit(solution)/shard_map/ppermute | solution.py:323
  11.9 4.9 %collective-permute-start.1 = (f32[256,128]{1,0:T(8,128)}, f32[256,128]{1,0:T(8,128)S(1)}, u32[]{:S(2)}, u32[]{:S(2)}) collective-permute-start(f32[256,128]{1,0:T(8,128)} %get-tuple-element.19), channel_id=1, source_target_pairs={{16,32},{48,64},{80,96},{112,0},{32,16},{64,48},{96,80},{0,112},{1... | collective-permute-start | bytes 393224 | tf_op jit(solution)/shard_map/ppermute | solution.py:323
  16.8 0.6 fusion.owner_ref
  17.5 2.0 %collective-permute-done.1.far_ref = f32[256,128]{1,0:T(8,128)S(1)} collective-permute-done((f32[256,128]{1,0:T(8,128)}, f32[256,128]{1,0:T(8,128)S(1)}, u32[]{:S(2)}, u32[]{:S(2)}) %collective-permute-start.1) | collective-permute-done | bytes 131104 | tf_op jit(solution)/shard_map/ppermute | solution.py:323
  19.5 0.6 copy-done.8
  20.2 8.6 %first_substep.1 = (f32[24,256,128]{2,1,0:T(8,128)}, f32[256,128]{1,0:T(8,128)}, f32[256,128]{1,0:T(8,128)}, f32[64,256]{1,0:T(8,128)}) custom-call(s32[2]{0:T(128)} %and_select_fusion.1.parity_ref, f32[24,256,128]{2,1,0:T(8,128)} %get-tuple-element.17.q_ref, f32[4,1440,128]{2,1,0:T(8,128)} %bitcast.27, f32[256,128]{1,0:T(8,128)} %copy-done.7, ...), custom_call_target="tpu_custom_call" | custom-call | flops 10000000 | bytes 9000000 | tf_op jit(solution)/shard_map/first_substep/pallas_call | solution.py:391
  28.9 5.0 %collective-permute-start.5 = (f32[256,128]{1,0:T(8,128)}, f32[256,128]{1,0:T(8,128)S(1)}, u32[]{:S(2)}, u32[]{:S(2)}) collective-permute-start(f32[256,128]{1,0:T(8,128)} %get-tuple-element.23), channel_id=1, source_target_pairs={{16,32},{48,64},{80,96},{112,0},{32,16},{64,48},{96,80},{0,112},{1... | collective-permute-start | bytes 393224 | tf_op jit(solution)/shard_map/ppermute | solution.py:323
  34.1 0.7 broadcast_in_dim_reshape.2.gain_ref
  34.8 0.8 reshape.96
  35.6 4.3 %collective-permute-start.6 = (f32[64,256]{1,0:T(8,128)}, f32[64,256]{1,0:T(8,128)S(1)}, u32[]{:S(2)}, u32[]{:S(2)}) collective-permute-start(f32[64,256]{1,0:T(8,128)} %get-tuple-element.24), channel_id=1, source_target_pairs={{0,1},{2,3},{4,5},{6,7},{8,9},{10,11},{12,13},{14,15},{1,0},{3,2},... | collective-permute-start | bytes 196616 | tf_op jit(solution)/shard_map/ppermute | solution.py:323
  39.9 2.2 %batch_ids.1 = (s32[24,128]{1,0:T(8,128)}, bf16[128,3072]{1,0:T(8,128)(2,1)}) custom-call(s32[1,3072]{1,0:T(1,128)} %order_ref.1, f32[1,3072]{1,0:T(1,128)} %fusion.owner_ref), custom_call_target="tpu_custom_call" | custom-call | flops 1000000000 | bytes 2000000 | tf_op jit(solution)/shard_map/batch_ids/pallas_call | solution.py:376
  42.1 1.7 %collective-permute-done.7.chip_ref = f32[64,256]{1,0:T(8,128)S(1)} collective-permute-done((f32[64,256]{1,0:T(8,128)}, f32[64,256]{1,0:T(8,128)S(1)}, u32[]{:S(2)}, u32[]{:S(2)}) %collective-permute-start.7) | collective-permute-done | bytes 65568 | tf_op jit(solution)/shard_map/ppermute | solution.py:323
  43.9 0.6 copy-done.12
  44.6 12.3 %second_substep.1 = (f32[24,256,128]{2,1,0:T(8,128)}, f32[512,128]{1,0:T(8,128)}) custom-call(s32[2]{0:T(128)} %and_select_fusion.1.parity_ref, f32[24,256,128]{2,1,0:T(8,128)} %get-tuple-element.21.q_ref, f32[4,1440,128]{2,1,0:T(8,128)} %bitcast.28, f32[256,128]{1,0:T(8,128)} %copy-done.5, f32[256,128]{1,0:T(8,128)} %copy-done.6, f32[64,256]{1,0:T(8,128)} %copy-done.11, ...), custom_call_target="tpu_custom_call" | custom-call | flops 1000000000 | bytes 9000000 | tf_op jit(solution)/shard_map/second_substep/pallas_call | solution.py:403
  56.9 6.6 %all-to-all-start = ((f32[128,4,128]{2,1,0:T(4,128)}), f32[128,4,128]{2,1,0:T(4,128)}, u32[]{:S(2)}, u32[]{:S(2)}) async-start(f32[128,4,128]{2,1,0:T(4,128)} %bitcast.32), calls=%async_computation | async-start | bytes 524288 | tf_op jit(solution)/shard_map/all_to_all | solution.py:415
  63.5 0.1 broadcast_multiply_fusion.refs_5_
  63.7 10.6 %all-to-all-done = f32[128,4,128]{2,1,0:T(4,128)} async-done(((f32[128,4,128]{2,1,0:T(4,128)}), f32[128,4,128]{2,1,0:T(4,128)}, u32[]{:S(2)}, u32[]{:S(2)}) %all-to-all-start) | async-done | bytes 262176 | tf_op jit(solution)/shard_map/all_to_all | solution.py:415
  74.2 1.7 %merge_statistics.1 = f32[512,128]{1,0:T(8,128)} custom-call(f32[512,128]{1,0:T(8,128)} %bitcast.5.stats_ref, f32[1,256]{1,0:T(1,128)} %broadcast_in_dim_reshape.2.gain_ref), custom_call_target="tpu_custom_call" | custom-call | flops 1000000 | bytes 1000000 | tf_op jit(solution)/shard_map/merge_statistics/pallas_call | solution.py:416
  76.0 4.6 %all-to-all-start.1 = ((f32[128,4,128]{2,1,0:T(4,128)}), f32[128,4,128]{2,1,0:T(4,128)S(1)}, u32[]{:S(2)}, u32[]{:S(2)}) async-start(f32[128,4,128]{2,1,0:T(4,128)} %bitcast.30), calls=%async_computation.1 | async-start | bytes 524288 | tf_op jit(solution)/shard_map/all_to_all | solution.py:426
  80.6 1.0 pad_bitcast_fusion
  81.6 0.1 copy.18
  81.9 0.1 broadcast_in_dim.10
  82.2 0.1 broadcast_in_dim.24
  82.3 9.2 %all-to-all-done.1 = f32[128,4,128]{2,1,0:T(4,128)S(1)} async-done(((f32[128,4,128]{2,1,0:T(4,128)}), f32[128,4,128]{2,1,0:T(4,128)S(1)}, u32[]{:S(2)}, u32[]{:S(2)}) %all-to-all-start.1) | async-done | bytes 262176 | tf_op jit(solution)/shard_map/all_to_all | solution.py:426
  91.5 0.3 broadcast_in_dim.23.refs_7_
  91.9 0.1 broadcast_in_dim.22.refs_3_
  92.1 1.9 %copy-done.1 = f32[24,256,128]{2,1,0:T(8,128)S(1)} copy-done((f32[24,256,128]{2,1,0:T(8,128)S(1)}, f32[24,256,128]{2,1,0:T(8,128)}, u32[]{:S(2)}) %copy-start.1) | copy-done | bytes 3145752
  94.0 18.4 %network.1 = f32[240,24,128]{2,1,0:T(8,128)} custom-call(f32[24,256,128]{2,1,0:T(8,128)S(1)} %copy-done.1, s32[24,128]{1,0:T(8,128)S(1)} %copy-done, f32[512,128]{1,0:T(8,128)S(1)} %bitcast.24, f32[256,128]{1,0:T(8,128)S(1)} %broadcast_in_dim.22.refs_3_, bf16[512,256]{1,0:T(8,128)(2,1)S(1)} %bitcast.25, ...), custom_call_target="tpu_custom_call" | custom-call | flops 6000000000 | bytes 9000000 | tf_op jit(solution)/shard_map/network/pallas_call | solution.py:432
  (57 shorter events, 1.0 us)
Async XLA Ops:
  0.0 17.4 %copy-start.3 = (bf16[512,240]{0,1:T(8,128)(2,1)S(1)}, bf16[512,240]{0,1:T(8,128)(2,1)}, u32[]{:S(2)}) copy-start(bf16[512,240]{0,1:T(8,128)(2,1)} %param.15) | copy-start | bytes 737284
  7.5 10.0 %collective-permute-start.2 = (f32[64,256]{1,0:T(8,128)}, f32[64,256]{1,0:T(8,128)S(1)}, u32[]{:S(2)}, u32[]{:S(2)}) collective-permute-start(f32[64,256]{1,0:T(8,128)} %get-tuple-element.20), channel_id=1, source_target_pairs={{0,1},{2,3},{4,5},{6,7},{8,9},{10,11},{12,13},{14,15},{1,0},{3,2},... | collective-permute-start | bytes 196616 | tf_op jit(solution)/shard_map/ppermute | solution.py:323
  8.9 8.6 %collective-permute-start.3 = (f32[64,256]{1,0:T(8,128)}, f32[64,256]{1,0:T(8,128)S(1)}, u32[]{:S(2)}, u32[]{:S(2)}) collective-permute-start(f32[64,256]{1,0:T(8,128)} %get-tuple-element.20), channel_id=1, source_target_pairs={{1,2},{3,4},{5,6},{7,8},{9,10},{11,12},{13,14},{15,0},{2,1},{4,3},... | collective-permute-start | bytes 196616 | tf_op jit(solution)/shard_map/ppermute | solution.py:323
  10.6 6.9 %collective-permute-start = (f32[256,128]{1,0:T(8,128)}, f32[256,128]{1,0:T(8,128)S(1)}, u32[]{:S(2)}, u32[]{:S(2)}) collective-permute-start(f32[256,128]{1,0:T(8,128)} %get-tuple-element.18), channel_id=1, source_target_pairs={{0,16},{32,48},{64,80},{96,112},{16,0},{48,32},{80,64},{112,96},{1... | collective-permute-start | bytes 393224 | tf_op jit(solution)/shard_map/ppermute | solution.py:323
  11.9 7.6 %collective-permute-start.1 = (f32[256,128]{1,0:T(8,128)}, f32[256,128]{1,0:T(8,128)S(1)}, u32[]{:S(2)}, u32[]{:S(2)}) collective-permute-start(f32[256,128]{1,0:T(8,128)} %get-tuple-element.19), channel_id=1, source_target_pairs={{16,32},{48,64},{80,96},{112,0},{32,16},{64,48},{96,80},{0,112},{1... | collective-permute-start | bytes 393224 | tf_op jit(solution)/shard_map/ppermute | solution.py:323
  17.5 2.0 %copy-start.9 = (f32[64,256]{1,0:T(8,128)}, f32[64,256]{1,0:T(8,128)S(1)}, u32[]{:S(2)}) copy-start(f32[64,256]{1,0:T(8,128)S(1)} %collective-permute-done.2.core_ref) | copy-start | bytes 196612
  17.5 2.0 %copy-start.10 = (f32[64,256]{1,0:T(8,128)}, f32[64,256]{1,0:T(8,128)S(1)}, u32[]{:S(2)}) copy-start(f32[64,256]{1,0:T(8,128)S(1)} %collective-permute-done.3.chip_ref) | copy-start | bytes 196612
  17.5 2.0 %copy-start.7 = (f32[256,128]{1,0:T(8,128)}, f32[256,128]{1,0:T(8,128)S(1)}, u32[]{:S(2)}) copy-start(f32[256,128]{1,0:T(8,128)S(1)} %collective-permute-done.near_ref) | copy-start | bytes 393220
  19.5 0.7 copy-start.8
  20.2 13.8 %copy-start.14 = (f32[240]{0:T(256)S(1)}, f32[240]{0:T(256)}, u32[]{:S(2)}) copy-start(f32[240]{0:T(256)} %param.13) | copy-start | bytes 2884
  20.2 14.6 %copy-start.4 = (bf16[240,512]{1,0:T(8,128)(2,1)S(1)}, bf16[240,512]{1,0:T(8,128)(2,1)}, u32[]{:S(2)}) copy-start(bf16[240,512]{1,0:T(8,128)(2,1)} %param.17) | copy-start | bytes 737284
  28.8 15.0 %collective-permute-start.4 = (f32[256,128]{1,0:T(8,128)}, f32[256,128]{1,0:T(8,128)S(1)}, u32[]{:S(2)}, u32[]{:S(2)}) collective-permute-start(f32[256,128]{1,0:T(8,128)} %get-tuple-element.22), channel_id=1, source_target_pairs={{0,16},{32,48},{64,80},{96,112},{16,0},{48,32},{80,64},{112,96},{1... | collective-permute-start | bytes 393224 | tf_op jit(solution)/shard_map/ppermute | solution.py:323
  28.9 14.9 %collective-permute-start.5 = (f32[256,128]{1,0:T(8,128)}, f32[256,128]{1,0:T(8,128)S(1)}, u32[]{:S(2)}, u32[]{:S(2)}) collective-permute-start(f32[256,128]{1,0:T(8,128)} %get-tuple-element.23), channel_id=1, source_target_pairs={{16,32},{48,64},{80,96},{112,0},{32,16},{64,48},{96,80},{0,112},{1... | collective-permute-start | bytes 393224 | tf_op jit(solution)/shard_map/ppermute | solution.py:323
  35.6 6.5 %collective-permute-start.6 = (f32[64,256]{1,0:T(8,128)}, f32[64,256]{1,0:T(8,128)S(1)}, u32[]{:S(2)}, u32[]{:S(2)}) collective-permute-start(f32[64,256]{1,0:T(8,128)} %get-tuple-element.24), channel_id=1, source_target_pairs={{0,1},{2,3},{4,5},{6,7},{8,9},{10,11},{12,13},{14,15},{1,0},{3,2},... | collective-permute-start | bytes 196616 | tf_op jit(solution)/shard_map/ppermute | solution.py:323
  39.9 3.9 %collective-permute-start.7 = (f32[64,256]{1,0:T(8,128)}, f32[64,256]{1,0:T(8,128)S(1)}, u32[]{:S(2)}, u32[]{:S(2)}) collective-permute-start(f32[64,256]{1,0:T(8,128)} %get-tuple-element.24), channel_id=1, source_target_pairs={{1,2},{3,4},{5,6},{7,8},{9,10},{11,12},{13,14},{15,0},{2,1},{4,3},... | collective-permute-start | bytes 196616 | tf_op jit(solution)/shard_map/ppermute | solution.py:323
  42.1 1.7 %copy-start.11 = (f32[64,256]{1,0:T(8,128)}, f32[64,256]{1,0:T(8,128)S(1)}, u32[]{:S(2)}) copy-start(f32[64,256]{1,0:T(8,128)S(1)} %collective-permute-done.6.core_ref) | copy-start | bytes 196612
  43.8 0.6 copy-start.12
  43.8 0.7 copy-start.5
  43.8 0.7 copy-start.6
  44.6 18.9 %copy-start.2 = (bf16[3,512,512]{2,1,0:T(8,128)(2,1)S(1)}, bf16[3,512,512]{2,1,0:T(8,128)(2,1)}, u32[]{:S(2)}) copy-start(bf16[3,512,512]{2,1,0:T(8,128)(2,1)} %param.16) | copy-start | bytes 4718596
  56.9 17.3 %all-to-all-start = ((f32[128,4,128]{2,1,0:T(4,128)}), f32[128,4,128]{2,1,0:T(4,128)}, u32[]{:S(2)}, u32[]{:S(2)}) async-start(f32[128,4,128]{2,1,0:T(4,128)} %bitcast.32), calls=%async_computation | async-start | bytes 524288 | tf_op jit(solution)/shard_map/all_to_all | solution.py:415
  63.5 18.3 %copy-start.15 = (f32[240]{0:T(256)S(1)}, f32[240]{0:T(256)}, u32[]{:S(2)}) copy-start(f32[240]{0:T(256)} %param.14) | copy-start | bytes 2884
  63.5 18.6 %copy-start.16 = (f32[240]{0:T(256)S(1)}, f32[240]{0:T(256)}, u32[]{:S(2)}) copy-start(f32[240]{0:T(256)} %param.19) | copy-start | bytes 2884
  63.5 18.8 %copy-start.13 = (f32[4,512]{1,0:T(4,128)S(1)}, f32[4,512]{1,0:T(4,128)}, u32[]{:S(2)}) copy-start(f32[4,512]{1,0:T(4,128)} %param.18) | copy-start | bytes 24580
  63.6 28.4 %copy-start = (s32[24,128]{1,0:T(8,128)S(1)}, s32[24,128]{1,0:T(8,128)}, u32[]{:S(2)}) copy-start(s32[24,128]{1,0:T(8,128)} %get-tuple-element.26.batch_ref.refs_1_) | copy-start | bytes 36868
  76.0 15.6 %all-to-all-start.1 = ((f32[128,4,128]{2,1,0:T(4,128)}), f32[128,4,128]{2,1,0:T(4,128)S(1)}, u32[]{:S(2)}, u32[]{:S(2)}) async-start(f32[128,4,128]{2,1,0:T(4,128)} %bitcast.30), calls=%async_computation.1 | async-start | bytes 524288 | tf_op jit(solution)/shard_map/all_to_all | solution.py:426
  92.1 1.9 %copy-start.1 = (f32[24,256,128]{2,1,0:T(8,128)S(1)}, f32[24,256,128]{2,1,0:T(8,128)}, u32[]{:S(2)}) copy-start(f32[24,256,128]{2,1,0:T(8,128)} %get-tuple-element.27.refs_0_) | copy-start | bytes 9437188

commit v2 on v1

v2 whole, which is shorter than its diff:
```python
import functools

import jax
import jax.numpy as jnp
from jax import lax
from jax.experimental import pallas as pl
from jax.experimental.pallas import tpu as pltpu
from jax.sharding import PartitionSpec as P

FIELDS = 4
LEVELS = 60
CHUNKS = 8
ROWS = 24
COLS = 128
FEATS = 256
HALF = ROWS // 2
MIB = 1 << 20
NT = (((1,), (1,)), ((), ()))
NN = (((1,), (0,)), ((), ()))


def params(grid=False, limit=60):
    return pltpu.CompilerParams(
        dimension_semantics=("arbitrary",) if grid else None, vmem_limit_bytes=limit * MIB
    )


def lanes_of(shape):
    return lax.broadcasted_iota(jnp.int32, shape, 1)


def valid_rows(chunk):
    level = chunk * 8 + lax.broadcasted_iota(jnp.int32, (8, COLS), 0)
    return level < LEVELS


def level_copies(hbm_ref, vmem_ref, sem):
    copies = []
    for c in range(CHUNKS):
        rows = ROWS * min(8, LEVELS - 8 * c)
        copies.append(
            pltpu.make_async_copy(
                hbm_ref.at[:, pl.ds(8 * ROWS * c, rows), :],
                vmem_ref.at[c, :, pl.ds(0, rows), :],
                sem.at[c],
            )
        )
    return copies


def wait_for(chunk, *groups):
    for c in range(CHUNKS):

        @pl.when(chunk == c)
        def _(c=c):
            for copies in groups:
                copies[c].wait()


class ColumnPacker:
    def __init__(self):
        self.pair = lanes_of((8, COLS)) // 2
        self.halves = [jnp.zeros((8, COLS), jnp.float32) for _ in range(2)]

    def add(self, i, f, tile):
        m = 4 * (i % HALF) + f
        moved = pltpu.roll(tile, 2 * m + 1, axis=1)
        self.halves[i // HALF] = jnp.where(self.pair == m, moved, self.halves[i // HALF])

    def store(self, ref, row):
        for h in range(2):
            ref[pl.ds(row, 8), COLS * h : COLS * (h + 1)] = self.halves[h]


def pair_of(last, first):
    return jnp.where(
        lanes_of((8, COLS)) % 2 == 0,
        jnp.broadcast_to(last[:, COLS - 1 :], (8, COLS)),
        jnp.broadcast_to(first[:, :1], (8, COLS)),
    )


def swap_flag(parity_ref, axis, rows):
    return jnp.full((rows, COLS), parity_ref[axis], jnp.int32) == 0


def mixed(rate, here, below, above, after, before):
    return (
        here
        + rate[0] * (below - here)
        + rate[1] * (above - here)
        + rate[2] * (after - here)
        + rate[3] * (before - here)
    )


def first_kernel(
    parity_ref,
    x_hbm,
    r_hbm,
    part_hbm,
    near_ref,
    far_ref,
    cols_ref,
    x_ref,
    r_ref,
    part_ref,
    x_sem,
    r_sem,
    out_sem,
):
    x_copies = level_copies(x_hbm, x_ref, x_sem)
    r_copies = level_copies(r_hbm, r_ref, r_sem)
    for c in range(CHUNKS):
        x_copies[c].start()
        r_copies[c].start()
    lane = lanes_of((8, COLS))
    zero = jnp.zeros((8, COLS), jnp.float32)
    even = swap_flag(parity_ref, 0, 8)

    def one_chunk(c, carry):
        valid = valid_rows(c)
        wait_for(c, x_copies, r_copies)

        def cell(i, f):
            return jnp.where(valid, x_ref[c, f, pl.ds(i, 8, stride=ROWS), :], 0.0)

        def rate_of(i, k):
            return jnp.where(valid, r_ref[c, k, pl.ds(i, 8, stride=ROWS), :], 0.0)

        for i in range(ROWS):
            rate = [rate_of(i, k) for k in range(4)]
            for f in range(FIELDS):
                here = cell(i, f)
                part_ref[c, i, 8 * f : 8 * f + 8, :] = mixed(
                    rate,
                    here,
                    cell(i + 1, f) if i < ROWS - 1 else zero,
                    cell(i - 1, f) if i > 0 else zero,
                    jnp.where(lane == COLS - 1, 0.0, pltpu.roll(here, COLS - 1, axis=1)),
                    jnp.where(lane == 0, 0.0, pltpu.roll(here, 1, axis=1)),
                )
        pltpu.make_async_copy(part_ref.at[c], part_hbm.at[c], out_sem.at[c]).start()

        start = pl.multiple_of(EDGE_ROWS * c, 8)
        for f in range(2 * FIELDS + 1):
            if f < FIELDS:
                last, first = cell(ROWS - 1, f), cell(0, f)
            elif f < 2 * FIELDS:
                rows = slice(8 * (f - FIELDS), 8 * (f - FIELDS) + 8)
                last, first = part_ref[c, ROWS - 1, rows, :], part_ref[c, 0, rows, :]
            else:
                last, first = rate_of(ROWS - 1, 0), rate_of(0, 1)
            near_ref[pl.ds(start + 8 * f, 8), :] = jnp.where(even, last, first)
            far_ref[pl.ds(start + 8 * f, 8), :] = jnp.where(even, first, last)

        row = pl.multiple_of(8 * c, 8)
        packer = ColumnPacker()
        for i in range(ROWS):
            for f in range(FIELDS):
                packer.add(i, f, cell(i, f))
        packer.store(cols_ref, row)
        packer = ColumnPacker()
        for i in range(ROWS):
            for f in range(FIELDS):
                packer.add(i, f, part_ref[c, i, 8 * f : 8 * f + 8, :])
        packer.store(cols_ref, 64 + row)
        for h in range(2):
            acc = zero
            for i in range(HALF):
                pair = pair_of(rate_of(HALF * h + i, 2), rate_of(HALF * h + i, 3))
                acc = jnp.where(lane // 8 == i, pair, acc)
            outer = rate_of(0, 1) if h == 0 else rate_of(ROWS - 1, 0)
            acc = jnp.where(lane // 8 == HALF, pair_of(outer, outer), acc)
            cols_ref[pl.ds(128 + row, 8), COLS * h : COLS * (h + 1)] = acc
        return carry

    lax.fori_loop(0, CHUNKS, one_chunk, 0)
    for c in range(CHUNKS):
        pltpu.make_async_copy(part_ref.at[c], part_hbm.at[c], out_sem.at[c]).wait()


def merged_columns(even_y, core, chip):
    right = jnp.where(even_y, core, chip)
    left = jnp.where(even_y, chip, core)
    return jnp.where(
        lanes_of((8, COLS)) % 2 == 0,
        pltpu.roll(right, COLS - 1, axis=1),
        pltpu.roll(left, 1, axis=1),
    )


def corner_kernel(parity_ref, cols_ref, core_ref, chip_ref, near_ref, far_ref):
    even = swap_flag(parity_ref, 0, 8)
    even_y = swap_flag(parity_ref, 1, 8)
    lane = lanes_of((8, COLS))
    for c in range(CHUNKS):
        sent = []
        for h in range(2):
            part = slice(COLS * h, COLS * (h + 1))
            rows = slice(8 * c, 8 * c + 8)
            beside = merged_columns(even_y, core_ref[rows, part], chip_ref[rows, part])
            given = cols_ref[128 + 8 * c : 136 + 8 * c, part] * beside
            back = 8 * (HALF - 1) * h
            sent.append(
                jnp.where(
                    lane < 8,
                    pltpu.roll(beside, (COLS - back) % COLS, axis=1),
                    pltpu.roll(given, (COLS + 8 - back) % COLS, axis=1),
                )
            )
        first, last = sent
        near_ref[8 * c : 8 * c + 8, :] = jnp.where(even, last, first)
        far_ref[8 * c : 8 * c + 8, :] = jnp.where(even, first, last)


def second_kernel(
    share,
    parity_ref,
    part_hbm,
    r_hbm,
    own_near_ref,
    own_far_ref,
    near_ref,
    far_ref,
    cols_ref,
    core_ref,
    chip_ref,
    corner_near_ref,
    corner_far_ref,
    hot_hbm,
    batch_ref,
    moved_hbm,
    stats_ref,
    part_ref,
    r_ref,
    hot_ref,
    moved_ref,
    x_ref,
    hi_ref,
    lo_ref,
    part_sem,
    r_sem,
    out_sem,
    hot_sem,
):
    part_copies = [
        pltpu.make_async_copy(part_hbm.at[c], part_ref.at[c], part_sem.at[c])
        for c in range(CHUNKS)
    ]
    r_copies = level_copies(r_hbm, r_ref, r_sem)
    for c in range(CHUNKS):
        part_copies[c].start()
        r_copies[c].start()
    hot_copy = pltpu.make_async_copy(hot_hbm, hot_ref, hot_sem)
    hot_copy.start()
    lane = lanes_of((8, COLS))
    rim = (lane == 0) | (lane == COLS - 1)
    even = swap_flag(parity_ref, 0, 8)
    even_y = swap_flag(parity_ref, 1, 8)

    def one_chunk(c, carry):
        valid = valid_rows(c)
        row = pl.multiple_of(8 * c, 8)
        start = pl.multiple_of(EDGE_ROWS * c, 8)
        wait_for(c, part_copies, r_copies)

        def edge(near, far, f, below):
            a, b = near[pl.ds(start + 8 * f, 8), :], far[pl.ds(start + 8 * f, 8), :]
            return jnp.where(even, a, b) if below else jnp.where(even, b, a)

        def rate_of(i, k):
            return r_ref[c, k, pl.ds(i, 8, stride=ROWS), :]

        corner = [corner_near_ref[pl.ds(row, 8), :], corner_far_ref[pl.ds(row, 8), :]]
        corner = [jnp.where(even, corner[1], corner[0]), jnp.where(even, corner[0], corner[1])]
        rings, gains = [], []
        for h in range(2):
            lanes = slice(COLS * h, COLS * (h + 1))
            cells, parts, rates = (
                merged_columns(
                    even_y,
                    core_ref[pl.ds(64 * k + row, 8), lanes],
                    chip_ref[pl.ds(64 * k + row, 8), lanes],
                )
                for k in range(3)
            )
            diagonal = corner[h]
            if h == 1:
                diagonal = pltpu.roll(diagonal, 8 * (HALF - 1), axis=1)
            shift = COLS - 8 * HALF if h == 0 else COLS - 8
            spot = lane // 8 == (0 if h == 0 else HALF - 1)
            extra = jnp.where(spot, pltpu.roll(rates, shift, axis=1) * diagonal, 0.0)
            rings.append(parts + rates * cols_ref[pl.ds(row, 8), lanes] + extra)
            gains.append(cols_ref[pl.ds(128 + row, 8), lanes] * cells)

        outer = []
        for side, i in enumerate((0, ROWS - 1)):
            down = side == 1
            rate = edge(near_ref, far_ref, 2 * FIELDS, down)
            tiles = []
            for f in range(FIELDS):
                turned = pltpu.roll(corner[side], COLS - (9 + 2 * f), axis=1)
                tiles.append(
                    edge(near_ref, far_ref, FIELDS + f, down)
                    + rate * edge(own_near_ref, own_far_ref, f, down)
                    + jnp.where(rim, turned, 0.0)
                )
            outer.append(tiles)

        for i in range(ROWS):
            for f in range(FIELDS):
                m = 4 * (i % HALF) + f
                turned = pltpu.roll(gains[i // HALF], COLS - (2 * m + 1), axis=1)
                tile = part_ref[c, i, 8 * f : 8 * f + 8, :] + jnp.where(rim, turned, 0.0)
                if i == 0:
                    tile = tile + rate_of(0, 1) * edge(near_ref, far_ref, f, False)
                if i == ROWS - 1:
                    tile = tile + rate_of(ROWS - 1, 0) * edge(near_ref, far_ref, f, True)
                part_ref[c, i, 8 * f : 8 * f + 8, :] = tile

        for i in range(ROWS):
            rate = [rate_of(i, k) for k in range(4)]
            kept = []
            for f in range(FIELDS):
                rows = slice(8 * f, 8 * f + 8)
                m = 4 * (i % HALF) + f
                here = part_ref[c, i, rows, :]
                above = outer[0][f] if i == 0 else part_ref[c, i - 1, rows, :]
                below = outer[1][f] if i == ROWS - 1 else part_ref[c, i + 1, rows, :]
                turned = pltpu.roll(rings[i // HALF], COLS - (2 * m + 1), axis=1)
                after = jnp.where(lane == COLS - 1, turned, pltpu.roll(here, COLS - 1, axis=1))
                before = jnp.where(lane == 0, turned, pltpu.roll(here, 1, axis=1))
                tile = jnp.where(valid, mixed(rate, here, below, above, after, before), 0.0)
                moved_ref[c, i, rows, :] = tile
                kept.append(tile)
            for f in (0, 2):
                both = jnp.concatenate(kept[f : f + 2], axis=0).astype(jnp.bfloat16)
                x_ref[pl.ds(pl.multiple_of(32 * c + 8 * f, 16), 16), COLS * i : COLS * (i + 1)] = (
                    both
                )
        pltpu.make_async_copy(moved_ref.at[c], moved_hbm.at[c], out_sem.at[c]).start()
        return carry

    lax.fori_loop(0, CHUNKS, one_chunk, 0)
    hot_copy.wait()
    hot = hot_ref[...]
    sums = lax.dot_general(x_ref[...], hot, NT, preferred_element_type=jnp.float32)
    mean = sums * (1.0 / share)
    for i in range(ROWS):
        part = slice(COLS * i, COLS * (i + 1))
        index = jnp.broadcast_to(batch_ref[i : i + 1, :], (FEATS, COLS))
        own = jnp.take_along_axis(mean, index, axis=1)
        away = x_ref[:, part].astype(jnp.float32) - own
        square = away * away
        high = square.astype(jnp.bfloat16)
        hi_ref[:, part] = high
        lo_ref[:, part] = (square - high.astype(jnp.float32)).astype(jnp.bfloat16)
    spread = lax.dot_general(
        hi_ref[...], hot, NT, preferred_element_type=jnp.float32
    ) + lax.dot_general(lo_ref[...], hot, NT, preferred_element_type=jnp.float32)
    store_parts(stats_ref, (mean[:COLS].T, mean[COLS:].T, spread[:COLS].T, spread[COLS:].T))
    for c in range(CHUNKS):
        pltpu.make_async_copy(moved_ref.at[c], moved_hbm.at[c], out_sem.at[c]).wait()


def store_parts(ref, parts):
    for k, part in enumerate(parts):
        ref[pl.ds(k, part.shape[0], stride=4), :] = part


def load_parts(ref):
    return [ref[pl.ds(k, ref.shape[0] // 4, stride=4), :] for k in range(4)]


def batch_kernel(order_ref, owner_ref, batch_ref, hot_ref):
    order = order_ref[...]
    shape = (32, order.shape[1])
    high = lax.broadcasted_iota(jnp.int32, shape, 0) == order // COLS
    left = jnp.where(high, owner_ref[...], 0.0).astype(jnp.bfloat16)
    shape = (COLS, order.shape[1])
    low = lax.broadcasted_iota(jnp.int32, shape, 0) == order % COLS
    right = jnp.where(low, 1.0, 0.0).astype(jnp.bfloat16)
    found = lax.dot_general(left, right, NT, preferred_element_type=jnp.float32)
    batch = found[:ROWS].astype(jnp.int32)
    batch_ref[...] = batch
    groups = lax.broadcasted_iota(jnp.int32, (COLS, COLS), 0)
    for i in range(ROWS):
        hot_ref[:, COLS * i : COLS * (i + 1)] = jnp.where(
            groups == batch[i : i + 1, :], 1.0, 0.0
        ).astype(jnp.bfloat16)


def merge_kernel(share, stats_ref, gain_ref, out_ref):
    count = stats_ref.shape[0] // 4
    parts = load_parts(stats_ref)
    merged = []
    for k in range(2):
        mean = jnp.sum(parts[k], axis=0, keepdims=True) * (1.0 / count)
        away = parts[k] - mean
        total = jnp.sum(parts[k + 2] + share * (away * away), axis=0, keepdims=True)
        gain = gain_ref[:, COLS * k : COLS * (k + 1)]
        merged.append((mean, lax.rsqrt(total * (1.0 / (count * share)) + 1e-05) * gain))
    values = (merged[0][0], merged[1][0], merged[0][1], merged[1][1])
    store_parts(out_ref, [jnp.broadcast_to(v, (count, COLS)) for v in values])


def network_kernel(
    moved_ref,
    batch_ref,
    stats_ref,
    shift_ref,
    first_ref,
    inner_ref,
    last_ref,
    bias_ref,
    final_ref,
    out_block_ref,
    mean_ref,
    scale_ref,
):
    out_ref = out_block_ref.reshape(FIELDS * LEVELS * 8, COLS)

    @pl.when(pl.program_id(0) == 0)
    def _():
        parts = load_parts(stats_ref)
        for k in range(2):
            mean_ref[COLS * k : COLS * (k + 1), :] = parts[k].T
            scale_ref[COLS * k : COLS * (k + 1), :] = parts[k + 2].T

    mean = mean_ref[...]
    scale = scale_ref[...]
    shift = shift_ref[...]

    def dot(a, b):
        return lax.dot_general(a, b, NN, preferred_element_type=jnp.float32)

    def act(product, layer):
        t = product + bias_ref[layer : layer + 1, :]
        return (t + t * jnp.tanh(t)).astype(jnp.bfloat16)

    normed = []
    for i in range(8):
        index = jnp.broadcast_to(batch_ref[i : i + 1, :], (FEATS, COLS))
        x = moved_ref[:, i].reshape(FEATS, COLS).astype(jnp.bfloat16).astype(jnp.float32)
        away = x - jnp.take_along_axis(mean, index, axis=1)
        tile = away * jnp.take_along_axis(scale, index, axis=1) + shift
        normed.append(tile.T.astype(jnp.bfloat16))
    hidden = act(dot(jnp.concatenate(normed, axis=0), first_ref[...]), 0)
    for layer in range(3):
        hidden = act(dot(hidden, inner_ref[layer]), layer + 1)
    tendency = dot(hidden, last_ref[...]) + final_ref[...]
    tendency = tendency.astype(jnp.bfloat16).astype(jnp.float32)
    for i in range(8):
        change = tendency[COLS * i : COLS * (i + 1), :].T
        for chunk in range(CHUNKS):
            rows = min(8, LEVELS - 8 * chunk)
            for f in range(FIELDS):
                row = 32 * chunk + 8 * f
                new = moved_ref[chunk, i, 8 * f : 8 * f + rows, :] + change[row : row + rows]
                out_ref[pl.ds((LEVELS * f + 8 * chunk) * 8 + i, rows, stride=8), :] = new


def whole(shape):
    return pl.BlockSpec(shape, lambda c: (0,) * len(shape))


EDGE_ROWS = 8 * (2 * FIELDS + 1)
SCALAR_SPEC = pl.BlockSpec(memory_space=pltpu.SMEM)
VMEM_SPEC = pl.BlockSpec(memory_space=pltpu.VMEM)
HBM_SPEC = pl.BlockSpec(memory_space=pltpu.HBM)
GRID_SHAPE = (CHUNKS, ROWS, 32, COLS)
LEVEL_SHAPE = (CHUNKS, 4, 8 * ROWS, COLS)


def f32(*shape):
    return jax.ShapeDtypeStruct(shape, jnp.float32)


def cost(flops, size):
    return pl.CostEstimate(flops=flops, bytes_accessed=size, transcendentals=0)


def swap(values, axis, first):
    count = lax.axis_size(axis)
    step = 0 if first else 1
    pairs = [((i + step) % count, (i + 1 + step) % count) for i in range(0, count, 2)]
    return lax.ppermute(values, axis, pairs + [(b, a) for a, b in pairs])


def by_row(values):
    rest = values.shape[1:]
    values = values.reshape(FIELDS, LEVELS, *rest)
    values = jnp.pad(values, ((0, 0), (0, 64 - LEVELS)) + ((0, 0),) * len(rest))
    values = values.reshape(FIELDS, CHUNKS, 8, *rest).swapaxes(0, 1)
    return values.reshape(FEATS, *rest)


def body(
    tracers,
    rates,
    column_order,
    norm_gain,
    norm_shift,
    weight_first,
    weight_hidden,
    weight_last,
    bias_hidden,
    bias_last,
):
    count = lax.axis_size("bx") * lax.axis_size("by")
    columns = ROWS * COLS
    share = columns // count
    width = weight_first.shape[0]
    x = tracers.reshape(FIELDS, LEVELS * ROWS, COLS)
    r = rates.reshape(4, LEVELS * ROWS, COLS)
    parity = jnp.stack([lax.axis_index("bx"), lax.axis_index("by")]).astype(jnp.int32) % 2

    dma = pltpu.SemaphoreType.DMA
    part, near, far, cols = pl.pallas_call(
        first_kernel,
        in_specs=[SCALAR_SPEC, HBM_SPEC, HBM_SPEC],
        out_specs=[HBM_SPEC, VMEM_SPEC, VMEM_SPEC, VMEM_SPEC],
        out_shape=[
            f32(*GRID_SHAPE),
            f32(CHUNKS * EDGE_ROWS, COLS),
            f32(CHUNKS * EDGE_ROWS, COLS),
            f32(3 * 64, 2 * COLS),
        ],
        scratch_shapes=[
            pltpu.VMEM(LEVEL_SHAPE, jnp.float32),
            pltpu.VMEM(LEVEL_SHAPE, jnp.float32),
            pltpu.VMEM(GRID_SHAPE, jnp.float32),
            dma((CHUNKS,)),
            dma((CHUNKS,)),
            dma((CHUNKS,)),
        ],
        compiler_params=params(),
        cost_estimate=cost(10**7, 9 * 10**6),
        name="first_substep",
    )(parity, x, r)
    core = swap(cols, "by", True)
    chip = swap(cols, "by", False)
    near_in = swap(near, "bx", True)
    far_in = swap(far, "bx", False)
    corners = pl.pallas_call(
        corner_kernel,
        in_specs=[SCALAR_SPEC, VMEM_SPEC, VMEM_SPEC, VMEM_SPEC],
        out_specs=[VMEM_SPEC, VMEM_SPEC],
        out_shape=[f32(64, COLS), f32(64, COLS)],
        compiler_params=params(limit=32),
        cost_estimate=cost(10**5, 10**6),
        name="corners",
    )(parity, cols, core, chip)
    corner_near = swap(corners[0], "bx", True)
    corner_far = swap(corners[1], "bx", False)

    owner = (jnp.arange(columns, dtype=jnp.int32) // share).astype(jnp.float32)[None, :]
    batch, hot = pl.pallas_call(
        batch_kernel,
        in_specs=[VMEM_SPEC, VMEM_SPEC],
        out_specs=[VMEM_SPEC, VMEM_SPEC],
        out_shape=[
            jax.ShapeDtypeStruct((ROWS, COLS), jnp.int32),
            jax.ShapeDtypeStruct((COLS, columns), jnp.bfloat16),
        ],
        compiler_params=params(),
        cost_estimate=cost(10**9, 2 * 10**6),
        name="batch_ids",
    )(column_order, owner)

    moved, stats = pl.pallas_call(
        functools.partial(second_kernel, share),
        in_specs=[SCALAR_SPEC, HBM_SPEC, HBM_SPEC] + [VMEM_SPEC] * 9 + [HBM_SPEC, VMEM_SPEC],
        out_specs=[HBM_SPEC, VMEM_SPEC],
        out_shape=[f32(*GRID_SHAPE), f32(4 * count, COLS)],
        scratch_shapes=[
            pltpu.VMEM(GRID_SHAPE, jnp.float32),
            pltpu.VMEM(LEVEL_SHAPE, jnp.float32),
            pltpu.VMEM((COLS, columns), jnp.bfloat16),
            pltpu.VMEM(GRID_SHAPE, jnp.float32),
            pltpu.VMEM((FEATS, columns), jnp.bfloat16),
            pltpu.VMEM((FEATS, columns), jnp.bfloat16),
            pltpu.VMEM((FEATS, columns), jnp.bfloat16),
            dma((CHUNKS,)),
            dma((CHUNKS,)),
            dma((CHUNKS,)),
            dma,
        ],
        compiler_params=params(),
        cost_estimate=cost(10**9, 9 * 10**6),
        name="second_substep",
    )(
        parity,
        part,
        r,
        near,
        far,
        near_in,
        far_in,
        cols,
        core,
        chip,
        corner_near,
        corner_far,
        hot,
        batch,
    )

    gathered = lax.all_to_all(stats, ("bx", "by"), split_axis=0, concat_axis=0, tiled=True)
    merged = pl.pallas_call(
        functools.partial(merge_kernel, float(share)),
        in_specs=[VMEM_SPEC, VMEM_SPEC],
        out_specs=VMEM_SPEC,
        out_shape=jax.ShapeDtypeStruct((4 * count, COLS), jnp.float32),
        compiler_params=params(),
        cost_estimate=cost(10**6, 10**6),
        name="merge_statistics",
    )(gathered, by_row(norm_gain)[None, :])
    known = lax.all_to_all(merged, ("bx", "by"), split_axis=0, concat_axis=0, tiled=True)

    half = jnp.bfloat16(0.5)
    new = pl.pallas_call(
        network_kernel,
        grid=(3,),
        in_specs=[
            pl.BlockSpec((CHUNKS, 8, 32, COLS), lambda c: (0, c, 0, 0)),
            pl.BlockSpec((8, COLS), lambda c: (c, 0)),
            whole((4 * count, COLS)),
            whole((FEATS, COLS)),
            whole((FEATS, width)),
            whole((3, width, width)),
            whole((width, FEATS)),
            whole((4, width)),
            whole((1, FEATS)),
        ],
        out_specs=pl.BlockSpec((FIELDS * LEVELS, 8, COLS), lambda c: (0, c, 0)),
        out_shape=f32(FIELDS * LEVELS, ROWS, COLS),
        scratch_shapes=[pltpu.VMEM((FEATS, COLS), jnp.float32) for _ in range(2)],
        compiler_params=params(True),
        cost_estimate=cost(6 * 10**9, 9 * 10**6),
        name="network",
    )(
        moved,
        batch,
        known,
        jnp.broadcast_to(by_row(norm_shift)[:, None], (FEATS, COLS)),
        by_row(weight_first.T) * half,
        weight_hidden.swapaxes(1, 2) * half,
        by_row(weight_last).T,
        bias_hidden * 0.5,
        by_row(bias_last)[None, :],
    )
    return new.reshape(tracers.shape)


def solution(mesh):
    placed = (
        P(None, None, "bx", "by"),
        P(None, None, "bx", "by"),
        P(("bx", "by"), None),
        P(),
        P(),
        P(),
        P(),
        P(),
        P(),
        P(),
    )
    return jax.shard_map(
        body, mesh=mesh, in_specs=placed, out_specs=P(None, None, "bx", "by"), check_vma=False
    )
```

time: 113 us -> 99.4 us (0.88)
  Pallas kernels: 50.1 us -> 37.6 us
  waiting for transfers between devices: 23.4 us -> 17.3 us
  starting transfers between devices: 29.9 us -> 32.3 us
  other arithmetic: 1.46 us -> 3.25 us
  local copies, waits for them, and re-layouts: 7.18 us -> 8.36 us
    pallas_call x6, Pallas kernels: 50.1 us -> 37.6 us  [the longest x1 12.7 us: body(): pl.pallas_call(network_kernel, grid=(3,), in_specs=[pl.BlockSpec((CHUNKS,...]
    ppermute x8 -> x6, waiting for transfers between devices: 3.69 us -> 0.02 us  [swap(): return lax.ppermute(values, axis, pairs + [(b, a) for a, b in pairs])]
    ppermute x8 -> x6, starting transfers between devices: 18.7 us -> 21.5 us  [swap(): return lax.ppermute(values, axis, pairs + [(b, a) for a, b in pairs])]
    all_to_all x1, waiting for transfers between devices: 9.19 us -> 7.6 us  [body(): lax.all_to_all(merged, ('bx', 'by'), split_axis=0, concat_axis=0, tiled=T...]
    mul x2, other arithmetic: 0.19 us -> 1.36 us  [the longest x1 1.31 us: body(): weight_hidden.swapaxes(1, 2) * half]
    unnamed x34 -> x29, local copies, waits for them, and re-layouts: 3.28 us -> 2.99 us
  transfers between devices with their start and end apart: 10 -> 8, of which waited for: 4 -> 2; matrix products, arithmetic and copies ran while one was open for 4% -> 8% of each run, Pallas kernels for 2% -> 3%
where the time goes in v2:
time: 99.4 us; the launch traced here: 99 us
  Pallas kernels  37.6 us (38%)
  starting transfers between devices  32.3 us (32%)
  waiting for transfers between devices  17.3 us (17%)
  local copies, waits for them, and re-layouts  8.36 us (8%)
  other arithmetic  3.25 us (3%)
    ppermute x6, starting transfers between devices, swap(): return lax.ppermute(values, axis, pairs + [(b, a) for a, b in pairs])  21.5 us
    pallas_call x1, Pallas kernels, body(): pl.pallas_call(network_kernel, grid=(3,), in_specs=[pl.BlockSpec((CHUNKS,...  12.7 us
    pallas_call x1, Pallas kernels, body(): pl.pallas_call(functools.partial(second_kernel, share), in_specs=[SCALAR_...  11.7 us
    all_to_all x1, waiting for transfers between devices, body(): lax.all_to_all(stats, ('bx', 'by'), split_axis=0, concat_axis=0, tiled=True)  9.66 us
    pallas_call x1, Pallas kernels, body(): pl.pallas_call(first_kernel, in_specs=[SCALAR_SPEC, HBM_SPEC, HBM_SPEC],...  8.57 us
    all_to_all x1, waiting for transfers between devices, body(): lax.all_to_all(merged, ('bx', 'by'), split_axis=0, concat_axis=0, tiled=T...  7.6 us
    all_to_all x1, starting transfers between devices, body(): lax.all_to_all(stats, ('bx', 'by'), split_axis=0, concat_axis=0, tiled=True)  6.18 us
    all_to_all x1, starting transfers between devices, body(): lax.all_to_all(merged, ('bx', 'by'), split_axis=0, concat_axis=0, tiled=T...  4.61 us
  transfers between devices with their start and end apart: 8, of which 2 were waited for; matrix products, arithmetic and copies ran while one was open for 8% of the time, Pallas kernels for 3%

profile of v2, /device:TPU:1, one launch (start us, length us, event | category | flops | bytes accessed | tf_op | source)
XLA Modules:
  0.0 99.0 jit_solution(9649493161617705211)
XLA Ops:
  0.0 0.7 and_select_fusion.1.parity_ref
  0.7 8.6 %first_substep.1 = (f32[8,24,32,128]{3,2,1,0:T(8,128)}, f32[576,128]{1,0:T(8,128)}, f32[576,128]{1,0:T(8,128)}, f32[192,256]{1,0:T(8,128)}) custom-call(s32[2]{0:T(128)} %and_select_fusion.1.parity_ref, f32[4,1440,128]{2,1,0:T(8,128)} %bitcast.28, f32[4,1440,128]{2,1,0:T(8,128)} %bitcast.26), custom_call_target="tpu_custom_call" | custom-call | flops 10000000 | bytes 9000000 | tf_op jit(solution)/shard_map/first_substep/pallas_call | solution.py:520
  9.3 1.5 %collective-permute-start.2 = (f32[192,256]{1,0:T(8,128)}, f32[192,256]{1,0:T(8,128)S(1)}, u32[]{:S(2)}, u32[]{:S(2)}) collective-permute-start(f32[192,256]{1,0:T(8,128)} %get-tuple-element.18.cols_ref), channel_id=1, source_target_pairs={{0,1},{2,3},{4,5},{6,7},{8,9},{10,11},{12,13},{14,15},{1,0},{3,2},... | collective-permute-start | bytes 589832 | tf_op jit(solution)/shard_map/ppermute | solution.py:488
  10.8 1.7 %collective-permute-start.3 = (f32[192,256]{1,0:T(8,128)}, f32[192,256]{1,0:T(8,128)S(1)}, u32[]{:S(2)}, u32[]{:S(2)}) collective-permute-start(f32[192,256]{1,0:T(8,128)} %get-tuple-element.18.cols_ref), channel_id=1, source_target_pairs={{1,2},{3,4},{5,6},{7,8},{9,10},{11,12},{13,14},{15,0},{2,1},{4,3},... | collective-permute-start | bytes 589832 | tf_op jit(solution)/shard_map/ppermute | solution.py:488
  12.5 1.3 %collective-permute-start = (f32[576,128]{1,0:T(8,128)}, f32[576,128]{1,0:T(8,128)}, u32[]{:S(2)}, u32[]{:S(2)}) collective-permute-start(f32[576,128]{1,0:T(8,128)} %get-tuple-element.16.own_near_ref), channel_id=1, source_target_pairs={{0,16},{32,48},{64,80},{96,112},{16,0},{48,32},{80,64},{112,96},{1... | collective-permute-start | bytes 884744 | tf_op jit(solution)/shard_map/ppermute | solution.py:488
  13.8 4.9 %collective-permute-start.1 = (f32[576,128]{1,0:T(8,128)}, f32[576,128]{1,0:T(8,128)}, u32[]{:S(2)}, u32[]{:S(2)}) collective-permute-start(f32[576,128]{1,0:T(8,128)} %get-tuple-element.17.own_far_ref), channel_id=1, source_target_pairs={{16,32},{48,64},{80,96},{112,0},{32,16},{64,48},{96,80},{0,112},{1... | collective-permute-start | bytes 884744 | tf_op jit(solution)/shard_map/ppermute | solution.py:488
  18.7 0.6 fusion.owner_ref
  19.4 1.0 copy-done
  20.4 0.7 corners.1
  21.1 0.6 collective-permute-start.4
  21.7 11.5 %collective-permute-start.5 = (f32[64,128]{1,0:T(8,128)S(1)}, f32[64,128]{1,0:T(8,128)S(1)}, u32[]{:S(2)}, u32[]{:S(2)}) collective-permute-start(f32[64,128]{1,0:T(8,128)S(1)} %get-tuple-element.20), channel_id=1, source_target_pairs={{16,32},{48,64},{80,96},{112,0},{32,16},{64,48},{96,80},{0,112},{1... | collective-permute-start | bytes 98312 | tf_op jit(solution)/shard_map/ppermute | solution.py:488
  33.2 2.2 %batch_ids.1 = (s32[24,128]{1,0:T(8,128)}, bf16[128,3072]{1,0:T(8,128)(2,1)}) custom-call(s32[1,3072]{1,0:T(1,128)} %order_ref.1, f32[1,3072]{1,0:T(1,128)} %fusion.owner_ref), custom_call_target="tpu_custom_call" | custom-call | flops 1000000000 | bytes 2000000 | tf_op jit(solution)/shard_map/batch_ids/pallas_call | solution.py:559
  35.4 0.1 reshape.89
  35.6 0.7 broadcast_in_dim_reshape.7.gain_ref
  36.3 0.7 copy.21
  37.0 1.0 %reshape.93 = bf16[4,60,512]{2,1,0:T(8,128)(2,1)S(1)} reshape(bf16[240,512]{1,0:T(8,128)(2,1)} %bitcast.36) | data formatting | bytes 491520 | tf_op jit(solution)/shard_map/reshape | solution.py:493
  38.1 0.5 copy-done.8
  38.6 11.7 %second_substep.1 = (f32[8,24,32,128]{3,2,1,0:T(8,128)}, f32[512,128]{1,0:T(8,128)}) custom-call(s32[2]{0:T(128)} %and_select_fusion.1.parity_ref, f32[8,24,32,128]{3,2,1,0:T(8,128)} %get-tuple-element.15.part_hbm, f32[4,1440,128]{2,1,0:T(8,128)} %bitcast.27, f32[576,128]{1,0:T(8,128)} %get-tuple-element.16.own_near_ref, ...), custom_call_target="tpu_custom_call" | custom-call | flops 1000000000 | bytes 9000000 | tf_op jit(solution)/shard_map/second_substep/pallas_call | solution.py:572
  50.3 6.2 %all-to-all-start = ((f32[128,4,128]{2,1,0:T(4,128)}), f32[128,4,128]{2,1,0:T(4,128)S(1)}, u32[]{:S(2)}, u32[]{:S(2)}) async-start(f32[128,4,128]{2,1,0:T(4,128)} %bitcast.35), calls=%async_computation | async-start | bytes 524288 | tf_op jit(solution)/shard_map/all_to_all | solution.py:610
  56.5 1.3 %multiply_bitcast_fusion.inner_ref = bf16[3,512,512]{2,1,0:T(8,128)(2,1)} fusion(bf16[3,512,512]{1,2,0:T(8,128)(2,1)S(1)} %copy.21), kind=kLoop, calls=%fused_computation | loop fusion | flops 786432 | bytes 3145728 | tf_op jit(solution)/shard_map/mul | solution.py:649
  57.9 9.7 %all-to-all-done = f32[128,4,128]{2,1,0:T(4,128)S(1)} async-done(((f32[128,4,128]{2,1,0:T(4,128)}), f32[128,4,128]{2,1,0:T(4,128)S(1)}, u32[]{:S(2)}, u32[]{:S(2)}) %all-to-all-start) | async-done | bytes 262176 | tf_op jit(solution)/shard_map/all_to_all | solution.py:610
  67.5 0.7 copy-done.5
  68.2 1.8 %merge_statistics.1 = f32[512,128]{1,0:T(8,128)} custom-call(f32[512,128]{1,0:T(8,128)} %bitcast.30, f32[1,256]{1,0:T(1,128)} %broadcast_in_dim_reshape.7.gain_ref), custom_call_target="tpu_custom_call" | custom-call | flops 1000000 | bytes 1000000 | tf_op jit(solution)/shard_map/merge_statistics/pallas_call | solution.py:611
  70.0 4.6 %all-to-all-start.1 = ((f32[128,4,128]{2,1,0:T(4,128)}), f32[128,4,128]{2,1,0:T(4,128)S(1)}, u32[]{:S(2)}, u32[]{:S(2)}) async-start(f32[128,4,128]{2,1,0:T(4,128)} %bitcast.29), calls=%async_computation.1 | async-start | bytes 524288 | tf_op jit(solution)/shard_map/all_to_all | solution.py:620
  74.7 0.8 copy.23
  75.6 0.7 copy.20
  76.5 0.1 broadcast_in_dim.8
  76.7 0.7 broadcast_in_dim_reshape.8.final_ref
  77.4 0.6 broadcast_multiply_fusion.bias_ref
  78.0 7.6 %all-to-all-done.1 = f32[128,4,128]{2,1,0:T(4,128)S(1)} async-done(((f32[128,4,128]{2,1,0:T(4,128)}), f32[128,4,128]{2,1,0:T(4,128)S(1)}, u32[]{:S(2)}, u32[]{:S(2)}) %all-to-all-start.1) | async-done | bytes 262176 | tf_op jit(solution)/shard_map/all_to_all | solution.py:620
  85.6 0.8 broadcast_in_dim.9.shift_ref
  86.4 12.7 %network.1 = f32[240,24,128]{2,1,0:T(8,128)} custom-call(f32[8,24,32,128]{3,2,1,0:T(8,128)} %get-tuple-element.23.moved_ref, s32[24,128]{1,0:T(8,128)} %get-tuple-element.22.batch_ref, f32[512,128]{1,0:T(8,128)} %bitcast.32, f32[256,128]{1,0:T(8,128)} %broadcast_in_dim.9.shift_ref, bf16[256,512]{1,0:T(8,128)(2,1)} %bitcast.34, ...), custom_call_target="tpu_custom_call" | custom-call | flops 6000000000 | bytes 9000000 | tf_op jit(solution)/shard_map/network/pallas_call | solution.py:623
  (46 shorter events, 0.7 us)
Async XLA Ops:
  0.7 18.6 %copy-start.7 = (bf16[240,512]{1,0:T(8,128)(2,1)S(1)}, bf16[240,512]{1,0:T(8,128)(2,1)}, u32[]{:S(2)}) copy-start(bf16[240,512]{1,0:T(8,128)(2,1)} %param.17) | copy-start | bytes 737284
  0.7 18.7 %copy-start.3 = (s32[2]{0:T(128)S(1)}, s32[2]{0:T(128)}, u32[]{:S(2)}) copy-start(s32[2]{0:T(128)} %and_select_fusion.1.parity_ref) | copy-start | bytes 28
  9.3 10.1 %collective-permute-start.2 = (f32[192,256]{1,0:T(8,128)}, f32[192,256]{1,0:T(8,128)S(1)}, u32[]{:S(2)}, u32[]{:S(2)}) collective-permute-start(f32[192,256]{1,0:T(8,128)} %get-tuple-element.18.cols_ref), channel_id=1, source_target_pairs={{0,1},{2,3},{4,5},{6,7},{8,9},{10,11},{12,13},{14,15},{1,0},{3,2},... | collective-permute-start | bytes 589832 | tf_op jit(solution)/shard_map/ppermute | solution.py:488
  10.8 8.6 %collective-permute-start.3 = (f32[192,256]{1,0:T(8,128)}, f32[192,256]{1,0:T(8,128)S(1)}, u32[]{:S(2)}, u32[]{:S(2)}) collective-permute-start(f32[192,256]{1,0:T(8,128)} %get-tuple-element.18.cols_ref), channel_id=1, source_target_pairs={{1,2},{3,4},{5,6},{7,8},{9,10},{11,12},{13,14},{15,0},{2,1},{4,3},... | collective-permute-start | bytes 589832 | tf_op jit(solution)/shard_map/ppermute | solution.py:488
  12.5 25.6 %collective-permute-start = (f32[576,128]{1,0:T(8,128)}, f32[576,128]{1,0:T(8,128)}, u32[]{:S(2)}, u32[]{:S(2)}) collective-permute-start(f32[576,128]{1,0:T(8,128)} %get-tuple-element.16.own_near_ref), channel_id=1, source_target_pairs={{0,16},{32,48},{64,80},{96,112},{16,0},{48,32},{80,64},{112,96},{1... | collective-permute-start | bytes 884744 | tf_op jit(solution)/shard_map/ppermute | solution.py:488
  13.8 24.3 %collective-permute-start.1 = (f32[576,128]{1,0:T(8,128)}, f32[576,128]{1,0:T(8,128)}, u32[]{:S(2)}, u32[]{:S(2)}) collective-permute-start(f32[576,128]{1,0:T(8,128)} %get-tuple-element.17.own_far_ref), channel_id=1, source_target_pairs={{16,32},{48,64},{80,96},{112,0},{32,16},{64,48},{96,80},{0,112},{1... | collective-permute-start | bytes 884744 | tf_op jit(solution)/shard_map/ppermute | solution.py:488
  19.4 16.0 %copy-start.1 = (f32[192,256]{1,0:T(8,128)}, f32[192,256]{1,0:T(8,128)S(1)}, u32[]{:S(2)}) copy-start(f32[192,256]{1,0:T(8,128)S(1)} %collective-permute-done.2.core_ref) | copy-start | bytes 589828
  19.4 1.0 copy-start
  20.4 15.0 %copy-start.2 = (f32[192,256]{1,0:T(8,128)}, f32[192,256]{1,0:T(8,128)S(1)}, u32[]{:S(2)}) copy-start(f32[192,256]{1,0:T(8,128)S(1)} %collective-permute-done.3.chip_ref) | copy-start | bytes 589828
  21.1 16.9 %collective-permute-start.4 = (f32[64,128]{1,0:T(8,128)S(1)}, f32[64,128]{1,0:T(8,128)S(1)}, u32[]{:S(2)}, u32[]{:S(2)}) collective-permute-start(f32[64,128]{1,0:T(8,128)S(1)} %get-tuple-element.19), channel_id=1, source_target_pairs={{0,16},{32,48},{64,80},{96,112},{16,0},{48,32},{80,64},{112,96},{1... | collective-permute-start | bytes 98312 | tf_op jit(solution)/shard_map/ppermute | solution.py:488
  21.7 13.7 %copy-start.11 = (f32[240]{0:T(256)S(1)}, f32[240]{0:T(256)}, u32[]{:S(2)}) copy-start(f32[240]{0:T(256)} %param.13) | copy-start | bytes 2884
  21.7 14.6 %copy-start.4 = (bf16[3,512,512]{2,1,0:T(8,128)(2,1)S(1)}, bf16[3,512,512]{2,1,0:T(8,128)(2,1)}, u32[]{:S(2)}) copy-start(bf16[3,512,512]{2,1,0:T(8,128)(2,1)} %param.16) | copy-start | bytes 4718596
  21.7 16.3 %collective-permute-start.5 = (f32[64,128]{1,0:T(8,128)S(1)}, f32[64,128]{1,0:T(8,128)S(1)}, u32[]{:S(2)}, u32[]{:S(2)}) collective-permute-start(f32[64,128]{1,0:T(8,128)S(1)} %get-tuple-element.20), channel_id=1, source_target_pairs={{16,32},{48,64},{80,96},{112,0},{32,16},{64,48},{96,80},{0,112},{1... | collective-permute-start | bytes 98312 | tf_op jit(solution)/shard_map/ppermute | solution.py:488
  38.0 0.6 copy-start.8
  38.0 0.6 copy-start.9
  50.3 17.2 %all-to-all-start = ((f32[128,4,128]{2,1,0:T(4,128)}), f32[128,4,128]{2,1,0:T(4,128)S(1)}, u32[]{:S(2)}, u32[]{:S(2)}) async-start(f32[128,4,128]{2,1,0:T(4,128)} %bitcast.35), calls=%async_computation | async-start | bytes 524288 | tf_op jit(solution)/shard_map/all_to_all | solution.py:610
  67.5 0.7 copy-start.5
  68.2 8.1 %copy-start.12 = (f32[240]{0:T(256)S(1)}, f32[240]{0:T(256)}, u32[]{:S(2)}) copy-start(f32[240]{0:T(256)} %param.14) | copy-start | bytes 2884
  68.2 8.3 %copy-start.13 = (f32[240]{0:T(256)S(1)}, f32[240]{0:T(256)}, u32[]{:S(2)}) copy-start(f32[240]{0:T(256)} %param.19) | copy-start | bytes 2884
  68.2 9.2 %copy-start.10 = (f32[4,512]{1,0:T(4,128)S(1)}, f32[4,512]{1,0:T(4,128)}, u32[]{:S(2)}) copy-start(f32[4,512]{1,0:T(4,128)} %param.18) | copy-start | bytes 24580
  70.0 15.6 %all-to-all-start.1 = ((f32[128,4,128]{2,1,0:T(4,128)}), f32[128,4,128]{2,1,0:T(4,128)S(1)}, u32[]{:S(2)}, u32[]{:S(2)}) async-start(f32[128,4,128]{2,1,0:T(4,128)} %bitcast.29), calls=%async_computation.1 | async-start | bytes 524288 | tf_op jit(solution)/shard_map/all_to_all | solution.py:620
  85.6 0.8 copy-start.6

commit v3 on v2

--- a/solution.py
+++ b/solution.py
@@ -19,10 +19,8 @@
 NN = (((1,), (0,)), ((), ()))
 
 
-def params(grid=False, limit=60):
-    return pltpu.CompilerParams(
-        dimension_semantics=("arbitrary",) if grid else None, vmem_limit_bytes=limit * MIB
-    )
+def params(limit):
+    return pltpu.CompilerParams(vmem_limit_bytes=limit * MIB)
 
 
 def lanes_of(shape):
@@ -80,8 +78,8 @@
     )
 
 
-def swap_flag(parity_ref, axis, rows):
-    return jnp.full((rows, COLS), parity_ref[axis], jnp.int32) == 0
+def is_even(axis):
+    return jnp.full((8, COLS), lax.axis_index(axis) % 2, jnp.int32) == 0
 
 
 def mixed(rate, here, below, above, after, before):
@@ -95,16 +93,18 @@
 
 
 def first_kernel(
-    parity_ref,
     x_hbm,
     r_hbm,
     part_hbm,
+    near_out_ref,
+    far_out_ref,
+    cols_out_ref,
+    x_ref,
+    r_ref,
+    part_ref,
     near_ref,
     far_ref,
     cols_ref,
-    x_ref,
-    r_ref,
-    part_ref,
     x_sem,
     r_sem,
     out_sem,
@@ -116,7 +116,7 @@
         r_copies[c].start()
     lane = lanes_of((8, COLS))
     zero = jnp.zeros((8, COLS), jnp.float32)
-    even = swap_flag(parity_ref, 0, 8)
+    even = is_even("bx")
 
     def one_chunk(c, carry):
         valid = valid_rows(c)
@@ -176,6 +176,9 @@
         return carry
 
     lax.fori_loop(0, CHUNKS, one_chunk, 0)
+    for out, kept in ((near_out_ref, near_ref), (far_out_ref, far_ref)):
+        out[...] = kept[...].astype(jnp.bfloat16)
+    cols_out_ref[...] = cols_ref[...].astype(jnp.bfloat16)
     for c in range(CHUNKS):
         pltpu.make_async_copy(part_ref.at[c], part_hbm.at[c], out_sem.at[c]).wait()
 
@@ -190,17 +193,21 @@
     )
 
 
-def corner_kernel(parity_ref, cols_ref, core_ref, chip_ref, near_ref, far_ref):
-    even = swap_flag(parity_ref, 0, 8)
-    even_y = swap_flag(parity_ref, 1, 8)
+def corner_kernel(cols_ref, core_ref, chip_ref, near_in, far_in, near_ref, far_ref):
+    even = is_even("bx")
+    even_y = is_even("by")
     lane = lanes_of((8, COLS))
+    cols = cols_ref[...].astype(jnp.float32)
+    core = core_ref[...].astype(jnp.float32)
+    chip = chip_ref[...].astype(jnp.float32)
+    nears, fars = [], []
     for c in range(CHUNKS):
         sent = []
         for h in range(2):
             part = slice(COLS * h, COLS * (h + 1))
             rows = slice(8 * c, 8 * c + 8)
-            beside = merged_columns(even_y, core_ref[rows, part], chip_ref[rows, part])
-            given = cols_ref[128 + 8 * c : 136 + 8 * c, part] * beside
+            beside = merged_columns(even_y, core[rows, part], chip[rows, part])
+            given = cols[128 + 8 * c : 136 + 8 * c, part] * beside
             back = 8 * (HALF - 1) * h
             sent.append(
                 jnp.where(
@@ -210,24 +217,24 @@
                 )
             )
         first, last = sent
-        near_ref[8 * c : 8 * c + 8, :] = jnp.where(even, last, first)
-        far_ref[8 * c : 8 * c + 8, :] = jnp.where(even, first, last)
+        nears.append(jnp.where(even, last, first))
+        fars.append(jnp.where(even, first, last))
+    for out, given, corner in ((near_ref, near_in, nears), (far_ref, far_in, fars)):
+        out[:EDGES, :] = given[...]
+        out[EDGES:, :] = jnp.concatenate(corner, axis=0).astype(jnp.bfloat16)
 
 
 def second_kernel(
     share,
-    parity_ref,
     part_hbm,
     r_hbm,
-    own_near_ref,
-    own_far_ref,
-    near_ref,
-    far_ref,
-    cols_ref,
-    core_ref,
-    chip_ref,
-    corner_near_ref,
-    corner_far_ref,
+    own_near_in,
+    own_far_in,
+    near_in,
+    far_in,
+    cols_in,
+    core_in,
+    chip_in,
     hot_hbm,
     batch_ref,
     moved_hbm,
@@ -239,6 +246,13 @@
     x_ref,
     hi_ref,
     lo_ref,
+    own_near_ref,
+    own_far_ref,
+    near_ref,
+    far_ref,
+    cols_ref,
+    core_ref,
+    chip_ref,
     part_sem,
     r_sem,
     out_sem,
@@ -254,10 +268,20 @@
         r_copies[c].start()
     hot_copy = pltpu.make_async_copy(hot_hbm, hot_ref, hot_sem)
     hot_copy.start()
+    for kept, given in (
+        (own_near_ref, own_near_in),
+        (own_far_ref, own_far_in),
+        (near_ref, near_in),
+        (far_ref, far_in),
+        (cols_ref, cols_in),
+        (core_ref, core_in),
+        (chip_ref, chip_in),
+    ):
+        kept[...] = given[...].astype(jnp.float32)
     lane = lanes_of((8, COLS))
     rim = (lane == 0) | (lane == COLS - 1)
-    even = swap_flag(parity_ref, 0, 8)
-    even_y = swap_flag(parity_ref, 1, 8)
+    even = is_even("bx")
+    even_y = is_even("by")
 
     def one_chunk(c, carry):
         valid = valid_rows(c)
@@ -272,7 +296,7 @@
         def rate_of(i, k):
             return r_ref[c, k, pl.ds(i, 8, stride=ROWS), :]
 
-        corner = [corner_near_ref[pl.ds(row, 8), :], corner_far_ref[pl.ds(row, 8), :]]
+        corner = [near_ref[pl.ds(EDGES + row, 8), :], far_ref[pl.ds(EDGES + row, 8), :]]
         corner = [jnp.where(even, corner[1], corner[0]), jnp.where(even, corner[0], corner[1])]
         rings, gains = [], []
         for h in range(2):
@@ -406,31 +430,56 @@
 
 
 def network_kernel(
+    moved_hbm,
+    batch_ref,
+    stats_hbm,
+    shift_ref,
+    first_hbm,
+    inner_hbm,
+    last_hbm,
+    bias_ref,
+    final_ref,
+    out_hbm,
     moved_ref,
-    batch_ref,
     stats_ref,
-    shift_ref,
     first_ref,
     inner_ref,
     last_ref,
-    bias_ref,
-    final_ref,
-    out_block_ref,
+    out_ref,
     mean_ref,
     scale_ref,
+    even_ref,
+    odd_ref,
+    moved_sem,
+    weight_sem,
+    out_sem,
 ):
-    out_ref = out_block_ref.reshape(FIELDS * LEVELS * 8, COLS)
-
-    @pl.when(pl.program_id(0) == 0)
-    def _():
-        parts = load_parts(stats_ref)
-        for k in range(2):
-            mean_ref[COLS * k : COLS * (k + 1), :] = parts[k].T
-            scale_ref[COLS * k : COLS * (k + 1), :] = parts[k + 2].T
-
-    mean = mean_ref[...]
-    scale = scale_ref[...]
-    shift = shift_ref[...]
+    blocks = ROWS // BLOCK
+    moved_copies = [
+        pltpu.make_async_copy(
+            moved_hbm.at[:, pl.ds(BLOCK * b, BLOCK)],
+            moved_ref.at[:, pl.ds(BLOCK * b, BLOCK)],
+            moved_sem.at[b],
+        )
+        for b in range(blocks)
+    ]
+    stats_copy = pltpu.make_async_copy(stats_hbm, stats_ref, weight_sem.at[0])
+    weight_copies = [
+        pltpu.make_async_copy(given, kept, weight_sem.at[k + 1])
+        for k, (given, kept) in enumerate(
+            ((first_hbm, first_ref), (inner_hbm, inner_ref), (last_hbm, last_ref))
+        )
+    ]
+    stats_copy.start()
+    moved_copies[0].start()
+    for copy in weight_copies + moved_copies[1:]:
+        copy.start()
+    stats_copy.wait()
+    parts = load_parts(stats_ref)
+    for k in range(2):
+        mean_ref[COLS * k : COLS * (k + 1), :] = parts[k].T
+        scale_ref[COLS * k : COLS * (k + 1), :] = parts[k + 2].T
+    out_rows = out_ref.reshape(FIELDS * LEVELS * ROWS, COLS)
 
     def dot(a, b):
         return lax.dot_general(a, b, NN, preferred_element_type=jnp.float32)
@@ -439,34 +488,63 @@
         t = product + bias_ref[layer : layer + 1, :]
         return (t + t * jnp.tanh(t)).astype(jnp.bfloat16)
 
-    normed = []
-    for i in range(8):
-        index = jnp.broadcast_to(batch_ref[i : i + 1, :], (FEATS, COLS))
-        x = moved_ref[:, i].reshape(FEATS, COLS).astype(jnp.bfloat16).astype(jnp.float32)
-        away = x - jnp.take_along_axis(mean, index, axis=1)
-        tile = away * jnp.take_along_axis(scale, index, axis=1) + shift
-        normed.append(tile.T.astype(jnp.bfloat16))
-    hidden = act(dot(jnp.concatenate(normed, axis=0), first_ref[...]), 0)
-    for layer in range(3):
-        hidden = act(dot(hidden, inner_ref[layer]), layer + 1)
-    tendency = dot(hidden, last_ref[...]) + final_ref[...]
-    tendency = tendency.astype(jnp.bfloat16).astype(jnp.float32)
-    for i in range(8):
-        change = tendency[COLS * i : COLS * (i + 1), :].T
-        for chunk in range(CHUNKS):
-            rows = min(8, LEVELS - 8 * chunk)
-            for f in range(FIELDS):
-                row = 32 * chunk + 8 * f
-                new = moved_ref[chunk, i, 8 * f : 8 * f + rows, :] + change[row : row + rows]
-                out_ref[pl.ds((LEVELS * f + 8 * chunk) * 8 + i, rows, stride=8), :] = new
-
-
-def whole(shape):
-    return pl.BlockSpec(shape, lambda c: (0,) * len(shape))
-
-
+    def normalize(block, normed_ref):
+        mean, scale = mean_ref[...], scale_ref[...]
+        for k in range(BLOCK):
+            i = BLOCK * block + k
+            index = jnp.broadcast_to(batch_ref[pl.ds(i, 1), :], (FEATS, COLS))
+            x = moved_ref[:, i].reshape(FEATS, COLS).astype(jnp.bfloat16).astype(jnp.float32)
+            away = x - jnp.take_along_axis(mean, index, axis=1)
+            tile = away * jnp.take_along_axis(scale, index, axis=1)
+            normed_ref[COLS * k : COLS * (k + 1), :] = (tile.T + shift_ref[...]).astype(
+                jnp.bfloat16
+            )
+
+    def layers(block, normed_ref):
+        hidden = act(dot(normed_ref[...], first_ref[...]), 0)
+        for layer in range(3):
+            hidden = act(dot(hidden, inner_ref[layer]), layer + 1)
+        tendency = dot(hidden, last_ref[...]) + final_ref[...]
+        tendency = tendency.astype(jnp.bfloat16).astype(jnp.float32)
+        for k in range(BLOCK):
+            i = BLOCK * block + k
+            change = tendency[COLS * k : COLS * (k + 1), :].T
+            for chunk in range(CHUNKS):
+                rows = min(8, LEVELS - 8 * chunk)
+                for f in range(FIELDS):
+                    row = 32 * chunk + 8 * f
+                    new = moved_ref[chunk, i, 8 * f : 8 * f + rows, :] + change[row : row + rows]
+                    start = (LEVELS * f + 8 * chunk) * ROWS + i
+                    out_rows[pl.ds(start, rows, stride=ROWS), :] = new
+
+    def out_copy(group):
+        part = pl.ds(pl.multiple_of(8 * group, 8), 8)
+        return pltpu.make_async_copy(
+            out_ref.at[:, part, :], out_hbm.at[:, part, :], out_sem.at[group]
+        )
+
+    moved_copies[0].wait()
+    normalize(0, even_ref)
+    for copy in weight_copies + moved_copies[1:]:
+        copy.wait()
+
+    def two_blocks(group, carry):
+        block = 2 * group
+        normalize(block + 1, odd_ref)
+        layers(block, even_ref)
+        normalize(jnp.minimum(block + 2, blocks - 1), even_ref)
+        layers(block + 1, odd_ref)
+        out_copy(group).start()
+        return carry
+
+    lax.fori_loop(0, blocks // 2, two_blocks, 0)
+    for group in range(blocks // 2):
+        out_copy(group).wait()
+
+
+BLOCK = 4
 EDGE_ROWS = 8 * (2 * FIELDS + 1)
-SCALAR_SPEC = pl.BlockSpec(memory_space=pltpu.SMEM)
+EDGES = CHUNKS * EDGE_ROWS
 VMEM_SPEC = pl.BlockSpec(memory_space=pltpu.VMEM)
 HBM_SPEC = pl.BlockSpec(memory_space=pltpu.HBM)
 GRID_SHAPE = (CHUNKS, ROWS, 32, COLS)
@@ -475,6 +553,10 @@
 
 def f32(*shape):
     return jax.ShapeDtypeStruct(shape, jnp.float32)
+
+
+def bf16(*shape):
+    return jax.ShapeDtypeStruct(shape, jnp.bfloat16)
 
 
 def cost(flops, size):
@@ -514,46 +596,46 @@
     width = weight_first.shape[0]
     x = tracers.reshape(FIELDS, LEVELS * ROWS, COLS)
     r = rates.reshape(4, LEVELS * ROWS, COLS)
-    parity = jnp.stack([lax.axis_index("bx"), lax.axis_index("by")]).astype(jnp.int32) % 2
 
     dma = pltpu.SemaphoreType.DMA
     part, near, far, cols = pl.pallas_call(
         first_kernel,
-        in_specs=[SCALAR_SPEC, HBM_SPEC, HBM_SPEC],
+        in_specs=[HBM_SPEC, HBM_SPEC],
         out_specs=[HBM_SPEC, VMEM_SPEC, VMEM_SPEC, VMEM_SPEC],
         out_shape=[
             f32(*GRID_SHAPE),
-            f32(CHUNKS * EDGE_ROWS, COLS),
-            f32(CHUNKS * EDGE_ROWS, COLS),
-            f32(3 * 64, 2 * COLS),
+            bf16(EDGES, COLS),
+            bf16(EDGES, COLS),
+            bf16(3 * 64, 2 * COLS),
         ],
         scratch_shapes=[
             pltpu.VMEM(LEVEL_SHAPE, jnp.float32),
             pltpu.VMEM(LEVEL_SHAPE, jnp.float32),
             pltpu.VMEM(GRID_SHAPE, jnp.float32),
+            pltpu.VMEM((EDGES, COLS), jnp.float32),
+            pltpu.VMEM((EDGES, COLS), jnp.float32),
+            pltpu.VMEM((3 * 64, 2 * COLS), jnp.float32),
             dma((CHUNKS,)),
             dma((CHUNKS,)),
             dma((CHUNKS,)),
         ],
-        compiler_params=params(),
+        compiler_params=params(62),
         cost_estimate=cost(10**7, 9 * 10**6),
         name="first_substep",
-    )(parity, x, r)
+    )(x, r)
     core = swap(cols, "by", True)
     chip = swap(cols, "by", False)
+    near, far = pl.pallas_call(
+        corner_kernel,
+        in_specs=[VMEM_SPEC] * 5,
+        out_specs=[VMEM_SPEC, VMEM_SPEC],
+        out_shape=[bf16(EDGES + 64, COLS), bf16(EDGES + 64, COLS)],
+        compiler_params=params(62),
+        cost_estimate=cost(10**5, 10**6),
+        name="corners",
+    )(cols, core, chip, near, far)
     near_in = swap(near, "bx", True)
     far_in = swap(far, "bx", False)
-    corners = pl.pallas_call(
-        corner_kernel,
-        in_specs=[SCALAR_SPEC, VMEM_SPEC, VMEM_SPEC, VMEM_SPEC],
-        out_specs=[VMEM_SPEC, VMEM_SPEC],
-        out_shape=[f32(64, COLS), f32(64, COLS)],
-        compiler_params=params(limit=32),
-        cost_estimate=cost(10**5, 10**6),
-        name="corners",
-    )(parity, cols, core, chip)
-    corner_near = swap(corners[0], "bx", True)
-    corner_far = swap(corners[1], "bx", False)
 
     owner = (jnp.arange(columns, dtype=jnp.int32) // share).astype(jnp.float32)[None, :]
     batch, hot = pl.pallas_call(
@@ -564,14 +646,14 @@
             jax.ShapeDtypeStruct((ROWS, COLS), jnp.int32),
             jax.ShapeDtypeStruct((COLS, columns), jnp.bfloat16),
         ],
-        compiler_params=params(),
+        compiler_params=params(62),
         cost_estimate=cost(10**9, 2 * 10**6),
         name="batch_ids",
     )(column_order, owner)
 
     moved, stats = pl.pallas_call(
         functools.partial(second_kernel, share),
-        in_specs=[SCALAR_SPEC, HBM_SPEC, HBM_SPEC] + [VMEM_SPEC] * 9 + [HBM_SPEC, VMEM_SPEC],
+        in_specs=[HBM_SPEC, HBM_SPEC] + [VMEM_SPEC] * 7 + [HBM_SPEC, VMEM_SPEC],
         out_specs=[HBM_SPEC, VMEM_SPEC],
         out_shape=[f32(*GRID_SHAPE), f32(4 * count, COLS)],
         scratch_shapes=[
@@ -582,16 +664,17 @@
             pltpu.VMEM((FEATS, columns), jnp.bfloat16),
             pltpu.VMEM((FEATS, columns), jnp.bfloat16),
             pltpu.VMEM((FEATS, columns), jnp.bfloat16),
+            *[pltpu.VMEM((EDGES + 64, COLS), jnp.float32) for _ in range(4)],
+            *[pltpu.VMEM((3 * 64, 2 * COLS), jnp.float32) for _ in range(3)],
             dma((CHUNKS,)),
             dma((CHUNKS,)),
             dma((CHUNKS,)),
             dma,
         ],
-        compiler_params=params(),
+        compiler_params=params(62),
         cost_estimate=cost(10**9, 9 * 10**6),
         name="second_substep",
     )(
-        parity,
         part,
         r,
         near,
@@ -601,19 +684,30 @@
         cols,
         core,
         chip,
-        corner_near,
-        corner_far,
         hot,
         batch,
     )
 
+    stats, *raw = lax.optimization_barrier(
+        (
+            stats,
+            norm_gain,
+            norm_shift,
+            weight_first,
+            weight_hidden,
+            weight_last,
+            bias_hidden,
+            bias_last,
+        )
+    )
+    norm_gain, norm_shift, weight_first, weight_hidden, weight_last, bias_hidden, bias_last = raw
     gathered = lax.all_to_all(stats, ("bx", "by"), split_axis=0, concat_axis=0, tiled=True)
     merged = pl.pallas_call(
         functools.partial(merge_kernel, float(share)),
         in_specs=[VMEM_SPEC, VMEM_SPEC],
         out_specs=VMEM_SPEC,
         out_shape=jax.ShapeDtypeStruct((4 * count, COLS), jnp.float32),
-        compiler_params=params(),
+        compiler_params=params(16),
         cost_estimate=cost(10**6, 10**6),
         name="merge_statistics",
     )(gathered, by_row(norm_gain)[None, :])
@@ -622,29 +716,42 @@
     half = jnp.bfloat16(0.5)
     new = pl.pallas_call(
         network_kernel,
-        grid=(3,),
         in_specs=[
-            pl.BlockSpec((CHUNKS, 8, 32, COLS), lambda c: (0, c, 0, 0)),
-            pl.BlockSpec((8, COLS), lambda c: (c, 0)),
-            whole((4 * count, COLS)),
-            whole((FEATS, COLS)),
-            whole((FEATS, width)),
-            whole((3, width, width)),
-            whole((width, FEATS)),
-            whole((4, width)),
-            whole((1, FEATS)),
+            HBM_SPEC,
+            VMEM_SPEC,
+            HBM_SPEC,
+            VMEM_SPEC,
+            HBM_SPEC,
+            HBM_SPEC,
+            HBM_SPEC,
+            VMEM_SPEC,
+            VMEM_SPEC,
         ],
-        out_specs=pl.BlockSpec((FIELDS * LEVELS, 8, COLS), lambda c: (0, c, 0)),
+        out_specs=HBM_SPEC,
         out_shape=f32(FIELDS * LEVELS, ROWS, COLS),
-        scratch_shapes=[pltpu.VMEM((FEATS, COLS), jnp.float32) for _ in range(2)],
-        compiler_params=params(True),
+        scratch_shapes=[
+            pltpu.VMEM(GRID_SHAPE, jnp.float32),
+            pltpu.VMEM((4 * count, COLS), jnp.float32),
+            pltpu.VMEM((FEATS, width), jnp.bfloat16),
+            pltpu.VMEM((3, width, width), jnp.bfloat16),
+            pltpu.VMEM((width, FEATS), jnp.bfloat16),
+            pltpu.VMEM((FIELDS * LEVELS, ROWS, COLS), jnp.float32),
+            pltpu.VMEM((FEATS, COLS), jnp.float32),
+            pltpu.VMEM((FEATS, COLS), jnp.float32),
+            pltpu.VMEM((BLOCK * COLS, FEATS), jnp.bfloat16),
+            pltpu.VMEM((BLOCK * COLS, FEATS), jnp.bfloat16),
+            dma((ROWS // BLOCK,)),
+            dma((4,)),
+            dma((3,)),
+        ],
+        compiler_params=params(62),
         cost_estimate=cost(6 * 10**9, 9 * 10**6),
         name="network",
     )(
         moved,
         batch,
         known,
-        jnp.broadcast_to(by_row(norm_shift)[:, None], (FEATS, COLS)),
+        by_row(norm_shift)[None, :],
         by_row(weight_first.T) * half,
         weight_hidden.swapaxes(1, 2) * half,
         by_row(weight_last).T,

time: 99.4 us -> 90.2 us (0.907)
  starting transfers between devices: 32.3 us -> 27.4 us
  waiting for transfers between devices: 17.3 us -> 15.6 us
  local copies, waits for them, and re-layouts: 8.36 us -> 7.11 us
  Pallas kernels: 37.6 us -> 36.4 us
    ppermute x6 -> x4, starting transfers between devices: 21.5 us -> 11.4 us  [swap(): return lax.ppermute(values, axis, pairs + [(b, a) for a, b in pairs])]
    all_to_all x1, starting transfers between devices: 6.18 us -> 11.4 us  [body(): lax.all_to_all(stats, ('bx', 'by'), split_axis=0, concat_axis=0, tiled=True)]
    all_to_all x1, waiting for transfers between devices: 9.66 us -> 7.17 us  [body(): lax.all_to_all(stats, ('bx', 'by'), split_axis=0, concat_axis=0, tiled=True)]
    ppermute x6 -> x4, waiting for transfers between devices: 0.02 us -> 1.4 us  [swap(): return lax.ppermute(values, axis, pairs + [(b, a) for a, b in pairs])]
    pallas_call x1, Pallas kernels: 1.78 us -> 0.78 us  [body(): pl.pallas_call(functools.partial(merge_kernel, float(share)), in_specs=[V...]
    unnamed x29 -> x28, local copies, waits for them, and re-layouts: 2.99 us -> 2.01 us
  transfers between devices with their start and end apart: 8 -> 6, of which waited for: 2 -> 5; matrix products, arithmetic and copies ran while one was open for 8% -> 9% of each run, Pallas kernels for 3% -> 2%
where the time goes in v3:
time: 90.2 us; the launch traced here: 89.9 us
  Pallas kernels  36.4 us (40%)
  starting transfers between devices  27.4 us (30%)
  waiting for transfers between devices  15.6 us (17%)
  local copies, waits for them, and re-layouts  7.11 us (8%)
  other arithmetic  3.27 us (4%)
    pallas_call x1, Pallas kernels, body(): pl.pallas_call(network_kernel, in_specs=[HBM_SPEC, VMEM_SPEC, HBM_SPEC, V...  12.1 us
    pallas_call x1, Pallas kernels, body(): pl.pallas_call(functools.partial(second_kernel, share), in_specs=[HBM_SPE...  11.7 us
    all_to_all x1, starting transfers between devices, body(): lax.all_to_all(stats, ('bx', 'by'), split_axis=0, concat_axis=0, tiled=True)  11.4 us
    ppermute x4, starting transfers between devices, swap(): return lax.ppermute(values, axis, pairs + [(b, a) for a, b in pairs])  11.4 us
    pallas_call x1, Pallas kernels, body(): pl.pallas_call(first_kernel, in_specs=[HBM_SPEC, HBM_SPEC], out_specs=[HB...  7.62 us
    all_to_all x1, waiting for transfers between devices, body(): lax.all_to_all(stats, ('bx', 'by'), split_axis=0, concat_axis=0, tiled=True)  7.17 us
    all_to_all x1, waiting for transfers between devices, body(): lax.all_to_all(merged, ('bx', 'by'), split_axis=0, concat_axis=0, tiled=T...  7.01 us
    all_to_all x1, starting transfers between devices, body(): lax.all_to_all(merged, ('bx', 'by'), split_axis=0, concat_axis=0, tiled=T...  4.61 us
  transfers between devices with their start and end apart: 6, of which 5 were waited for; matrix products, arithmetic and copies ran while one was open for 9% of the time, Pallas kernels for 2%

profile of v3, /device:TPU:1, one launch (start us, length us, event | category | flops | bytes accessed | tf_op | source)
XLA Modules:
  0.0 89.9 jit_solution(9393693493102719884)
XLA Ops:
  0.0 7.6 %first_substep.1 = (f32[8,24,32,128]{3,2,1,0:T(8,128)}, bf16[576,128]{1,0:T(8,128)(2,1)}, bf16[576,128]{1,0:T(8,128)(2,1)}, bf16[192,256]{1,0:T(8,128)(2,1)}) custom-call(f32[4,1440,128]{2,1,0:T(8,128)} %bitcast.27, f32[4,1440,128]{2,1,0:T(8,128)} %bitcast.25), custom_call_target="tpu_custom_call" | custom-call | flops 10000000 | bytes 9000000 | tf_op jit(solution)/shard_map/first_substep/pallas_call | solution.py:601
  7.6 3.1 %collective-permute-start.1 = (bf16[192,256]{1,0:T(8,128)(2,1)}, bf16[192,256]{1,0:T(8,128)(2,1)S(1)}, u32[]{:S(2)}, u32[]{:S(2)}) collective-permute-start(bf16[192,256]{1,0:T(8,128)(2,1)} %get-tuple-element.24.cols_ref.cols_in), channel_id=1, source_target_pairs={{1,2},{3,4},{5,6},{7,8},{9,10},{11,12},{13,14},{15,0},{2,1},{4,3},... | collective-permute-start | bytes 294920 | tf_op jit(solution)/shard_map/ppermute | solution.py:570
  10.7 2.0 %collective-permute-start = (bf16[192,256]{1,0:T(8,128)(2,1)}, bf16[192,256]{1,0:T(8,128)(2,1)S(1)}, u32[]{:S(2)}, u32[]{:S(2)}) collective-permute-start(bf16[192,256]{1,0:T(8,128)(2,1)} %get-tuple-element.24.cols_ref.cols_in), channel_id=1, source_target_pairs={{0,1},{2,3},{4,5},{6,7},{8,9},{10,11},{12,13},{14,15},{1,0},{3,2},... | collective-permute-start | bytes 294920 | tf_op jit(solution)/shard_map/ppermute | solution.py:570
  12.8 0.5 collective-permute-done.1.chip_ref.chip_in
  13.3 0.7 collective-permute-done.core_ref.core_in
  13.9 0.6 copy-done.4
  14.6 2.0 %corners.1 = (bf16[640,128]{1,0:T(8,128)(2,1)}, bf16[640,128]{1,0:T(8,128)(2,1)}) custom-call(bf16[192,256]{1,0:T(8,128)(2,1)} %get-tuple-element.24.cols_ref.cols_in, bf16[192,256]{1,0:T(8,128)(2,1)} %copy-done.4, bf16[192,256]{1,0:T(8,128)(2,1)} %copy-done.3, bf16[576,128]{1,0:T(8,128)(2,1)} %get-tuple-element.25.near_in, ...), custom_call_target="tpu_custom_call" | custom-call | flops 100000 | bytes 1000000 | tf_op jit(solution)/shard_map/corners/pallas_call | solution.py:628
  16.6 1.3 %collective-permute-start.2 = (bf16[640,128]{1,0:T(8,128)(2,1)}, bf16[640,128]{1,0:T(8,128)(2,1)S(1)}, u32[]{:S(2)}, u32[]{:S(2)}) collective-permute-start(bf16[640,128]{1,0:T(8,128)(2,1)} %get-tuple-element.27.own_near_in), channel_id=1, source_target_pairs={{0,16},{32,48},{64,80},{96,112},{16,0},{48,32},{80,64},{112,96},{1... | collective-permute-start | bytes 491528 | tf_op jit(solution)/shard_map/ppermute | solution.py:570
  17.9 4.9 %collective-permute-start.3 = (bf16[640,128]{1,0:T(8,128)(2,1)}, bf16[640,128]{1,0:T(8,128)(2,1)S(1)}, u32[]{:S(2)}, u32[]{:S(2)}) collective-permute-start(bf16[640,128]{1,0:T(8,128)(2,1)} %get-tuple-element.28.own_far_in), channel_id=1, source_target_pairs={{16,32},{48,64},{80,96},{112,0},{32,16},{64,48},{96,80},{0,112},{1... | collective-permute-start | bytes 491528 | tf_op jit(solution)/shard_map/ppermute | solution.py:570
  22.8 0.6 fusion.owner_ref
  23.4 2.2 %batch_ids.1 = (s32[24,128]{1,0:T(8,128)}, bf16[128,3072]{1,0:T(8,128)(2,1)}) custom-call(s32[1,3072]{1,0:T(1,128)} %order_ref.1, f32[1,3072]{1,0:T(1,128)} %fusion.owner_ref), custom_call_target="tpu_custom_call" | custom-call | flops 1000000000 | bytes 2000000 | tf_op jit(solution)/shard_map/batch_ids/pallas_call | solution.py:641
  25.6 0.2 collective-permute-done.3.far_in
  25.9 0.4 copy-done.8
  26.3 0.2 copy-done.9
  26.5 11.7 %second_substep.1 = (f32[8,24,32,128]{3,2,1,0:T(8,128)}, f32[512,128]{1,0:T(8,128)}) custom-call(f32[8,24,32,128]{3,2,1,0:T(8,128)} %get-tuple-element.23.part_hbm, f32[4,1440,128]{2,1,0:T(8,128)} %bitcast.26, bf16[640,128]{1,0:T(8,128)(2,1)} %get-tuple-element.27.own_near_in, bf16[640,128]{1,0:T(8,128)(2,1)} %get-tuple-element.28.own_far_in, ...), custom_call_target="tpu_custom_call" | custom-call | flops 1000000000 | bytes 9000000 | tf_op jit(solution)/shard_map/second_substep/pallas_call | solution.py:654
  38.3 11.4 %all-to-all-start = ((f32[128,4,128]{2,1,0:T(4,128)}), f32[128,4,128]{2,1,0:T(4,128)S(1)}, u32[]{:S(2)}, u32[]{:S(2)}) async-start(f32[128,4,128]{2,1,0:T(4,128)} %bitcast.30), calls=%async_computation | async-start | bytes 524288 | tf_op jit(solution)/shard_map/all_to_all | solution.py:704
  49.9 0.1 broadcast_in_dim_reshape.9.gain_ref
  50.0 0.7 multiply_bitcast_fusion.1
  50.8 0.8 reshape.93
  51.6 0.7 copy.15
  52.3 1.3 %multiply_bitcast_fusion.inner_hbm = bf16[3,512,512]{2,1,0:T(8,128)(2,1)} fusion(bf16[3,512,512]{1,2,0:T(8,128)(2,1)S(1)} %copy.15), kind=kLoop, calls=%fused_computation | loop fusion | flops 786432 | bytes 3145728 | tf_op jit(solution)/shard_map/mul | solution.py:756
  53.6 7.2 %all-to-all-done = f32[128,4,128]{2,1,0:T(4,128)S(1)} async-done(((f32[128,4,128]{2,1,0:T(4,128)}), f32[128,4,128]{2,1,0:T(4,128)S(1)}, u32[]{:S(2)}, u32[]{:S(2)}) %all-to-all-start) | async-done | bytes 262176 | tf_op jit(solution)/shard_map/all_to_all | solution.py:704
  60.7 0.8 merge_statistics.1
  61.5 4.6 %all-to-all-start.1 = ((f32[128,4,128]{2,1,0:T(4,128)}), f32[128,4,128]{2,1,0:T(4,128)S(1)}, u32[]{:S(2)}, u32[]{:S(2)}) async-start(f32[128,4,128]{2,1,0:T(4,128)} %bitcast.5), calls=%async_computation.1 | async-start | bytes 524288 | tf_op jit(solution)/shard_map/all_to_all | solution.py:714
  66.5 0.7 broadcast_in_dim_reshape.11.final_ref
  67.2 0.6 broadcast_in_dim_reshape.10.shift_ref
  67.9 0.7 copy.14
  68.7 0.8 copy.17
  69.5 0.6 broadcast_multiply_fusion.bias_ref
  70.1 7.0 %all-to-all-done.1 = f32[128,4,128]{2,1,0:T(4,128)S(1)} async-done(((f32[128,4,128]{2,1,0:T(4,128)}), f32[128,4,128]{2,1,0:T(4,128)S(1)}, u32[]{:S(2)}, u32[]{:S(2)}) %all-to-all-start.1) | async-done | bytes 262176 | tf_op jit(solution)/shard_map/all_to_all | solution.py:714
  77.1 0.7 copy-done.5
  77.8 12.1 %network.1 = f32[240,24,128]{2,1,0:T(8,128)} custom-call(f32[8,24,32,128]{3,2,1,0:T(8,128)} %get-tuple-element.31.moved_hbm, s32[24,128]{1,0:T(8,128)} %get-tuple-element.30.batch_ref, f32[512,128]{1,0:T(8,128)} %bitcast.29, f32[1,256]{1,0:T(1,128)} %broadcast_in_dim_reshape.10.shift_ref, bf16[256,512]{1,0:T(8,128)(2,1)} %bitcast.31, ...), custom_call_target="tpu_custom_call" | custom-call | flops 6000000000 | bytes 9000000 | tf_op jit(solution)/shard_map/network/pallas_call | solution.py:717
  (40 shorter events, 0.7 us)
Async XLA Ops:
  7.6 5.6 %collective-permute-start.1 = (bf16[192,256]{1,0:T(8,128)(2,1)}, bf16[192,256]{1,0:T(8,128)(2,1)S(1)}, u32[]{:S(2)}, u32[]{:S(2)}) collective-permute-start(bf16[192,256]{1,0:T(8,128)(2,1)} %get-tuple-element.24.cols_ref.cols_in), channel_id=1, source_target_pairs={{1,2},{3,4},{5,6},{7,8},{9,10},{11,12},{13,14},{15,0},{2,1},{4,3},... | collective-permute-start | bytes 294920 | tf_op jit(solution)/shard_map/ppermute | solution.py:570
  10.7 3.2 %collective-permute-start = (bf16[192,256]{1,0:T(8,128)(2,1)}, bf16[192,256]{1,0:T(8,128)(2,1)S(1)}, u32[]{:S(2)}, u32[]{:S(2)}) collective-permute-start(bf16[192,256]{1,0:T(8,128)(2,1)} %get-tuple-element.24.cols_ref.cols_in), channel_id=1, source_target_pairs={{0,1},{2,3},{4,5},{6,7},{8,9},{10,11},{12,13},{14,15},{1,0},{3,2},... | collective-permute-start | bytes 294920 | tf_op jit(solution)/shard_map/ppermute | solution.py:570
  13.3 0.7 copy-start.3
  13.9 0.6 copy-start.4
  16.6 9.0 %collective-permute-start.2 = (bf16[640,128]{1,0:T(8,128)(2,1)}, bf16[640,128]{1,0:T(8,128)(2,1)S(1)}, u32[]{:S(2)}, u32[]{:S(2)}) collective-permute-start(bf16[640,128]{1,0:T(8,128)(2,1)} %get-tuple-element.27.own_near_in), channel_id=1, source_target_pairs={{0,16},{32,48},{64,80},{96,112},{16,0},{48,32},{80,64},{112,96},{1... | collective-permute-start | bytes 491528 | tf_op jit(solution)/shard_map/ppermute | solution.py:570
  17.9 8.0 %collective-permute-start.3 = (bf16[640,128]{1,0:T(8,128)(2,1)}, bf16[640,128]{1,0:T(8,128)(2,1)S(1)}, u32[]{:S(2)}, u32[]{:S(2)}) collective-permute-start(bf16[640,128]{1,0:T(8,128)(2,1)} %get-tuple-element.28.own_far_in), channel_id=1, source_target_pairs={{16,32},{48,64},{80,96},{112,0},{32,16},{64,48},{96,80},{0,112},{1... | collective-permute-start | bytes 491528 | tf_op jit(solution)/shard_map/ppermute | solution.py:570
  25.6 0.7 copy-start.8
  25.9 0.7 copy-start.9
  26.5 11.7 %copy-start.11 = (f32[240]{0:T(256)S(1)}, f32[240]{0:T(256)}, u32[]{:S(2)}) copy-start(f32[240]{0:T(256)} %param.13) | copy-start | bytes 2884
  26.5 23.4 %copy-start.6 = (bf16[512,240]{0,1:T(8,128)(2,1)S(1)}, bf16[512,240]{0,1:T(8,128)(2,1)}, u32[]{:S(2)}) copy-start(bf16[512,240]{0,1:T(8,128)(2,1)} %param.15) | copy-start | bytes 737284
  26.5 24.3 %copy-start.7 = (bf16[240,512]{1,0:T(8,128)(2,1)S(1)}, bf16[240,512]{1,0:T(8,128)(2,1)}, u32[]{:S(2)}) copy-start(bf16[240,512]{1,0:T(8,128)(2,1)} %param.17) | copy-start | bytes 737284
  38.2 13.3 %copy-start = (bf16[3,512,512]{2,1,0:T(8,128)(2,1)S(1)}, bf16[3,512,512]{2,1,0:T(8,128)(2,1)}, u32[]{:S(2)}) copy-start(bf16[3,512,512]{2,1,0:T(8,128)(2,1)} %param.16) | copy-start | bytes 4718596
  38.3 22.4 %all-to-all-start = ((f32[128,4,128]{2,1,0:T(4,128)}), f32[128,4,128]{2,1,0:T(4,128)S(1)}, u32[]{:S(2)}, u32[]{:S(2)}) async-start(f32[128,4,128]{2,1,0:T(4,128)} %bitcast.30), calls=%async_computation | async-start | bytes 524288 | tf_op jit(solution)/shard_map/all_to_all | solution.py:704
  52.3 13.9 %copy-start.2 = (bf16[4,60,512]{2,1,0:T(8,128)(2,1)S(1)}, bf16[4,60,512]{2,1,0:T(8,128)(2,1)}, u32[]{:S(2)}) copy-start(bf16[4,60,512]{2,1,0:T(8,128)(2,1)} %reshape.93) | copy-start | bytes 737284
  53.6 12.6 %copy-start.12 = (f32[240]{0:T(256)S(1)}, f32[240]{0:T(256)}, u32[]{:S(2)}) copy-start(f32[240]{0:T(256)} %param.14) | copy-start | bytes 2884
  53.6 12.7 %copy-start.13 = (f32[240]{0:T(256)S(1)}, f32[240]{0:T(256)}, u32[]{:S(2)}) copy-start(f32[240]{0:T(256)} %param.19) | copy-start | bytes 2884
  53.6 14.3 %copy-start.1 = (bf16[8,4,8,512]{3,2,0,1:T(8,128)(2,1)S(1)}, bf16[8,4,8,512]{3,2,0,1:T(8,128)(2,1)}, u32[]{:S(2)}) copy-start(bf16[8,4,8,512]{3,2,0,1:T(8,128)(2,1)} %multiply_bitcast_fusion.1) | copy-start | bytes 786436
  60.7 8.8 %copy-start.10 = (f32[4,512]{1,0:T(4,128)S(1)}, f32[4,512]{1,0:T(4,128)}, u32[]{:S(2)}) copy-start(f32[4,512]{1,0:T(4,128)} %param.18) | copy-start | bytes 24580
  61.5 15.6 %all-to-all-start.1 = ((f32[128,4,128]{2,1,0:T(4,128)}), f32[128,4,128]{2,1,0:T(4,128)S(1)}, u32[]{:S(2)}, u32[]{:S(2)}) async-start(f32[128,4,128]{2,1,0:T(4,128)} %bitcast.5), calls=%async_computation.1 | async-start | bytes 524288 | tf_op jit(solution)/shard_map/all_to_all | solution.py:714
  77.1 0.7 copy-start.5

commit v4 on v3

--- a/solution.py
+++ b/solution.py
@@ -46,6 +46,13 @@
     return copies
 
 
+def copies_of(given, kept, sem, first=0):
+    return [
+        pltpu.make_async_copy(a, b, sem.at[first + k])
+        for k, (a, b) in enumerate(zip(given, kept, strict=True))
+    ]
+
+
 def wait_for(chunk, *groups):
     for c in range(CHUNKS):
 
@@ -96,18 +103,22 @@
     x_hbm,
     r_hbm,
     part_hbm,
-    near_out_ref,
-    far_out_ref,
-    cols_out_ref,
+    near_hbm,
+    far_hbm,
+    cols_hbm,
     x_ref,
     r_ref,
     part_ref,
     near_ref,
     far_ref,
     cols_ref,
+    near_out_ref,
+    far_out_ref,
+    cols_out_ref,
     x_sem,
     r_sem,
     out_sem,
+    edge_sem,
 ):
     x_copies = level_copies(x_hbm, x_ref, x_sem)
     r_copies = level_copies(r_hbm, r_ref, r_sem)
@@ -179,8 +190,17 @@
     for out, kept in ((near_out_ref, near_ref), (far_out_ref, far_ref)):
         out[...] = kept[...].astype(jnp.bfloat16)
     cols_out_ref[...] = cols_ref[...].astype(jnp.bfloat16)
+    copies = copies_of(
+        (cols_out_ref, near_out_ref, far_out_ref),
+        (cols_hbm, near_hbm.at[pl.ds(0, EDGES), :], far_hbm.at[pl.ds(0, EDGES), :]),
+        edge_sem,
+    )
+    for copy in copies:
+        copy.start()
     for c in range(CHUNKS):
         pltpu.make_async_copy(part_ref.at[c], part_hbm.at[c], out_sem.at[c]).wait()
+    for copy in copies:
+        copy.wait()
 
 
 def merged_columns(even_y, core, chip):
@@ -193,13 +213,29 @@
     )
 
 
-def corner_kernel(cols_ref, core_ref, chip_ref, near_in, far_in, near_ref, far_ref):
+def corner_kernel(
+    cols_hbm,
+    core_ref,
+    chip_ref,
+    near_in,
+    far_in,
+    near_hbm,
+    far_hbm,
+    rates_ref,
+    near_ref,
+    far_ref,
+    sem,
+):
+    del near_in, far_in
+    copy = pltpu.make_async_copy(cols_hbm.at[pl.ds(128, 64), :], rates_ref, sem.at[2])
+    copy.start()
+    copy.wait()
     even = is_even("bx")
     even_y = is_even("by")
     lane = lanes_of((8, COLS))
-    cols = cols_ref[...].astype(jnp.float32)
-    core = core_ref[...].astype(jnp.float32)
-    chip = chip_ref[...].astype(jnp.float32)
+    rates = rates_ref[...].astype(jnp.float32)
+    core = core_ref[:64, :].astype(jnp.float32)
+    chip = chip_ref[:64, :].astype(jnp.float32)
     nears, fars = [], []
     for c in range(CHUNKS):
         sent = []
@@ -207,7 +243,7 @@
             part = slice(COLS * h, COLS * (h + 1))
             rows = slice(8 * c, 8 * c + 8)
             beside = merged_columns(even_y, core[rows, part], chip[rows, part])
-            given = cols[128 + 8 * c : 136 + 8 * c, part] * beside
+            given = rates[rows, part] * beside
             back = 8 * (HALF - 1) * h
             sent.append(
                 jnp.where(
@@ -219,9 +255,14 @@
         first, last = sent
         nears.append(jnp.where(even, last, first))
         fars.append(jnp.where(even, first, last))
-    for out, given, corner in ((near_ref, near_in, nears), (far_ref, far_in, fars)):
-        out[:EDGES, :] = given[...]
-        out[EDGES:, :] = jnp.concatenate(corner, axis=0).astype(jnp.bfloat16)
+    near_ref[...] = jnp.concatenate(nears, axis=0).astype(jnp.bfloat16)
+    far_ref[...] = jnp.concatenate(fars, axis=0).astype(jnp.bfloat16)
+    arrays = (near_hbm.at[pl.ds(EDGES, 64), :], far_hbm.at[pl.ds(EDGES, 64), :])
+    copies = copies_of((near_ref, far_ref), arrays, sem)
+    for copy in copies:
+        copy.start()
+    for copy in copies:
+        copy.wait()
 
 
 def second_kernel(
@@ -236,9 +277,8 @@
     core_in,
     chip_in,
     hot_hbm,
-    batch_ref,
     moved_hbm,
-    stats_ref,
+    stats_hbm,
     part_ref,
     r_ref,
     hot_ref,
@@ -253,11 +293,26 @@
     cols_ref,
     core_ref,
     chip_ref,
+    own_near_16,
+    own_far_16,
+    near_16,
+    far_16,
+    cols_16,
+    core_16,
+    chip_16,
+    stats_ref,
     part_sem,
     r_sem,
     out_sem,
     hot_sem,
+    edge_sem,
 ):
+    edges_in = (own_near_in, own_far_in, near_in, far_in, cols_in, core_in, chip_in)
+    edges_16 = (own_near_16, own_far_16, near_16, far_16, cols_16, core_16, chip_16)
+    edges = (own_near_ref, own_far_ref, near_ref, far_ref, cols_ref, core_ref, chip_ref)
+    edge_copies = copies_of(edges_in, edges_16, edge_sem)
+    for copy in edge_copies:
+        copy.start()
     part_copies = [
         pltpu.make_async_copy(part_hbm.at[c], part_ref.at[c], part_sem.at[c])
         for c in range(CHUNKS)
@@ -268,15 +323,8 @@
         r_copies[c].start()
     hot_copy = pltpu.make_async_copy(hot_hbm, hot_ref, hot_sem)
     hot_copy.start()
-    for kept, given in (
-        (own_near_ref, own_near_in),
-        (own_far_ref, own_far_in),
-        (near_ref, near_in),
-        (far_ref, far_in),
-        (cols_ref, cols_in),
-        (core_ref, core_in),
-        (chip_ref, chip_in),
-    ):
+    for copy, kept, given in zip(edge_copies, edges, edges_16, strict=True):
+        copy.wait()
         kept[...] = given[...].astype(jnp.float32)
     lane = lanes_of((8, COLS))
     rim = (lane == 0) | (lane == COLS - 1)
@@ -371,11 +419,13 @@
     hot = hot_ref[...]
     sums = lax.dot_general(x_ref[...], hot, NT, preferred_element_type=jnp.float32)
     mean = sums * (1.0 / share)
-    for i in range(ROWS):
-        part = slice(COLS * i, COLS * (i + 1))
-        index = jnp.broadcast_to(batch_ref[i : i + 1, :], (FEATS, COLS))
-        own = jnp.take_along_axis(mean, index, axis=1)
-        away = x_ref[:, part].astype(jnp.float32) - own
+    near_mean = mean.astype(jnp.bfloat16)
+    for i in range(0, ROWS, 4):
+        part = slice(COLS * i, COLS * (i + 4))
+        centre = lax.dot_general(
+            near_mean, hot_ref[:, part], NN, preferred_element_type=jnp.float32
+        )
+        away = x_ref[:, part].astype(jnp.float32) - centre
         square = away * away
         high = square.astype(jnp.bfloat16)
         hi_ref[:, part] = high
@@ -383,9 +433,14 @@
     spread = lax.dot_general(
         hi_ref[...], hot, NT, preferred_element_type=jnp.float32
     ) + lax.dot_general(lo_ref[...], hot, NT, preferred_element_type=jnp.float32)
+    offset = mean - near_mean.astype(jnp.float32)
+    spread = spread - share * (offset * offset)
     store_parts(stats_ref, (mean[:COLS].T, mean[COLS:].T, spread[:COLS].T, spread[COLS:].T))
+    stats_copy = pltpu.make_async_copy(stats_ref, stats_hbm, hot_sem)
+    stats_copy.start()
     for c in range(CHUNKS):
         pltpu.make_async_copy(moved_ref.at[c], moved_hbm.at[c], out_sem.at[c]).wait()
+    stats_copy.wait()
 
 
 def store_parts(ref, parts):
@@ -431,20 +486,24 @@
 
 def network_kernel(
     moved_hbm,
-    batch_ref,
+    batch_hbm,
     stats_hbm,
-    shift_ref,
+    shift_hbm,
     first_hbm,
     inner_hbm,
     last_hbm,
-    bias_ref,
-    final_ref,
+    bias_hbm,
+    final_hbm,
     out_hbm,
     moved_ref,
+    batch_ref,
     stats_ref,
+    shift_ref,
     first_ref,
     inner_ref,
     last_ref,
+    bias_ref,
+    final_ref,
     out_ref,
     mean_ref,
     scale_ref,
@@ -463,18 +522,19 @@
         )
         for b in range(blocks)
     ]
-    stats_copy = pltpu.make_async_copy(stats_hbm, stats_ref, weight_sem.at[0])
-    weight_copies = [
-        pltpu.make_async_copy(given, kept, weight_sem.at[k + 1])
-        for k, (given, kept) in enumerate(
-            ((first_hbm, first_ref), (inner_hbm, inner_ref), (last_hbm, last_ref))
-        )
-    ]
-    stats_copy.start()
-    moved_copies[0].start()
-    for copy in weight_copies + moved_copies[1:]:
+    early_copies = copies_of(
+        (stats_hbm, batch_hbm, shift_hbm), (stats_ref, batch_ref, shift_ref), weight_sem
+    )
+    weight_copies = copies_of(
+        (first_hbm, bias_hbm, inner_hbm, last_hbm, final_hbm),
+        (first_ref, bias_ref, inner_ref, last_ref, final_ref),
+        weight_sem,
+        3,
+    )
+    for copy in early_copies + moved_copies[:2] + weight_copies + moved_copies[2:]:
         copy.start()
-    stats_copy.wait()
+    for copy in early_copies:
+        copy.wait()
     parts = load_parts(stats_ref)
     for k in range(2):
         mean_ref[COLS * k : COLS * (k + 1), :] = parts[k].T
@@ -525,11 +585,17 @@
 
     moved_copies[0].wait()
     normalize(0, even_ref)
-    for copy in weight_copies + moved_copies[1:]:
+    for copy in weight_copies:
         copy.wait()
 
     def two_blocks(group, carry):
         block = 2 * group
+        for b in range(1, blocks):
+
+            @pl.when(block == (b - 1) // 2 * 2)
+            def _(b=b):
+                moved_copies[b].wait()
+
         normalize(block + 1, odd_ref)
         layers(block, even_ref)
         normalize(jnp.minimum(block + 2, blocks - 1), even_ref)
@@ -601,11 +667,11 @@
     part, near, far, cols = pl.pallas_call(
         first_kernel,
         in_specs=[HBM_SPEC, HBM_SPEC],
-        out_specs=[HBM_SPEC, VMEM_SPEC, VMEM_SPEC, VMEM_SPEC],
+        out_specs=[HBM_SPEC] * 4,
         out_shape=[
             f32(*GRID_SHAPE),
-            bf16(EDGES, COLS),
-            bf16(EDGES, COLS),
+            bf16(EDGES + 64, COLS),
+            bf16(EDGES + 64, COLS),
             bf16(3 * 64, 2 * COLS),
         ],
         scratch_shapes=[
@@ -615,9 +681,13 @@
             pltpu.VMEM((EDGES, COLS), jnp.float32),
             pltpu.VMEM((EDGES, COLS), jnp.float32),
             pltpu.VMEM((3 * 64, 2 * COLS), jnp.float32),
+            pltpu.VMEM((EDGES, COLS), jnp.bfloat16),
+            pltpu.VMEM((EDGES, COLS), jnp.bfloat16),
+            pltpu.VMEM((3 * 64, 2 * COLS), jnp.bfloat16),
             dma((CHUNKS,)),
             dma((CHUNKS,)),
             dma((CHUNKS,)),
+            dma((3,)),
         ],
         compiler_params=params(62),
         cost_estimate=cost(10**7, 9 * 10**6),
@@ -627,10 +697,17 @@
     chip = swap(cols, "by", False)
     near, far = pl.pallas_call(
         corner_kernel,
-        in_specs=[VMEM_SPEC] * 5,
-        out_specs=[VMEM_SPEC, VMEM_SPEC],
+        in_specs=[HBM_SPEC, VMEM_SPEC, VMEM_SPEC, HBM_SPEC, HBM_SPEC],
+        out_specs=[HBM_SPEC] * 2,
         out_shape=[bf16(EDGES + 64, COLS), bf16(EDGES + 64, COLS)],
-        compiler_params=params(62),
+        scratch_shapes=[
+            pltpu.VMEM((64, 2 * COLS), jnp.bfloat16),
+            pltpu.VMEM((64, COLS), jnp.bfloat16),
+            pltpu.VMEM((64, COLS), jnp.bfloat16),
+            dma((3,)),
+        ],
+        input_output_aliases={3: 0, 4: 1},
+        compiler_params=params(16),
         cost_estimate=cost(10**5, 10**6),
         name="corners",
     )(cols, core, chip, near, far)
@@ -653,8 +730,8 @@
 
     moved, stats = pl.pallas_call(
         functools.partial(second_kernel, share),
-        in_specs=[HBM_SPEC, HBM_SPEC] + [VMEM_SPEC] * 7 + [HBM_SPEC, VMEM_SPEC],
-        out_specs=[HBM_SPEC, VMEM_SPEC],
+        in_specs=[HBM_SPEC] * 10,
+        out_specs=[HBM_SPEC] * 2,
         out_shape=[f32(*GRID_SHAPE), f32(4 * count, COLS)],
         scratch_shapes=[
             pltpu.VMEM(GRID_SHAPE, jnp.float32),
@@ -666,10 +743,14 @@
             pltpu.VMEM((FEATS, columns), jnp.bfloat16),
             *[pltpu.VMEM((EDGES + 64, COLS), jnp.float32) for _ in range(4)],
             *[pltpu.VMEM((3 * 64, 2 * COLS), jnp.float32) for _ in range(3)],
+            *[pltpu.VMEM((EDGES + 64, COLS), jnp.bfloat16) for _ in range(4)],
+            *[pltpu.VMEM((3 * 64, 2 * COLS), jnp.bfloat16) for _ in range(3)],
+            pltpu.VMEM((4 * count, COLS), jnp.float32),
             dma((CHUNKS,)),
             dma((CHUNKS,)),
             dma((CHUNKS,)),
             dma,
+            dma((7,)),
         ],
         compiler_params=params(62),
         cost_estimate=cost(10**9, 9 * 10**6),
@@ -685,7 +766,6 @@
         core,
         chip,
         hot,
-        batch,
     )
 
     stats, *raw = lax.optimization_barrier(
@@ -716,32 +796,26 @@
     half = jnp.bfloat16(0.5)
     new = pl.pallas_call(
         network_kernel,
-        in_specs=[
-            HBM_SPEC,
-            VMEM_SPEC,
-            HBM_SPEC,
-            VMEM_SPEC,
-            HBM_SPEC,
-            HBM_SPEC,
-            HBM_SPEC,
-            VMEM_SPEC,
-            VMEM_SPEC,
-        ],
+        in_specs=[HBM_SPEC] * 9,
         out_specs=HBM_SPEC,
         out_shape=f32(FIELDS * LEVELS, ROWS, COLS),
         scratch_shapes=[
             pltpu.VMEM(GRID_SHAPE, jnp.float32),
+            pltpu.VMEM((ROWS, COLS), jnp.int32),
             pltpu.VMEM((4 * count, COLS), jnp.float32),
+            pltpu.VMEM((1, FEATS), jnp.float32),
             pltpu.VMEM((FEATS, width), jnp.bfloat16),
             pltpu.VMEM((3, width, width), jnp.bfloat16),
             pltpu.VMEM((width, FEATS), jnp.bfloat16),
+            pltpu.VMEM((4, width), jnp.float32),
+            pltpu.VMEM((1, FEATS), jnp.float32),
             pltpu.VMEM((FIELDS * LEVELS, ROWS, COLS), jnp.float32),
             pltpu.VMEM((FEATS, COLS), jnp.float32),
             pltpu.VMEM((FEATS, COLS), jnp.float32),
             pltpu.VMEM((BLOCK * COLS, FEATS), jnp.bfloat16),
             pltpu.VMEM((BLOCK * COLS, FEATS), jnp.bfloat16),
             dma((ROWS // BLOCK,)),
-            dma((4,)),
+            dma((8,)),
             dma((3,)),
         ],
         compiler_params=params(62),

time: 90.2 us -> 87.5 us (0.970)
  Pallas kernels: 36.4 us -> 33.3 us
  local copies, waits for them, and re-layouts: 7.11 us -> 8.37 us
  waiting for transfers between devices: 15.6 us -> 14.6 us
    pallas_call x2, Pallas kernels: 14.1 us -> 11.9 us  [the longest x1 11.1 us: body(): pl.pallas_call(network_kernel, in_specs=[HBM_SPEC] * 9, out_specs=HBM_SPE...]
    reshape x5, local copies, waits for them, and re-layouts: 1.07 us -> 2.01 us  [by_row(): values = values.reshape(FIELDS, LEVELS, *rest)]
    all_to_all x1, waiting for transfers between devices: 7.17 us -> 6.23 us  [body(): lax.all_to_all(stats, ('bx', 'by'), split_axis=0, concat_axis=0, tiled=True)]
  transfers between devices with their start and end apart: 6 -> 6, of which waited for: 5 -> 5; matrix products, arithmetic and copies ran while one was open for 9% -> 11% of each run, Pallas kernels for 2% -> 3%
where the time goes in v4:
time: 87.5 us; the launch traced here: 87.1 us
  Pallas kernels  33.3 us (38%)
  starting transfers between devices  27.4 us (31%)
  waiting for transfers between devices  14.6 us (17%)
  local copies, waits for them, and re-layouts  8.37 us (10%)
  other arithmetic  3.27 us (4%)
    ppermute x4, starting transfers between devices, swap(): return lax.ppermute(values, axis, pairs + [(b, a) for a, b in pairs])  11.4 us
    all_to_all x1, starting transfers between devices, body(): lax.all_to_all(stats, ('bx', 'by'), split_axis=0, concat_axis=0, tiled=True)  11.4 us
    pallas_call x1, Pallas kernels, body(): pl.pallas_call(functools.partial(second_kernel, share), in_specs=[HBM_SPE...  11.3 us
    pallas_call x1, Pallas kernels, body(): pl.pallas_call(network_kernel, in_specs=[HBM_SPEC] * 9, out_specs=HBM_SPE...  11.1 us
    pallas_call x1, Pallas kernels, body(): pl.pallas_call(first_kernel, in_specs=[HBM_SPEC, HBM_SPEC], out_specs=[HB...  7.08 us
    all_to_all x1, waiting for transfers between devices, body(): lax.all_to_all(merged, ('bx', 'by'), split_axis=0, concat_axis=0, tiled=T...  7.01 us
    all_to_all x1, waiting for transfers between devices, body(): lax.all_to_all(stats, ('bx', 'by'), split_axis=0, concat_axis=0, tiled=True)  6.23 us
    all_to_all x1, starting transfers between devices, body(): lax.all_to_all(merged, ('bx', 'by'), split_axis=0, concat_axis=0, tiled=T...  4.61 us
  transfers between devices with their start and end apart: 6, of which 5 were waited for; matrix products, arithmetic and copies ran while one was open for 11% of the time, Pallas kernels for 3%

profile of v4, /device:TPU:1, one launch (start us, length us, event | category | flops | bytes accessed | tf_op | source)
XLA Modules:
  0.0 87.1 jit_solution(10577279477240426254)
XLA Ops:
  0.0 7.1 %first_substep.1 = (f32[8,24,32,128]{3,2,1,0:T(8,128)}, bf16[640,128]{1,0:T(8,128)(2,1)}, bf16[640,128]{1,0:T(8,128)(2,1)}, bf16[192,256]{1,0:T(8,128)(2,1)}) custom-call(f32[4,1440,128]{2,1,0:T(8,128)} %bitcast.27, f32[4,1440,128]{2,1,0:T(8,128)} %bitcast.25), custom_call_target="tpu_custom_call" | custom-call | flops 10000000 | bytes 9000000 | tf_op jit(solution)/shard_map/first_substep/pallas_call | solution.py:667
  7.1 3.1 %collective-permute-start.1 = (bf16[192,256]{1,0:T(8,128)(2,1)}, bf16[192,256]{1,0:T(8,128)(2,1)S(1)}, u32[]{:S(2)}, u32[]{:S(2)}) collective-permute-start(bf16[192,256]{1,0:T(8,128)(2,1)} %get-tuple-element.24.cols_hbm.cols_in), channel_id=1, source_target_pairs={{1,2},{3,4},{5,6},{7,8},{9,10},{11,12},{13,14},{15,0},{2,1},{4,3},... | collective-permute-start | bytes 294920 | tf_op jit(solution)/shard_map/ppermute | solution.py:636
  10.2 2.0 %collective-permute-start = (bf16[192,256]{1,0:T(8,128)(2,1)}, bf16[192,256]{1,0:T(8,128)(2,1)S(1)}, u32[]{:S(2)}, u32[]{:S(2)}) collective-permute-start(bf16[192,256]{1,0:T(8,128)(2,1)} %get-tuple-element.24.cols_hbm.cols_in), channel_id=1, source_target_pairs={{0,1},{2,3},{4,5},{6,7},{8,9},{10,11},{12,13},{14,15},{1,0},{3,2},... | collective-permute-start | bytes 294920 | tf_op jit(solution)/shard_map/ppermute | solution.py:636
  12.2 0.5 collective-permute-done.1.chip_ref.chip_in
  12.7 0.7 collective-permute-done.core_ref.core_in
  13.4 0.9 %copy-done = bf16[192,256]{1,0:T(8,128)(2,1)S(1)} copy-done((bf16[192,256]{1,0:T(8,128)(2,1)S(1)}, bf16[192,256]{1,0:T(8,128)(2,1)}, u32[]{:S(2)}) %copy-start) | copy-done | bytes 98328
  14.3 0.8 corners.1
  15.1 1.4 %collective-permute-start.2 = (bf16[640,128]{1,0:T(8,128)(2,1)}, bf16[640,128]{1,0:T(8,128)(2,1)S(1)}, u32[]{:S(2)}, u32[]{:S(2)}) collective-permute-start(bf16[640,128]{1,0:T(8,128)(2,1)} %get-tuple-element.27.own_near_in), channel_id=1, source_target_pairs={{0,16},{32,48},{64,80},{96,112},{16,0},{48,32},{80,64},{112,96},{1... | collective-permute-start | bytes 491528 | tf_op jit(solution)/shard_map/ppermute | solution.py:636
  16.5 4.9 %collective-permute-start.3 = (bf16[640,128]{1,0:T(8,128)(2,1)}, bf16[640,128]{1,0:T(8,128)(2,1)S(1)}, u32[]{:S(2)}, u32[]{:S(2)}) collective-permute-start(bf16[640,128]{1,0:T(8,128)(2,1)} %get-tuple-element.28.own_far_in), channel_id=1, source_target_pairs={{16,32},{48,64},{80,96},{112,0},{32,16},{64,48},{96,80},{0,112},{1... | collective-permute-start | bytes 491528 | tf_op jit(solution)/shard_map/ppermute | solution.py:636
  21.4 0.6 fusion.owner_ref
  22.1 2.2 %batch_ids.1 = (s32[24,128]{1,0:T(8,128)}, bf16[128,3072]{1,0:T(8,128)(2,1)}) custom-call(s32[1,3072]{1,0:T(1,128)} %order_ref.1, f32[1,3072]{1,0:T(1,128)} %fusion.owner_ref), custom_call_target="tpu_custom_call" | custom-call | flops 1000000000 | bytes 2000000 | tf_op jit(solution)/shard_map/batch_ids/pallas_call | solution.py:718
  24.3 0.2 collective-permute-done.3.far_in
  24.5 0.4 copy-done.8
  24.9 0.3 copy-done.9
  25.2 11.3 %second_substep.1 = (f32[8,24,32,128]{3,2,1,0:T(8,128)}, f32[512,128]{1,0:T(8,128)}) custom-call(f32[8,24,32,128]{3,2,1,0:T(8,128)} %get-tuple-element.23.part_hbm, f32[4,1440,128]{2,1,0:T(8,128)} %bitcast.26, bf16[640,128]{1,0:T(8,128)(2,1)} %get-tuple-element.27.own_near_in, bf16[640,128]{1,0:T(8,128)(2,1)} %get-tuple-element.28.own_far_in, ...), custom_call_target="tpu_custom_call" | custom-call | flops 1000000000 | bytes 9000000 | tf_op jit(solution)/shard_map/second_substep/pallas_call | solution.py:731
  36.6 11.4 %all-to-all-start = ((f32[128,4,128]{2,1,0:T(4,128)}), f32[128,4,128]{2,1,0:T(4,128)S(1)}, u32[]{:S(2)}, u32[]{:S(2)}) async-start(f32[128,4,128]{2,1,0:T(4,128)} %bitcast.30), calls=%async_computation | async-start | bytes 524288 | tf_op jit(solution)/shard_map/all_to_all | solution.py:784
  48.1 0.1 broadcast_in_dim_reshape.9.gain_ref
  48.3 0.7 multiply_bitcast_fusion.1
  49.0 1.7 %reshape.93 = bf16[4,60,512]{2,1,0:T(8,128)(2,1)} reshape(bf16[240,512]{1,0:T(8,128)(2,1)} %param.17) | data formatting | bytes 491520 | tf_op jit(solution)/shard_map/reshape | solution.py:641
  50.7 0.7 copy.17
  51.4 1.3 %multiply_bitcast_fusion.inner_hbm = bf16[3,512,512]{2,1,0:T(8,128)(2,1)} fusion(bf16[3,512,512]{1,2,0:T(8,128)(2,1)S(1)} %copy.17), kind=kLoop, calls=%fused_computation | loop fusion | flops 786432 | bytes 3145728 | tf_op jit(solution)/shard_map/mul | solution.py:830
  52.7 6.2 %all-to-all-done = f32[128,4,128]{2,1,0:T(4,128)S(1)} async-done(((f32[128,4,128]{2,1,0:T(4,128)}), f32[128,4,128]{2,1,0:T(4,128)S(1)}, u32[]{:S(2)}, u32[]{:S(2)}) %all-to-all-start) | async-done | bytes 262176 | tf_op jit(solution)/shard_map/all_to_all | solution.py:784
  59.0 0.8 merge_statistics.1
  59.8 4.6 %all-to-all-start.1 = ((f32[128,4,128]{2,1,0:T(4,128)}), f32[128,4,128]{2,1,0:T(4,128)S(1)}, u32[]{:S(2)}, u32[]{:S(2)}) async-start(f32[128,4,128]{2,1,0:T(4,128)} %bitcast.5), calls=%async_computation.1 | async-start | bytes 524288 | tf_op jit(solution)/shard_map/all_to_all | solution.py:794
  64.7 0.7 broadcast_in_dim_reshape.11.final_hbm
  65.5 0.6 broadcast_in_dim_reshape.10.shift_hbm
  66.1 0.7 copy.16
  66.9 0.8 copy.19
  67.7 0.6 broadcast_multiply_fusion.bias_hbm
  68.3 7.0 %all-to-all-done.1 = f32[128,4,128]{2,1,0:T(4,128)S(1)} async-done(((f32[128,4,128]{2,1,0:T(4,128)}), f32[128,4,128]{2,1,0:T(4,128)S(1)}, u32[]{:S(2)}, u32[]{:S(2)}) %all-to-all-start.1) | async-done | bytes 262176 | tf_op jit(solution)/shard_map/all_to_all | solution.py:794
  75.3 0.7 copy-done.6
  76.0 11.1 %network.1 = f32[240,24,128]{2,1,0:T(8,128)} custom-call(f32[8,24,32,128]{3,2,1,0:T(8,128)} %get-tuple-element.30.moved_hbm, s32[24,128]{1,0:T(8,128)} %get-tuple-element.31.batch_hbm, f32[512,128]{1,0:T(8,128)} %bitcast.29, f32[1,256]{1,0:T(1,128)} %broadcast_in_dim_reshape.10.shift_hbm, bf16[256,512]{1,0:T(8,128)(2,1)} %bitcast.31, ...), custom_call_target="tpu_custom_call" | custom-call | flops 6000000000 | bytes 9000000 | tf_op jit(solution)/shard_map/network/pallas_call | solution.py:797
  (40 shorter events, 0.7 us)
Async XLA Ops:
  7.1 5.6 %collective-permute-start.1 = (bf16[192,256]{1,0:T(8,128)(2,1)}, bf16[192,256]{1,0:T(8,128)(2,1)S(1)}, u32[]{:S(2)}, u32[]{:S(2)}) collective-permute-start(bf16[192,256]{1,0:T(8,128)(2,1)} %get-tuple-element.24.cols_hbm.cols_in), channel_id=1, source_target_pairs={{1,2},{3,4},{5,6},{7,8},{9,10},{11,12},{13,14},{15,0},{2,1},{4,3},... | collective-permute-start | bytes 294920 | tf_op jit(solution)/shard_map/ppermute | solution.py:636
  10.2 3.2 %collective-permute-start = (bf16[192,256]{1,0:T(8,128)(2,1)}, bf16[192,256]{1,0:T(8,128)(2,1)S(1)}, u32[]{:S(2)}, u32[]{:S(2)}) collective-permute-start(bf16[192,256]{1,0:T(8,128)(2,1)} %get-tuple-element.24.cols_hbm.cols_in), channel_id=1, source_target_pairs={{0,1},{2,3},{4,5},{6,7},{8,9},{10,11},{12,13},{14,15},{1,0},{3,2},... | collective-permute-start | bytes 294920 | tf_op jit(solution)/shard_map/ppermute | solution.py:636
  12.7 11.6 %copy-start.1 = (bf16[192,256]{1,0:T(8,128)(2,1)}, bf16[192,256]{1,0:T(8,128)(2,1)S(1)}, u32[]{:S(2)}) copy-start(bf16[192,256]{1,0:T(8,128)(2,1)S(1)} %collective-permute-done.1.chip_ref.chip_in) | copy-start | bytes 294916
  13.4 10.9 %copy-start.2 = (bf16[192,256]{1,0:T(8,128)(2,1)}, bf16[192,256]{1,0:T(8,128)(2,1)S(1)}, u32[]{:S(2)}) copy-start(bf16[192,256]{1,0:T(8,128)(2,1)S(1)} %collective-permute-done.core_ref.core_in) | copy-start | bytes 294916
  13.4 0.9 %copy-start = (bf16[192,256]{1,0:T(8,128)(2,1)S(1)}, bf16[192,256]{1,0:T(8,128)(2,1)}, u32[]{:S(2)}) copy-start(bf16[192,256]{1,0:T(8,128)(2,1)} %get-tuple-element.24.cols_hbm.cols_in) | copy-start | bytes 294916
  15.1 9.1 %collective-permute-start.2 = (bf16[640,128]{1,0:T(8,128)(2,1)}, bf16[640,128]{1,0:T(8,128)(2,1)S(1)}, u32[]{:S(2)}, u32[]{:S(2)}) collective-permute-start(bf16[640,128]{1,0:T(8,128)(2,1)} %get-tuple-element.27.own_near_in), channel_id=1, source_target_pairs={{0,16},{32,48},{64,80},{96,112},{16,0},{48,32},{80,64},{112,96},{1... | collective-permute-start | bytes 491528 | tf_op jit(solution)/shard_map/ppermute | solution.py:636
  16.5 8.0 %collective-permute-start.3 = (bf16[640,128]{1,0:T(8,128)(2,1)}, bf16[640,128]{1,0:T(8,128)(2,1)S(1)}, u32[]{:S(2)}, u32[]{:S(2)}) collective-permute-start(bf16[640,128]{1,0:T(8,128)(2,1)} %get-tuple-element.28.own_far_in), channel_id=1, source_target_pairs={{16,32},{48,64},{80,96},{112,0},{32,16},{64,48},{96,80},{0,112},{1... | collective-permute-start | bytes 491528 | tf_op jit(solution)/shard_map/ppermute | solution.py:636
  24.3 0.7 copy-start.8
  24.5 0.7 copy-start.9
  25.2 11.3 %copy-start.11 = (f32[240]{0:T(256)S(1)}, f32[240]{0:T(256)}, u32[]{:S(2)}) copy-start(f32[240]{0:T(256)} %param.13) | copy-start | bytes 2884
  25.2 23.0 %copy-start.7 = (bf16[512,240]{0,1:T(8,128)(2,1)S(1)}, bf16[512,240]{0,1:T(8,128)(2,1)}, u32[]{:S(2)}) copy-start(bf16[512,240]{0,1:T(8,128)(2,1)} %param.15) | copy-start | bytes 737284
  36.5 14.2 %copy-start.3 = (bf16[3,512,512]{2,1,0:T(8,128)(2,1)S(1)}, bf16[3,512,512]{2,1,0:T(8,128)(2,1)}, u32[]{:S(2)}) copy-start(bf16[3,512,512]{2,1,0:T(8,128)(2,1)} %param.16) | copy-start | bytes 4718596
  36.6 22.4 %all-to-all-start = ((f32[128,4,128]{2,1,0:T(4,128)}), f32[128,4,128]{2,1,0:T(4,128)S(1)}, u32[]{:S(2)}, u32[]{:S(2)}) async-start(f32[128,4,128]{2,1,0:T(4,128)} %bitcast.30), calls=%async_computation | async-start | bytes 524288 | tf_op jit(solution)/shard_map/all_to_all | solution.py:784
  51.4 12.9 %copy-start.5 = (bf16[4,60,512]{2,1,0:T(8,128)(2,1)S(1)}, bf16[4,60,512]{2,1,0:T(8,128)(2,1)}, u32[]{:S(2)}) copy-start(bf16[4,60,512]{2,1,0:T(8,128)(2,1)} %reshape.93) | copy-start | bytes 737284
  52.7 11.7 %copy-start.12 = (f32[240]{0:T(256)S(1)}, f32[240]{0:T(256)}, u32[]{:S(2)}) copy-start(f32[240]{0:T(256)} %param.14) | copy-start | bytes 2884
  52.7 11.8 %copy-start.13 = (f32[240]{0:T(256)S(1)}, f32[240]{0:T(256)}, u32[]{:S(2)}) copy-start(f32[240]{0:T(256)} %param.19) | copy-start | bytes 2884
  52.7 13.4 %copy-start.4 = (bf16[8,4,8,512]{3,2,0,1:T(8,128)(2,1)S(1)}, bf16[8,4,8,512]{3,2,0,1:T(8,128)(2,1)}, u32[]{:S(2)}) copy-start(bf16[8,4,8,512]{3,2,0,1:T(8,128)(2,1)} %multiply_bitcast_fusion.1) | copy-start | bytes 786436
  59.0 8.8 %copy-start.10 = (f32[4,512]{1,0:T(4,128)S(1)}, f32[4,512]{1,0:T(4,128)}, u32[]{:S(2)}) copy-start(f32[4,512]{1,0:T(4,128)} %param.18) | copy-start | bytes 24580
  59.8 15.6 %all-to-all-start.1 = ((f32[128,4,128]{2,1,0:T(4,128)}), f32[128,4,128]{2,1,0:T(4,128)S(1)}, u32[]{:S(2)}, u32[]{:S(2)}) async-start(f32[128,4,128]{2,1,0:T(4,128)} %bitcast.5), calls=%async_computation.1 | async-start | bytes 524288 | tf_op jit(solution)/shard_map/all_to_all | solution.py:794
  75.3 0.7 copy-start.6

commit v5 on v4

--- a/solution.py
+++ b/solution.py
@@ -72,9 +72,9 @@
         moved = pltpu.roll(tile, 2 * m + 1, axis=1)
         self.halves[i // HALF] = jnp.where(self.pair == m, moved, self.halves[i // HALF])
 
-    def store(self, ref, row):
+    def store(self, ref, row, valid):
         for h in range(2):
-            ref[pl.ds(row, 8), COLS * h : COLS * (h + 1)] = self.halves[h]
+            ref[pl.ds(row, 8), COLS * h : COLS * (h + 1)] = jnp.where(valid, self.halves[h], 0.0)
 
 
 def pair_of(last, first):
@@ -128,22 +128,23 @@
     lane = lanes_of((8, COLS))
     zero = jnp.zeros((8, COLS), jnp.float32)
     even = is_even("bx")
+    odd = jnp.logical_not(even)
 
     def one_chunk(c, carry):
         valid = valid_rows(c)
         wait_for(c, x_copies, r_copies)
 
         def cell(i, f):
-            return jnp.where(valid, x_ref[c, f, pl.ds(i, 8, stride=ROWS), :], 0.0)
+            return x_ref[c, f, pl.ds(i, 8, stride=ROWS), :]
 
         def rate_of(i, k):
-            return jnp.where(valid, r_ref[c, k, pl.ds(i, 8, stride=ROWS), :], 0.0)
+            return r_ref[c, k, pl.ds(i, 8, stride=ROWS), :]
 
         for i in range(ROWS):
             rate = [rate_of(i, k) for k in range(4)]
             for f in range(FIELDS):
                 here = cell(i, f)
-                part_ref[c, i, 8 * f : 8 * f + 8, :] = mixed(
+                new = mixed(
                     rate,
                     here,
                     cell(i + 1, f) if i < ROWS - 1 else zero,
@@ -151,6 +152,7 @@
                     jnp.where(lane == COLS - 1, 0.0, pltpu.roll(here, COLS - 1, axis=1)),
                     jnp.where(lane == 0, 0.0, pltpu.roll(here, 1, axis=1)),
                 )
+                part_ref[c, i, 8 * f : 8 * f + 8, :] = jnp.where(valid, new, 0.0)
         pltpu.make_async_copy(part_ref.at[c], part_hbm.at[c], out_sem.at[c]).start()
 
         start = pl.multiple_of(EDGE_ROWS * c, 8)
@@ -162,20 +164,29 @@
                 last, first = part_ref[c, ROWS - 1, rows, :], part_ref[c, 0, rows, :]
             else:
                 last, first = rate_of(ROWS - 1, 0), rate_of(0, 1)
-            near_ref[pl.ds(start + 8 * f, 8), :] = jnp.where(even, last, first)
-            far_ref[pl.ds(start + 8 * f, 8), :] = jnp.where(even, first, last)
+            near_ref[pl.ds(start + 8 * f, 8), :] = jnp.where(valid & even, last, 0.0) + jnp.where(
+                valid & odd, first, 0.0
+            )
+            far_ref[pl.ds(start + 8 * f, 8), :] = jnp.where(valid & even, first, 0.0) + jnp.where(
+                valid & odd, last, 0.0
+            )
 
         row = pl.multiple_of(8 * c, 8)
+        last = pair_of(rate_of(ROWS - 1, 2), rate_of(ROWS - 1, 3))
+        first = pair_of(rate_of(0, 2), rate_of(0, 3))
+        spot = valid & (lane // 8 == 1)
+        near_ref[pl.ds(EDGES + row, 8), :] = jnp.where(spot, jnp.where(even, last, first), 0.0)
+        far_ref[pl.ds(EDGES + row, 8), :] = jnp.where(spot, jnp.where(even, first, last), 0.0)
         packer = ColumnPacker()
         for i in range(ROWS):
             for f in range(FIELDS):
                 packer.add(i, f, cell(i, f))
-        packer.store(cols_ref, row)
+        packer.store(cols_ref, row, valid)
         packer = ColumnPacker()
         for i in range(ROWS):
             for f in range(FIELDS):
                 packer.add(i, f, part_ref[c, i, 8 * f : 8 * f + 8, :])
-        packer.store(cols_ref, 64 + row)
+        packer.store(cols_ref, 64 + row, valid)
         for h in range(2):
             acc = zero
             for i in range(HALF):
@@ -183,7 +194,7 @@
                 acc = jnp.where(lane // 8 == i, pair, acc)
             outer = rate_of(0, 1) if h == 0 else rate_of(ROWS - 1, 0)
             acc = jnp.where(lane // 8 == HALF, pair_of(outer, outer), acc)
-            cols_ref[pl.ds(128 + row, 8), COLS * h : COLS * (h + 1)] = acc
+            cols_ref[pl.ds(128 + row, 8), COLS * h : COLS * (h + 1)] = jnp.where(valid, acc, 0.0)
         return carry
 
     lax.fori_loop(0, CHUNKS, one_chunk, 0)
@@ -192,7 +203,7 @@
     cols_out_ref[...] = cols_ref[...].astype(jnp.bfloat16)
     copies = copies_of(
         (cols_out_ref, near_out_ref, far_out_ref),
-        (cols_hbm, near_hbm.at[pl.ds(0, EDGES), :], far_hbm.at[pl.ds(0, EDGES), :]),
+        (cols_hbm, near_hbm, far_hbm),
         edge_sem,
     )
     for copy in copies:
@@ -214,51 +225,39 @@
 
 
 def corner_kernel(
-    cols_hbm,
-    core_ref,
-    chip_ref,
-    near_in,
-    far_in,
-    near_hbm,
-    far_hbm,
-    rates_ref,
-    near_ref,
-    far_ref,
-    sem,
+    core_ref, chip_ref, near_in, far_in, near_hbm, far_hbm, near_ref, far_ref, sem
 ):
-    del near_in, far_in
-    copy = pltpu.make_async_copy(cols_hbm.at[pl.ds(128, 64), :], rates_ref, sem.at[2])
-    copy.start()
-    copy.wait()
+    corners_in = [given.at[pl.ds(EDGES, 64), :] for given in (near_in, far_in)]
+    copies = copies_of(corners_in, (near_ref, far_ref), sem)
+    for copy in copies:
+        copy.start()
     even = is_even("bx")
     even_y = is_even("by")
     lane = lanes_of((8, COLS))
-    rates = rates_ref[...].astype(jnp.float32)
     core = core_ref[:64, :].astype(jnp.float32)
     chip = chip_ref[:64, :].astype(jnp.float32)
+    for copy in copies:
+        copy.wait()
+    near_rates = near_ref[...].astype(jnp.float32)
+    far_rates = far_ref[...].astype(jnp.float32)
     nears, fars = [], []
     for c in range(CHUNKS):
-        sent = []
+        rows = slice(8 * c, 8 * c + 8)
+        cells, again = [], []
         for h in range(2):
             part = slice(COLS * h, COLS * (h + 1))
-            rows = slice(8 * c, 8 * c + 8)
             beside = merged_columns(even_y, core[rows, part], chip[rows, part])
-            given = rates[rows, part] * beside
             back = 8 * (HALF - 1) * h
-            sent.append(
-                jnp.where(
-                    lane < 8,
-                    pltpu.roll(beside, (COLS - back) % COLS, axis=1),
-                    pltpu.roll(given, (COLS + 8 - back) % COLS, axis=1),
-                )
-            )
-        first, last = sent
-        nears.append(jnp.where(even, last, first))
-        fars.append(jnp.where(even, first, last))
+            cells.append(pltpu.roll(beside, (COLS - back) % COLS, axis=1))
+            again.append(pltpu.roll(beside, (COLS + 8 - back) % COLS, axis=1))
+        near = jnp.where(even, again[1], again[0]) * near_rates[rows]
+        far = jnp.where(even, again[0], again[1]) * far_rates[rows]
+        nears.append(jnp.where(lane < 8, jnp.where(even, cells[1], cells[0]), near))
+        fars.append(jnp.where(lane < 8, jnp.where(even, cells[0], cells[1]), far))
     near_ref[...] = jnp.concatenate(nears, axis=0).astype(jnp.bfloat16)
     far_ref[...] = jnp.concatenate(fars, axis=0).astype(jnp.bfloat16)
-    arrays = (near_hbm.at[pl.ds(EDGES, 64), :], far_hbm.at[pl.ds(EDGES, 64), :])
-    copies = copies_of((near_ref, far_ref), arrays, sem)
+    corners_out = [out.at[pl.ds(EDGES, 64), :] for out in (near_hbm, far_hbm)]
+    copies = copies_of((near_ref, far_ref), corners_out, sem)
     for copy in copies:
         copy.start()
     for copy in copies:
@@ -277,11 +276,13 @@
     core_in,
     chip_in,
     hot_hbm,
+    hot_t_hbm,
     moved_hbm,
     stats_hbm,
     part_ref,
     r_ref,
     hot_ref,
+    hot_t_ref,
     moved_ref,
     x_ref,
     hi_ref,
@@ -321,8 +322,9 @@
     for c in range(CHUNKS):
         part_copies[c].start()
         r_copies[c].start()
-    hot_copy = pltpu.make_async_copy(hot_hbm, hot_ref, hot_sem)
-    hot_copy.start()
+    hot_copies = copies_of((hot_hbm, hot_t_hbm), (hot_ref, hot_t_ref), hot_sem)
+    for copy in hot_copies:
+        copy.start()
     for copy, kept, given in zip(edge_copies, edges, edges_16, strict=True):
         copy.wait()
         kept[...] = given[...].astype(jnp.float32)
@@ -415,9 +417,10 @@
         return carry
 
     lax.fori_loop(0, CHUNKS, one_chunk, 0)
-    hot_copy.wait()
-    hot = hot_ref[...]
-    sums = lax.dot_general(x_ref[...], hot, NT, preferred_element_type=jnp.float32)
+    for copy in hot_copies:
+        copy.wait()
+    hot_t = hot_t_ref[...]
+    sums = lax.dot_general(x_ref[...], hot_t, NN, preferred_element_type=jnp.float32)
     mean = sums * (1.0 / share)
     near_mean = mean.astype(jnp.bfloat16)
     for i in range(0, ROWS, 4):
@@ -431,12 +434,12 @@
         hi_ref[:, part] = high
         lo_ref[:, part] = (square - high.astype(jnp.float32)).astype(jnp.bfloat16)
     spread = lax.dot_general(
-        hi_ref[...], hot, NT, preferred_element_type=jnp.float32
-    ) + lax.dot_general(lo_ref[...], hot, NT, preferred_element_type=jnp.float32)
+        hi_ref[...], hot_t, NN, preferred_element_type=jnp.float32
+    ) + lax.dot_general(lo_ref[...], hot_t, NN, preferred_element_type=jnp.float32)
     offset = mean - near_mean.astype(jnp.float32)
     spread = spread - share * (offset * offset)
     store_parts(stats_ref, (mean[:COLS].T, mean[COLS:].T, spread[:COLS].T, spread[COLS:].T))
-    stats_copy = pltpu.make_async_copy(stats_ref, stats_hbm, hot_sem)
+    stats_copy = pltpu.make_async_copy(stats_ref, stats_hbm, hot_sem.at[0])
     stats_copy.start()
     for c in range(CHUNKS):
         pltpu.make_async_copy(moved_ref.at[c], moved_hbm.at[c], out_sem.at[c]).wait()
@@ -452,7 +455,7 @@
     return [ref[pl.ds(k, ref.shape[0] // 4, stride=4), :] for k in range(4)]
 
 
-def batch_kernel(order_ref, owner_ref, batch_ref, hot_ref):
+def batch_kernel(order_ref, owner_ref, batch_ref, hot_ref, hot_t_ref):
     order = order_ref[...]
     shape = (32, order.shape[1])
     high = lax.broadcasted_iota(jnp.int32, shape, 0) == order // COLS
@@ -465,9 +468,9 @@
     batch_ref[...] = batch
     groups = lax.broadcasted_iota(jnp.int32, (COLS, COLS), 0)
     for i in range(ROWS):
-        hot_ref[:, COLS * i : COLS * (i + 1)] = jnp.where(
-            groups == batch[i : i + 1, :], 1.0, 0.0
-        ).astype(jnp.bfloat16)
+        tile = jnp.where(groups == batch[i : i + 1, :], 1.0, 0.0)
+        hot_ref[:, COLS * i : COLS * (i + 1)] = tile.astype(jnp.bfloat16)
+        hot_t_ref[COLS * i : COLS * (i + 1), :] = tile.T.astype(jnp.bfloat16)
 
 
 def merge_kernel(share, stats_ref, gain_ref, out_ref):
@@ -678,11 +681,11 @@
             pltpu.VMEM(LEVEL_SHAPE, jnp.float32),
             pltpu.VMEM(LEVEL_SHAPE, jnp.float32),
             pltpu.VMEM(GRID_SHAPE, jnp.float32),
-            pltpu.VMEM((EDGES, COLS), jnp.float32),
-            pltpu.VMEM((EDGES, COLS), jnp.float32),
+            pltpu.VMEM((EDGES + 64, COLS), jnp.float32),
+            pltpu.VMEM((EDGES + 64, COLS), jnp.float32),
             pltpu.VMEM((3 * 64, 2 * COLS), jnp.float32),
-            pltpu.VMEM((EDGES, COLS), jnp.bfloat16),
-            pltpu.VMEM((EDGES, COLS), jnp.bfloat16),
+            pltpu.VMEM((EDGES + 64, COLS), jnp.bfloat16),
+            pltpu.VMEM((EDGES + 64, COLS), jnp.bfloat16),
             pltpu.VMEM((3 * 64, 2 * COLS), jnp.bfloat16),
             dma((CHUNKS,)),
             dma((CHUNKS,)),
@@ -697,31 +700,31 @@
     chip = swap(cols, "by", False)
     near, far = pl.pallas_call(
         corner_kernel,
-        in_specs=[HBM_SPEC, VMEM_SPEC, VMEM_SPEC, HBM_SPEC, HBM_SPEC],
+        in_specs=[VMEM_SPEC, VMEM_SPEC, HBM_SPEC, HBM_SPEC],
         out_specs=[HBM_SPEC] * 2,
         out_shape=[bf16(EDGES + 64, COLS), bf16(EDGES + 64, COLS)],
         scratch_shapes=[
-            pltpu.VMEM((64, 2 * COLS), jnp.bfloat16),
             pltpu.VMEM((64, COLS), jnp.bfloat16),
             pltpu.VMEM((64, COLS), jnp.bfloat16),
-            dma((3,)),
+            dma((2,)),
         ],
-        input_output_aliases={3: 0, 4: 1},
+        input_output_aliases={2: 0, 3: 1},
         compiler_params=params(16),
         cost_estimate=cost(10**5, 10**6),
         name="corners",
-    )(cols, core, chip, near, far)
+    )(core, chip, near, far)
     near_in = swap(near, "bx", True)
     far_in = swap(far, "bx", False)
 
     owner = (jnp.arange(columns, dtype=jnp.int32) // share).astype(jnp.float32)[None, :]
-    batch, hot = pl.pallas_call(
+    batch, hot, hot_t = pl.pallas_call(
         batch_kernel,
         in_specs=[VMEM_SPEC, VMEM_SPEC],
-        out_specs=[VMEM_SPEC, VMEM_SPEC],
+        out_specs=[VMEM_SPEC, VMEM_SPEC, VMEM_SPEC],
         out_shape=[
             jax.ShapeDtypeStruct((ROWS, COLS), jnp.int32),
             jax.ShapeDtypeStruct((COLS, columns), jnp.bfloat16),
+            jax.ShapeDtypeStruct((columns, COLS), jnp.bfloat16),
         ],
         compiler_params=params(62),
         cost_estimate=cost(10**9, 2 * 10**6),
@@ -730,13 +733,14 @@
 
     moved, stats = pl.pallas_call(
         functools.partial(second_kernel, share),
-        in_specs=[HBM_SPEC] * 10,
+        in_specs=[HBM_SPEC] * 11,
         out_specs=[HBM_SPEC] * 2,
         out_shape=[f32(*GRID_SHAPE), f32(4 * count, COLS)],
         scratch_shapes=[
             pltpu.VMEM(GRID_SHAPE, jnp.float32),
             pltpu.VMEM(LEVEL_SHAPE, jnp.float32),
             pltpu.VMEM((COLS, columns), jnp.bfloat16),
+            pltpu.VMEM((columns, COLS), jnp.bfloat16),
             pltpu.VMEM(GRID_SHAPE, jnp.float32),
             pltpu.VMEM((FEATS, columns), jnp.bfloat16),
             pltpu.VMEM((FEATS, columns), jnp.bfloat16),
@@ -749,7 +753,7 @@
             dma((CHUNKS,)),
             dma((CHUNKS,)),
             dma((CHUNKS,)),
-            dma,
+            dma((2,)),
             dma((7,)),
         ],
         compiler_params=params(62),
@@ -766,6 +770,7 @@
         core,
         chip,
         hot,
+        hot_t,
     )
 
     stats, *raw = lax.optimization_barrier(

time: 87.5 us -> 87 us (level)
  local copies, waits for them, and re-layouts: 8.37 us -> 6.52 us
    reshape x5, local copies, waits for them, and re-layouts: 2.01 us -> 1.07 us  [by_row(): values = values.reshape(FIELDS, LEVELS, *rest)]
    all_to_all x1, waiting for transfers between devices: 6.23 us -> 7.17 us  [body(): lax.all_to_all(stats, ('bx', 'by'), split_axis=0, concat_axis=0, tiled=True)]
    unnamed x28, local copies, waits for them, and re-layouts: 2.33 us -> 1.42 us
  transfers between devices with their start and end apart: 6 -> 6, of which waited for: 5 -> 4; matrix products, arithmetic and copies ran while one was open for 11% -> 10% of each run, Pallas kernels for 3% -> 3%
where the time goes in v5:
time: 87 us; the launch traced here: 86.5 us
  Pallas kernels  33.9 us (39%)
  starting transfers between devices  27.3 us (31%)
  waiting for transfers between devices  15.3 us (18%)
  local copies, waits for them, and re-layouts  6.52 us (7%)
  other arithmetic  3.26 us (4%)
    ppermute x4, starting transfers between devices, swap(): return lax.ppermute(values, axis, pairs + [(b, a) for a, b in pairs])  11.4 us
    all_to_all x1, starting transfers between devices, body(): lax.all_to_all(stats, ('bx', 'by'), split_axis=0, concat_axis=0, tiled=True)  11.3 us
    pallas_call x1, Pallas kernels, body(): pl.pallas_call(network_kernel, in_specs=[HBM_SPEC] * 9, out_specs=HBM_SPE...  11.1 us
    pallas_call x1, Pallas kernels, body(): pl.pallas_call(functools.partial(second_kernel, share), in_specs=[HBM_SPE...  10.8 us
    all_to_all x1, waiting for transfers between devices, body(): lax.all_to_all(stats, ('bx', 'by'), split_axis=0, concat_axis=0, tiled=True)  7.17 us
    pallas_call x1, Pallas kernels, body(): pl.pallas_call(first_kernel, in_specs=[HBM_SPEC, HBM_SPEC], out_specs=[HB...  7.09 us
    all_to_all x1, waiting for transfers between devices, body(): lax.all_to_all(merged, ('bx', 'by'), split_axis=0, concat_axis=0, tiled=T...  7.01 us
    all_to_all x1, starting transfers between devices, body(): lax.all_to_all(merged, ('bx', 'by'), split_axis=0, concat_axis=0, tiled=T...  4.61 us
  transfers between devices with their start and end apart: 6, of which 4 were waited for; matrix products, arithmetic and copies ran while one was open for 10% of the time, Pallas kernels for 3%

profile of v5, /device:TPU:1, one launch (start us, length us, event | category | flops | bytes accessed | tf_op | source)
XLA Modules:
  0.0 86.5 jit_solution(10476006158602446984)
XLA Ops:
  0.0 7.1 %first_substep.1 = (f32[8,24,32,128]{3,2,1,0:T(8,128)}, bf16[640,128]{1,0:T(8,128)(2,1)}, bf16[640,128]{1,0:T(8,128)(2,1)}, bf16[192,256]{1,0:T(8,128)(2,1)}) custom-call(f32[4,1440,128]{2,1,0:T(8,128)} %bitcast.27, f32[4,1440,128]{2,1,0:T(8,128)} %bitcast.25), custom_call_target="tpu_custom_call" | custom-call | flops 10000000 | bytes 9000000 | tf_op jit(solution)/shard_map/first_substep/pallas_call | solution.py:670
  7.1 3.1 %collective-permute-start.1 = (bf16[192,256]{1,0:T(8,128)(2,1)}, bf16[192,256]{1,0:T(8,128)(2,1)S(1)}, u32[]{:S(2)}, u32[]{:S(2)}) collective-permute-start(bf16[192,256]{1,0:T(8,128)(2,1)} %get-tuple-element.25.cols_in), channel_id=1, source_target_pairs={{1,2},{3,4},{5,6},{7,8},{9,10},{11,12},{13,14},{15,0},{2,1},{4,3},... | collective-permute-start | bytes 294920 | tf_op jit(solution)/shard_map/ppermute | solution.py:639
  10.2 2.0 %collective-permute-start = (bf16[192,256]{1,0:T(8,128)(2,1)}, bf16[192,256]{1,0:T(8,128)(2,1)S(1)}, u32[]{:S(2)}, u32[]{:S(2)}) collective-permute-start(bf16[192,256]{1,0:T(8,128)(2,1)} %get-tuple-element.25.cols_in), channel_id=1, source_target_pairs={{0,1},{2,3},{4,5},{6,7},{8,9},{10,11},{12,13},{14,15},{1,0},{3,2},... | collective-permute-start | bytes 294920 | tf_op jit(solution)/shard_map/ppermute | solution.py:639
  12.2 0.5 collective-permute-done.1.chip_ref.chip_in
  12.7 0.7 collective-permute-done.core_ref.core_in
  13.4 1.6 %corners.1 = (bf16[640,128]{1,0:T(8,128)(2,1)}, bf16[640,128]{1,0:T(8,128)(2,1)}) custom-call(bf16[192,256]{1,0:T(8,128)(2,1)S(1)} %collective-permute-done.core_ref.core_in, bf16[192,256]{1,0:T(8,128)(2,1)S(1)} %collective-permute-done.1.chip_ref.chip_in, bf16[640,128]{1,0:T(8,128)(2,1)} %get-tuple-element.26.near_in, ...), custom_call_target="tpu_custom_call", output_to_operand_aliasing={{0}: (2, {}), {1}: (3, {})} | custom-call | flops 100000 | bytes 1000000 | tf_op jit(solution)/shard_map/corners/pallas_call | solution.py:701
  14.9 1.4 %collective-permute-start.2 = (bf16[640,128]{1,0:T(8,128)(2,1)}, bf16[640,128]{1,0:T(8,128)(2,1)S(1)}, u32[]{:S(2)}, u32[]{:S(2)}) collective-permute-start(bf16[640,128]{1,0:T(8,128)(2,1)} %get-tuple-element.28.own_near_in), channel_id=1, source_target_pairs={{0,16},{32,48},{64,80},{96,112},{16,0},{48,32},{80,64},{112,96},{1... | collective-permute-start | bytes 491528 | tf_op jit(solution)/shard_map/ppermute | solution.py:639
  16.3 4.9 %collective-permute-start.3 = (bf16[640,128]{1,0:T(8,128)(2,1)}, bf16[640,128]{1,0:T(8,128)(2,1)S(1)}, u32[]{:S(2)}, u32[]{:S(2)}) collective-permute-start(bf16[640,128]{1,0:T(8,128)(2,1)} %get-tuple-element.29.own_far_in), channel_id=1, source_target_pairs={{16,32},{48,64},{80,96},{112,0},{32,16},{64,48},{96,80},{0,112},{1... | collective-permute-start | bytes 491528 | tf_op jit(solution)/shard_map/ppermute | solution.py:639
  21.2 0.6 fusion.owner_ref
  21.9 2.5 %batch_ids.1 = (s32[24,128]{1,0:T(8,128)}, bf16[128,3072]{1,0:T(8,128)(2,1)}, bf16[3072,128]{1,0:T(8,128)(2,1)}) custom-call(s32[1,3072]{1,0:T(1,128)} %order_ref.1, f32[1,3072]{1,0:T(1,128)} %fusion.owner_ref), custom_call_target="tpu_custom_call" | custom-call | flops 1000000000 | bytes 2000000 | tf_op jit(solution)/shard_map/batch_ids/pallas_call | solution.py:720
  24.4 0.6 copy-done.8
  25.1 10.8 %second_substep.1 = (f32[8,24,32,128]{3,2,1,0:T(8,128)}, f32[512,128]{1,0:T(8,128)}) custom-call(f32[8,24,32,128]{3,2,1,0:T(8,128)} %get-tuple-element.24.part_hbm, f32[4,1440,128]{2,1,0:T(8,128)} %bitcast.26, bf16[640,128]{1,0:T(8,128)(2,1)} %get-tuple-element.28.own_near_in, bf16[640,128]{1,0:T(8,128)(2,1)} %get-tuple-element.29.own_far_in, ...), custom_call_target="tpu_custom_call" | custom-call | flops 1000000000 | bytes 9000000 | tf_op jit(solution)/shard_map/second_substep/pallas_call | solution.py:734
  36.0 0.1 reshape.88
  36.1 11.3 %all-to-all-start = ((f32[128,4,128]{2,1,0:T(4,128)}), f32[128,4,128]{2,1,0:T(4,128)S(1)}, u32[]{:S(2)}, u32[]{:S(2)}) async-start(f32[128,4,128]{2,1,0:T(4,128)} %bitcast.30), calls=%async_computation | async-start | bytes 524288 | tf_op jit(solution)/shard_map/all_to_all | solution.py:789
  47.4 0.1 broadcast_in_dim_reshape.9.gain_ref
  47.6 0.7 multiply_bitcast_fusion.1
  48.3 0.8 reshape.93
  49.1 0.7 copy.17
  49.8 1.3 %multiply_bitcast_fusion.inner_hbm = bf16[3,512,512]{2,1,0:T(8,128)(2,1)} fusion(bf16[3,512,512]{1,2,0:T(8,128)(2,1)S(1)} %copy.17), kind=kLoop, calls=%fused_computation | loop fusion | flops 786432 | bytes 3145728 | tf_op jit(solution)/shard_map/mul | solution.py:835
  51.1 7.2 %all-to-all-done = f32[128,4,128]{2,1,0:T(4,128)S(1)} async-done(((f32[128,4,128]{2,1,0:T(4,128)}), f32[128,4,128]{2,1,0:T(4,128)S(1)}, u32[]{:S(2)}, u32[]{:S(2)}) %all-to-all-start) | async-done | bytes 262176 | tf_op jit(solution)/shard_map/all_to_all | solution.py:789
  58.3 0.8 merge_statistics.1
  59.1 4.6 %all-to-all-start.1 = ((f32[128,4,128]{2,1,0:T(4,128)}), f32[128,4,128]{2,1,0:T(4,128)S(1)}, u32[]{:S(2)}, u32[]{:S(2)}) async-start(f32[128,4,128]{2,1,0:T(4,128)} %bitcast.5), calls=%async_computation.1 | async-start | bytes 524288 | tf_op jit(solution)/shard_map/all_to_all | solution.py:799
  63.8 0.1 reshape.90
  63.8 0.1 reshape.96
  64.0 0.7 broadcast_in_dim_reshape.11.final_hbm
  64.8 0.6 broadcast_in_dim_reshape.10.shift_hbm
  65.4 0.7 copy.16
  66.2 0.8 copy.19
  67.1 0.6 broadcast_multiply_fusion.bias_hbm
  67.7 7.0 %all-to-all-done.1 = f32[128,4,128]{2,1,0:T(4,128)S(1)} async-done(((f32[128,4,128]{2,1,0:T(4,128)}), f32[128,4,128]{2,1,0:T(4,128)S(1)}, u32[]{:S(2)}, u32[]{:S(2)}) %all-to-all-start.1) | async-done | bytes 262176 | tf_op jit(solution)/shard_map/all_to_all | solution.py:799
  74.7 0.7 copy-done.5
  75.4 11.1 %network.1 = f32[240,24,128]{2,1,0:T(8,128)} custom-call(f32[8,24,32,128]{3,2,1,0:T(8,128)} %get-tuple-element.32.moved_hbm, s32[24,128]{1,0:T(8,128)} %get-tuple-element.33.batch_hbm, f32[512,128]{1,0:T(8,128)} %bitcast.29, f32[1,256]{1,0:T(1,128)} %broadcast_in_dim_reshape.10.shift_hbm, bf16[256,512]{1,0:T(8,128)(2,1)} %bitcast.31, ...), custom_call_target="tpu_custom_call" | custom-call | flops 6000000000 | bytes 9000000 | tf_op jit(solution)/shard_map/network/pallas_call | solution.py:802
  (40 shorter events, 0.5 us)
Async XLA Ops:
  7.1 5.6 %collective-permute-start.1 = (bf16[192,256]{1,0:T(8,128)(2,1)}, bf16[192,256]{1,0:T(8,128)(2,1)S(1)}, u32[]{:S(2)}, u32[]{:S(2)}) collective-permute-start(bf16[192,256]{1,0:T(8,128)(2,1)} %get-tuple-element.25.cols_in), channel_id=1, source_target_pairs={{1,2},{3,4},{5,6},{7,8},{9,10},{11,12},{13,14},{15,0},{2,1},{4,3},... | collective-permute-start | bytes 294920 | tf_op jit(solution)/shard_map/ppermute | solution.py:639
  10.2 3.2 %collective-permute-start = (bf16[192,256]{1,0:T(8,128)(2,1)}, bf16[192,256]{1,0:T(8,128)(2,1)S(1)}, u32[]{:S(2)}, u32[]{:S(2)}) collective-permute-start(bf16[192,256]{1,0:T(8,128)(2,1)} %get-tuple-element.25.cols_in), channel_id=1, source_target_pairs={{0,1},{2,3},{4,5},{6,7},{8,9},{10,11},{12,13},{14,15},{1,0},{3,2},... | collective-permute-start | bytes 294920 | tf_op jit(solution)/shard_map/ppermute | solution.py:639
  12.7 11.7 %copy-start = (bf16[192,256]{1,0:T(8,128)(2,1)}, bf16[192,256]{1,0:T(8,128)(2,1)S(1)}, u32[]{:S(2)}) copy-start(bf16[192,256]{1,0:T(8,128)(2,1)S(1)} %collective-permute-done.1.chip_ref.chip_in) | copy-start | bytes 294916
  13.4 11.0 %copy-start.1 = (bf16[192,256]{1,0:T(8,128)(2,1)}, bf16[192,256]{1,0:T(8,128)(2,1)S(1)}, u32[]{:S(2)}) copy-start(bf16[192,256]{1,0:T(8,128)(2,1)S(1)} %collective-permute-done.core_ref.core_in) | copy-start | bytes 294916
  14.9 9.5 %collective-permute-start.2 = (bf16[640,128]{1,0:T(8,128)(2,1)}, bf16[640,128]{1,0:T(8,128)(2,1)S(1)}, u32[]{:S(2)}, u32[]{:S(2)}) collective-permute-start(bf16[640,128]{1,0:T(8,128)(2,1)} %get-tuple-element.28.own_near_in), channel_id=1, source_target_pairs={{0,16},{32,48},{64,80},{96,112},{16,0},{48,32},{80,64},{112,96},{1... | collective-permute-start | bytes 491528 | tf_op jit(solution)/shard_map/ppermute | solution.py:639
  16.3 8.1 %collective-permute-start.3 = (bf16[640,128]{1,0:T(8,128)(2,1)}, bf16[640,128]{1,0:T(8,128)(2,1)S(1)}, u32[]{:S(2)}, u32[]{:S(2)}) collective-permute-start(bf16[640,128]{1,0:T(8,128)(2,1)} %get-tuple-element.29.own_far_in), channel_id=1, source_target_pairs={{16,32},{48,64},{80,96},{112,0},{32,16},{64,48},{96,80},{0,112},{1... | collective-permute-start | bytes 491528 | tf_op jit(solution)/shard_map/ppermute | solution.py:639
  24.4 0.7 copy-start.8
  24.4 0.7 copy-start.9
  25.1 10.8 %copy-start.11 = (f32[240]{0:T(256)S(1)}, f32[240]{0:T(256)}, u32[]{:S(2)}) copy-start(f32[240]{0:T(256)} %param.13) | copy-start | bytes 2884
  25.1 22.4 %copy-start.6 = (bf16[512,240]{0,1:T(8,128)(2,1)S(1)}, bf16[512,240]{0,1:T(8,128)(2,1)}, u32[]{:S(2)}) copy-start(bf16[512,240]{0,1:T(8,128)(2,1)} %param.15) | copy-start | bytes 737284
  25.1 23.2 %copy-start.7 = (bf16[240,512]{1,0:T(8,128)(2,1)S(1)}, bf16[240,512]{1,0:T(8,128)(2,1)}, u32[]{:S(2)}) copy-start(bf16[240,512]{1,0:T(8,128)(2,1)} %param.17) | copy-start | bytes 737284
  35.9 13.2 %copy-start.2 = (bf16[3,512,512]{2,1,0:T(8,128)(2,1)S(1)}, bf16[3,512,512]{2,1,0:T(8,128)(2,1)}, u32[]{:S(2)}) copy-start(bf16[3,512,512]{2,1,0:T(8,128)(2,1)} %param.16) | copy-start | bytes 4718596
  36.1 22.3 %all-to-all-start = ((f32[128,4,128]{2,1,0:T(4,128)}), f32[128,4,128]{2,1,0:T(4,128)S(1)}, u32[]{:S(2)}, u32[]{:S(2)}) async-start(f32[128,4,128]{2,1,0:T(4,128)} %bitcast.30), calls=%async_computation | async-start | bytes 524288 | tf_op jit(solution)/shard_map/all_to_all | solution.py:789
  49.8 13.9 %copy-start.4 = (bf16[4,60,512]{2,1,0:T(8,128)(2,1)S(1)}, bf16[4,60,512]{2,1,0:T(8,128)(2,1)}, u32[]{:S(2)}) copy-start(bf16[4,60,512]{2,1,0:T(8,128)(2,1)} %reshape.93) | copy-start | bytes 737284
  51.1 12.6 %copy-start.12 = (f32[240]{0:T(256)S(1)}, f32[240]{0:T(256)}, u32[]{:S(2)}) copy-start(f32[240]{0:T(256)} %param.14) | copy-start | bytes 2884
  51.1 12.7 %copy-start.13 = (f32[240]{0:T(256)S(1)}, f32[240]{0:T(256)}, u32[]{:S(2)}) copy-start(f32[240]{0:T(256)} %param.19) | copy-start | bytes 2884
  51.1 14.3 %copy-start.3 = (bf16[8,4,8,512]{3,2,0,1:T(8,128)(2,1)S(1)}, bf16[8,4,8,512]{3,2,0,1:T(8,128)(2,1)}, u32[]{:S(2)}) copy-start(bf16[8,4,8,512]{3,2,0,1:T(8,128)(2,1)} %multiply_bitcast_fusion.1) | copy-start | bytes 786436
  58.3 8.8 %copy-start.10 = (f32[4,512]{1,0:T(4,128)S(1)}, f32[4,512]{1,0:T(4,128)}, u32[]{:S(2)}) copy-start(f32[4,512]{1,0:T(4,128)} %param.18) | copy-start | bytes 24580
  59.1 15.6 %all-to-all-start.1 = ((f32[128,4,128]{2,1,0:T(4,128)}), f32[128,4,128]{2,1,0:T(4,128)S(1)}, u32[]{:S(2)}, u32[]{:S(2)}) async-start(f32[128,4,128]{2,1,0:T(4,128)} %bitcast.5), calls=%async_computation.1 | async-start | bytes 524288 | tf_op jit(solution)/shard_map/all_to_all | solution.py:799
  74.7 0.7 copy-start.5

commit v6 on v5

--- a/solution.py
+++ b/solution.py
@@ -197,7 +197,7 @@
             cols_ref[pl.ds(128 + row, 8), COLS * h : COLS * (h + 1)] = jnp.where(valid, acc, 0.0)
         return carry
 
-    lax.fori_loop(0, CHUNKS, one_chunk, 0)
+    lax.fori_loop(0, CHUNKS, one_chunk, 0, unroll=2)
     for out, kept in ((near_out_ref, near_ref), (far_out_ref, far_ref)):
         out[...] = kept[...].astype(jnp.bfloat16)
     cols_out_ref[...] = cols_ref[...].astype(jnp.bfloat16)

time: 87 us -> 87 us (level)
  no operation moved by 1% of the time
where the time goes in v6:
time: 87 us; the launch traced here: 86.5 us
  Pallas kernels  33.9 us (39%)
  starting transfers between devices  27.3 us (31%)
  waiting for transfers between devices  15.3 us (18%)
  local copies, waits for them, and re-layouts  6.52 us (7%)
  other arithmetic  3.26 us (4%)
    ppermute x4, starting transfers between devices, swap(): return lax.ppermute(values, axis, pairs + [(b, a) for a, b in pairs])  11.4 us
    all_to_all x1, starting transfers between devices, body(): lax.all_to_all(stats, ('bx', 'by'), split_axis=0, concat_axis=0, tiled=True)  11.3 us
    pallas_call x1, Pallas kernels, body(): pl.pallas_call(network_kernel, in_specs=[HBM_SPEC] * 9, out_specs=HBM_SPE...  11.1 us
    pallas_call x1, Pallas kernels, body(): pl.pallas_call(functools.partial(second_kernel, share), in_specs=[HBM_SPE...  10.8 us
    all_to_all x1, waiting for transfers between devices, body(): lax.all_to_all(stats, ('bx', 'by'), split_axis=0, concat_axis=0, tiled=True)  7.17 us
    pallas_call x1, Pallas kernels, body(): pl.pallas_call(first_kernel, in_specs=[HBM_SPEC, HBM_SPEC], out_specs=[HB...  7.15 us
    all_to_all x1, waiting for transfers between devices, body(): lax.all_to_all(merged, ('bx', 'by'), split_axis=0, concat_axis=0, tiled=T...  7.01 us
    all_to_all x1, starting transfers between devices, body(): lax.all_to_all(merged, ('bx', 'by'), split_axis=0, concat_axis=0, tiled=T...  4.61 us
  transfers between devices with their start and end apart: 6, of which 4 were waited for; matrix products, arithmetic and copies ran while one was open for 10% of the time, Pallas kernels for 3%

profile of v6, /device:TPU:1, one launch (start us, length us, event | category | flops | bytes accessed | tf_op | source)
XLA Modules:
  0.0 86.5 jit_solution(5980126713403214034)
XLA Ops:
  0.0 7.1 %first_substep.1 = (f32[8,24,32,128]{3,2,1,0:T(8,128)}, bf16[640,128]{1,0:T(8,128)(2,1)}, bf16[640,128]{1,0:T(8,128)(2,1)}, bf16[192,256]{1,0:T(8,128)(2,1)}) custom-call(f32[4,1440,128]{2,1,0:T(8,128)} %bitcast.27, f32[4,1440,128]{2,1,0:T(8,128)} %bitcast.25), custom_call_target="tpu_custom_call" | custom-call | flops 10000000 | bytes 9000000 | tf_op jit(solution)/shard_map/first_substep/pallas_call | solution.py:670
  7.2 3.1 %collective-permute-start.1 = (bf16[192,256]{1,0:T(8,128)(2,1)}, bf16[192,256]{1,0:T(8,128)(2,1)S(1)}, u32[]{:S(2)}, u32[]{:S(2)}) collective-permute-start(bf16[192,256]{1,0:T(8,128)(2,1)} %get-tuple-element.25.cols_in), channel_id=1, source_target_pairs={{1,2},{3,4},{5,6},{7,8},{9,10},{11,12},{13,14},{15,0},{2,1},{4,3},... | collective-permute-start | bytes 294920 | tf_op jit(solution)/shard_map/ppermute | solution.py:639
  10.3 2.0 %collective-permute-start = (bf16[192,256]{1,0:T(8,128)(2,1)}, bf16[192,256]{1,0:T(8,128)(2,1)S(1)}, u32[]{:S(2)}, u32[]{:S(2)}) collective-permute-start(bf16[192,256]{1,0:T(8,128)(2,1)} %get-tuple-element.25.cols_in), channel_id=1, source_target_pairs={{0,1},{2,3},{4,5},{6,7},{8,9},{10,11},{12,13},{14,15},{1,0},{3,2},... | collective-permute-start | bytes 294920 | tf_op jit(solution)/shard_map/ppermute | solution.py:639
  12.3 0.5 collective-permute-done.1.chip_ref.chip_in
  12.8 0.7 collective-permute-done.core_ref.core_in
  13.4 1.6 %corners.1 = (bf16[640,128]{1,0:T(8,128)(2,1)}, bf16[640,128]{1,0:T(8,128)(2,1)}) custom-call(bf16[192,256]{1,0:T(8,128)(2,1)S(1)} %collective-permute-done.core_ref.core_in, bf16[192,256]{1,0:T(8,128)(2,1)S(1)} %collective-permute-done.1.chip_ref.chip_in, bf16[640,128]{1,0:T(8,128)(2,1)} %get-tuple-element.26.near_in, ...), custom_call_target="tpu_custom_call", output_to_operand_aliasing={{0}: (2, {}), {1}: (3, {})} | custom-call | flops 100000 | bytes 1000000 | tf_op jit(solution)/shard_map/corners/pallas_call | solution.py:701
  15.0 1.4 %collective-permute-start.2 = (bf16[640,128]{1,0:T(8,128)(2,1)}, bf16[640,128]{1,0:T(8,128)(2,1)S(1)}, u32[]{:S(2)}, u32[]{:S(2)}) collective-permute-start(bf16[640,128]{1,0:T(8,128)(2,1)} %get-tuple-element.28.own_near_in), channel_id=1, source_target_pairs={{0,16},{32,48},{64,80},{96,112},{16,0},{48,32},{80,64},{112,96},{1... | collective-permute-start | bytes 491528 | tf_op jit(solution)/shard_map/ppermute | solution.py:639
  16.4 4.9 %collective-permute-start.3 = (bf16[640,128]{1,0:T(8,128)(2,1)}, bf16[640,128]{1,0:T(8,128)(2,1)S(1)}, u32[]{:S(2)}, u32[]{:S(2)}) collective-permute-start(bf16[640,128]{1,0:T(8,128)(2,1)} %get-tuple-element.29.own_far_in), channel_id=1, source_target_pairs={{16,32},{48,64},{80,96},{112,0},{32,16},{64,48},{96,80},{0,112},{1... | collective-permute-start | bytes 491528 | tf_op jit(solution)/shard_map/ppermute | solution.py:639
  21.3 0.6 fusion.owner_ref
  21.9 2.5 %batch_ids.1 = (s32[24,128]{1,0:T(8,128)}, bf16[128,3072]{1,0:T(8,128)(2,1)}, bf16[3072,128]{1,0:T(8,128)(2,1)}) custom-call(s32[1,3072]{1,0:T(1,128)} %order_ref.1, f32[1,3072]{1,0:T(1,128)} %fusion.owner_ref), custom_call_target="tpu_custom_call" | custom-call | flops 1000000000 | bytes 2000000 | tf_op jit(solution)/shard_map/batch_ids/pallas_call | solution.py:720
  24.5 0.6 copy-done.8
  25.2 10.8 %second_substep.1 = (f32[8,24,32,128]{3,2,1,0:T(8,128)}, f32[512,128]{1,0:T(8,128)}) custom-call(f32[8,24,32,128]{3,2,1,0:T(8,128)} %get-tuple-element.24.part_hbm, f32[4,1440,128]{2,1,0:T(8,128)} %bitcast.26, bf16[640,128]{1,0:T(8,128)(2,1)} %get-tuple-element.28.own_near_in, bf16[640,128]{1,0:T(8,128)(2,1)} %get-tuple-element.29.own_far_in, ...), custom_call_target="tpu_custom_call" | custom-call | flops 1000000000 | bytes 9000000 | tf_op jit(solution)/shard_map/second_substep/pallas_call | solution.py:734
  36.0 0.1 reshape.88
  36.1 11.3 %all-to-all-start = ((f32[128,4,128]{2,1,0:T(4,128)}), f32[128,4,128]{2,1,0:T(4,128)S(1)}, u32[]{:S(2)}, u32[]{:S(2)}) async-start(f32[128,4,128]{2,1,0:T(4,128)} %bitcast.30), calls=%async_computation | async-start | bytes 524288 | tf_op jit(solution)/shard_map/all_to_all | solution.py:789
  47.5 0.1 broadcast_in_dim_reshape.9.gain_ref
  47.7 0.7 multiply_bitcast_fusion.1
  48.4 0.8 reshape.93
  49.2 0.7 copy.17
  49.9 1.3 %multiply_bitcast_fusion.inner_hbm = bf16[3,512,512]{2,1,0:T(8,128)(2,1)} fusion(bf16[3,512,512]{1,2,0:T(8,128)(2,1)S(1)} %copy.17), kind=kLoop, calls=%fused_computation | loop fusion | flops 786432 | bytes 3145728 | tf_op jit(solution)/shard_map/mul | solution.py:835
  51.2 7.2 %all-to-all-done = f32[128,4,128]{2,1,0:T(4,128)S(1)} async-done(((f32[128,4,128]{2,1,0:T(4,128)}), f32[128,4,128]{2,1,0:T(4,128)S(1)}, u32[]{:S(2)}, u32[]{:S(2)}) %all-to-all-start) | async-done | bytes 262176 | tf_op jit(solution)/shard_map/all_to_all | solution.py:789
  58.4 0.8 merge_statistics.1
  59.1 4.6 %all-to-all-start.1 = ((f32[128,4,128]{2,1,0:T(4,128)}), f32[128,4,128]{2,1,0:T(4,128)S(1)}, u32[]{:S(2)}, u32[]{:S(2)}) async-start(f32[128,4,128]{2,1,0:T(4,128)} %bitcast.5), calls=%async_computation.1 | async-start | bytes 524288 | tf_op jit(solution)/shard_map/all_to_all | solution.py:799
  63.8 0.1 reshape.90
  63.9 0.1 reshape.96
  64.1 0.7 broadcast_in_dim_reshape.11.final_hbm
  64.9 0.6 broadcast_in_dim_reshape.10.shift_hbm
  65.5 0.7 copy.16
  66.3 0.8 copy.19
  67.1 0.6 broadcast_multiply_fusion.bias_hbm
  67.7 7.0 %all-to-all-done.1 = f32[128,4,128]{2,1,0:T(4,128)S(1)} async-done(((f32[128,4,128]{2,1,0:T(4,128)}), f32[128,4,128]{2,1,0:T(4,128)S(1)}, u32[]{:S(2)}, u32[]{:S(2)}) %all-to-all-start.1) | async-done | bytes 262176 | tf_op jit(solution)/shard_map/all_to_all | solution.py:799
  74.7 0.7 copy-done.5
  75.4 11.1 %network.1 = f32[240,24,128]{2,1,0:T(8,128)} custom-call(f32[8,24,32,128]{3,2,1,0:T(8,128)} %get-tuple-element.32.moved_hbm, s32[24,128]{1,0:T(8,128)} %get-tuple-element.33.batch_hbm, f32[512,128]{1,0:T(8,128)} %bitcast.29, f32[1,256]{1,0:T(1,128)} %broadcast_in_dim_reshape.10.shift_hbm, bf16[256,512]{1,0:T(8,128)(2,1)} %bitcast.31, ...), custom_call_target="tpu_custom_call" | custom-call | flops 6000000000 | bytes 9000000 | tf_op jit(solution)/shard_map/network/pallas_call | solution.py:802
  (40 shorter events, 0.5 us)
Async XLA Ops:
  7.2 5.6 %collective-permute-start.1 = (bf16[192,256]{1,0:T(8,128)(2,1)}, bf16[192,256]{1,0:T(8,128)(2,1)S(1)}, u32[]{:S(2)}, u32[]{:S(2)}) collective-permute-start(bf16[192,256]{1,0:T(8,128)(2,1)} %get-tuple-element.25.cols_in), channel_id=1, source_target_pairs={{1,2},{3,4},{5,6},{7,8},{9,10},{11,12},{13,14},{15,0},{2,1},{4,3},... | collective-permute-start | bytes 294920 | tf_op jit(solution)/shard_map/ppermute | solution.py:639
  10.3 3.2 %collective-permute-start = (bf16[192,256]{1,0:T(8,128)(2,1)}, bf16[192,256]{1,0:T(8,128)(2,1)S(1)}, u32[]{:S(2)}, u32[]{:S(2)}) collective-permute-start(bf16[192,256]{1,0:T(8,128)(2,1)} %get-tuple-element.25.cols_in), channel_id=1, source_target_pairs={{0,1},{2,3},{4,5},{6,7},{8,9},{10,11},{12,13},{14,15},{1,0},{3,2},... | collective-permute-start | bytes 294920 | tf_op jit(solution)/shard_map/ppermute | solution.py:639
  12.8 11.7 %copy-start = (bf16[192,256]{1,0:T(8,128)(2,1)}, bf16[192,256]{1,0:T(8,128)(2,1)S(1)}, u32[]{:S(2)}) copy-start(bf16[192,256]{1,0:T(8,128)(2,1)S(1)} %collective-permute-done.1.chip_ref.chip_in) | copy-start | bytes 294916
  13.4 11.0 %copy-start.1 = (bf16[192,256]{1,0:T(8,128)(2,1)}, bf16[192,256]{1,0:T(8,128)(2,1)S(1)}, u32[]{:S(2)}) copy-start(bf16[192,256]{1,0:T(8,128)(2,1)S(1)} %collective-permute-done.core_ref.core_in) | copy-start | bytes 294916
  15.0 9.5 %collective-permute-start.2 = (bf16[640,128]{1,0:T(8,128)(2,1)}, bf16[640,128]{1,0:T(8,128)(2,1)S(1)}, u32[]{:S(2)}, u32[]{:S(2)}) collective-permute-start(bf16[640,128]{1,0:T(8,128)(2,1)} %get-tuple-element.28.own_near_in), channel_id=1, source_target_pairs={{0,16},{32,48},{64,80},{96,112},{16,0},{48,32},{80,64},{112,96},{1... | collective-permute-start | bytes 491528 | tf_op jit(solution)/shard_map/ppermute | solution.py:639
  16.4 8.1 %collective-permute-start.3 = (bf16[640,128]{1,0:T(8,128)(2,1)}, bf16[640,128]{1,0:T(8,128)(2,1)S(1)}, u32[]{:S(2)}, u32[]{:S(2)}) collective-permute-start(bf16[640,128]{1,0:T(8,128)(2,1)} %get-tuple-element.29.own_far_in), channel_id=1, source_target_pairs={{16,32},{48,64},{80,96},{112,0},{32,16},{64,48},{96,80},{0,112},{1... | collective-permute-start | bytes 491528 | tf_op jit(solution)/shard_map/ppermute | solution.py:639
  24.5 0.7 copy-start.8
  24.5 0.7 copy-start.9
  25.2 10.8 %copy-start.11 = (f32[240]{0:T(256)S(1)}, f32[240]{0:T(256)}, u32[]{:S(2)}) copy-start(f32[240]{0:T(256)} %param.13) | copy-start | bytes 2884
  25.2 22.4 %copy-start.6 = (bf16[512,240]{0,1:T(8,128)(2,1)S(1)}, bf16[512,240]{0,1:T(8,128)(2,1)}, u32[]{:S(2)}) copy-start(bf16[512,240]{0,1:T(8,128)(2,1)} %param.15) | copy-start | bytes 737284
  25.2 23.2 %copy-start.7 = (bf16[240,512]{1,0:T(8,128)(2,1)S(1)}, bf16[240,512]{1,0:T(8,128)(2,1)}, u32[]{:S(2)}) copy-start(bf16[240,512]{1,0:T(8,128)(2,1)} %param.17) | copy-start | bytes 737284
  36.0 13.2 %copy-start.2 = (bf16[3,512,512]{2,1,0:T(8,128)(2,1)S(1)}, bf16[3,512,512]{2,1,0:T(8,128)(2,1)}, u32[]{:S(2)}) copy-start(bf16[3,512,512]{2,1,0:T(8,128)(2,1)} %param.16) | copy-start | bytes 4718596
  36.1 22.3 %all-to-all-start = ((f32[128,4,128]{2,1,0:T(4,128)}), f32[128,4,128]{2,1,0:T(4,128)S(1)}, u32[]{:S(2)}, u32[]{:S(2)}) async-start(f32[128,4,128]{2,1,0:T(4,128)} %bitcast.30), calls=%async_computation | async-start | bytes 524288 | tf_op jit(solution)/shard_map/all_to_all | solution.py:789
  49.9 13.9 %copy-start.4 = (bf16[4,60,512]{2,1,0:T(8,128)(2,1)S(1)}, bf16[4,60,512]{2,1,0:T(8,128)(2,1)}, u32[]{:S(2)}) copy-start(bf16[4,60,512]{2,1,0:T(8,128)(2,1)} %reshape.93) | copy-start | bytes 737284
  51.2 12.6 %copy-start.12 = (f32[240]{0:T(256)S(1)}, f32[240]{0:T(256)}, u32[]{:S(2)}) copy-start(f32[240]{0:T(256)} %param.14) | copy-start | bytes 2884
  51.2 12.7 %copy-start.13 = (f32[240]{0:T(256)S(1)}, f32[240]{0:T(256)}, u32[]{:S(2)}) copy-start(f32[240]{0:T(256)} %param.19) | copy-start | bytes 2884
  51.2 14.3 %copy-start.3 = (bf16[8,4,8,512]{3,2,0,1:T(8,128)(2,1)S(1)}, bf16[8,4,8,512]{3,2,0,1:T(8,128)(2,1)}, u32[]{:S(2)}) copy-start(bf16[8,4,8,512]{3,2,0,1:T(8,128)(2,1)} %multiply_bitcast_fusion.1) | copy-start | bytes 786436
  58.4 8.8 %copy-start.10 = (f32[4,512]{1,0:T(4,128)S(1)}, f32[4,512]{1,0:T(4,128)}, u32[]{:S(2)}) copy-start(f32[4,512]{1,0:T(4,128)} %param.18) | copy-start | bytes 24580
  59.1 15.6 %all-to-all-start.1 = ((f32[128,4,128]{2,1,0:T(4,128)}), f32[128,4,128]{2,1,0:T(4,128)S(1)}, u32[]{:S(2)}, u32[]{:S(2)}) async-start(f32[128,4,128]{2,1,0:T(4,128)} %bitcast.5), calls=%async_computation.1 | async-start | bytes 524288 | tf_op jit(solution)/shard_map/all_to_all | solution.py:799
  74.7 0.7 copy-start.5
